TPU v7x, 32 devices: a whole 2x2x4 slice. The times are simulated.
32 devices in a mesh: pairs: 2 (over x), section: 2 (over core), tp: 8 (over z, y).
Axes of the slice: x: 2, y: 2, z: 4, core: 2. Of those that a mesh axis runs over, the one named last changes fastest.
Arguments:
- queries: bfloat16 [4, 96, 16384], P(('pairs', 'section'), None, 'tp'), parts along dimension 0, may hold values from -8 to 8, as said below
- fresh_key_value: bfloat16 [4, 96, 2, 8, 128], P(('pairs', 'section'), 'tp'), parts along dimension 0, may hold values from -6 to 6, as said below
- key_value_page_store: bfloat16 [4, 16, 2, 8, 128, 128], P(('pairs', 'section'), 'tp'), parts along dimension 0, may hold values from -6 to 6
- prefix_len: int32 [2], P('pairs'), parts along dimension 0, may hold values from 512 to 1024
- page_table: int32 [32, 4], P('pairs'), parts along dimension 0, may hold values from 0 to 23, as said below
- context_len: int32 [32], P('pairs'), parts along dimension 0, may hold values from 1 to 512, as said below
Outputs:
- attended: bfloat16 [4, 96, 16384], P(('pairs', 'section'), None, 'tp'), parts along dimension 0
There are 2 independent parts, one for each index of `pairs`. A program takes and returns all parts, laid end to end along the dimension named above; each array names one. Nothing has to cross between parts.
Inputs may be any that keep to these rules, and one draw needn't show every extreme that they name: `queries`: mostly of order one; in a few rows of each side a query may match a key of its own side closely. `fresh_key_value`: mostly of order one. `page_table`: entries m of row r with m * 128 < context_len[r] are used; used entries are distinct over all rows; the others name any page and are not read. `context_len`: A row's length needs at most 4 pages.
All inputs are finite; a program needn't handle non-finite values.
Results may differ from a plain program's by a relative error of at most 0.0031.
Values may be sent and summed in bfloat16 or wider, within the bound.
No kernel may reach another device: no remote copies, remote signals or barrier semaphores. Data moves between devices by JAX's collectives and lax.ppermute only.
A program may use at most 128 MiB of HBM per device.

v0:
```python
from functools import partial
import math

import jax
import jax.numpy as jnp
from jax import lax
from jax.sharding import PartitionSpec as P

FIN_DEV = 1


def shifted(shard, axis, by):
    size = lax.axis_size(axis)
    pairs = [(i, i + by) for i in range(size) if 0 <= i + by < size]
    return lax.ppermute(shard, axis, pairs)


def build_visible(
    is_prefill,
    prefix_len,
    page_table,
    context_len,
    slot_count,
    per_device,
    prefix_pages,
    page_size,
    row_count,
):
    dec_rows, max_entries = page_table.shape
    key_index = jnp.arange(slot_count * page_size, dtype=jnp.int32)
    slot_of = key_index // page_size
    within = key_index % page_size
    device_of = slot_of // per_device
    local_of = slot_of % per_device
    prefix_pos = (device_of * prefix_pages + local_of) * page_size + within
    prefix_end = prefix_len[0]
    prefix_ok = (local_of < prefix_pages) & (prefix_pos < prefix_end)
    entries = jnp.arange(max_entries, dtype=jnp.int32)
    in_use = entries[None, :] * page_size < context_len[:, None]
    matches = (
        page_table[:, :, None] == jnp.arange(slot_count, dtype=jnp.int32)[None, None, :]
    ) & in_use[:, :, None]
    match_int = matches.astype(jnp.int32)
    row_ids = jnp.arange(dec_rows, dtype=jnp.int32)
    owned = jnp.sum(match_int, axis=(0, 1)) > 0
    owners = jnp.sum(match_int * row_ids[:, None, None], axis=(0, 1))
    offsets = jnp.sum(match_int * (entries * page_size)[None, :, None], axis=(0, 1))
    limits = jnp.sum(match_int * context_len[:, None, None], axis=(0, 1))
    decode_pos = jnp.repeat(offsets, page_size) + within
    decode_ok = jnp.repeat(owned, page_size) & (decode_pos < jnp.repeat(limits, page_size))
    decode_seq = jnp.repeat(owners, page_size)
    step_count = row_count // dec_rows
    query_index = jnp.arange(row_count, dtype=jnp.int32)
    decode_row = jnp.tile(row_ids, step_count)
    decode_qpos = jnp.tile(context_len, step_count) + query_index // dec_rows
    key_ok = jnp.where(is_prefill, prefix_ok, decode_ok)
    key_seq = jnp.where(is_prefill, 0, decode_seq)
    query_seq = jnp.where(is_prefill, 0, decode_row)
    query_pos = jnp.where(is_prefill, prefix_end + query_index, decode_qpos)
    cached = key_ok[None, :] & (key_seq[None, :] == query_seq[:, None])
    fresh = (query_seq[None, :] == query_seq[:, None]) & (query_pos[None, :] <= query_pos[:, None])
    return jnp.concatenate([cached, fresh], axis=1)


def attend_head(head_query, key_rows, value_rows, visible, factor):
    scores = (
        lax.dot_general(
            head_query, key_rows, (((1,), (1,)), ((), ())), preferred_element_type=jnp.float32
        )
        * factor
    )
    scores = jnp.where(visible, scores, -1e30)
    highest = jnp.max(scores, axis=1, keepdims=True)
    raw_weights = jnp.exp(scores - highest)
    denominator = jnp.sum(raw_weights, axis=1, keepdims=True)
    weights = raw_weights.astype(jnp.bfloat16)
    return (jnp.dot(weights, value_rows, preferred_element_type=jnp.float32) / denominator).astype(
        jnp.bfloat16
    )


def spread(pieces, tp_count):
    kv_heads = pieces.shape[3]
    chosen = jnp.arange(tp_count, dtype=jnp.int32) * kv_heads // tp_count
    return jnp.take(pieces, chosen, axis=3)


def to_heads(pages, new_rows):
    tp_count = lax.axis_size("tp")
    page_size = pages.shape[4]
    head_dim = pages.shape[5]
    got_pages, got_rows = (
        lax.all_to_all(spread(pages, tp_count), "tp", split_axis=3, concat_axis=1, tiled=True),
        lax.all_to_all(spread(new_rows, tp_count), "tp", split_axis=3, concat_axis=1, tiled=True),
    )
    head_pages = got_pages.reshape((-1, 2, page_size, head_dim))
    head_new = got_rows.reshape((-1, 2, head_dim))
    return (head_pages, head_new)


def body(queries, fresh_key_value, key_value_page_store, prefix_len, page_table, context_len):
    is_prefill = lax.axis_index("section") == 0
    pages_here = key_value_page_store.shape[1]
    page_size = key_value_page_store.shape[4]
    head_dim = key_value_page_store.shape[5]
    prefix_pages = pages_here - FIN_DEV
    row_count = queries.shape[1]
    pages_landed = shifted(key_value_page_store[:, prefix_pages:], "section", 1)
    key_pages, head_new = to_heads(
        jnp.concatenate([key_value_page_store, pages_landed], axis=1), fresh_key_value
    )
    key_rows = jnp.concatenate([key_pages[:, 0].reshape((-1, head_dim)), head_new[:, 0]], axis=0)
    value_rows = jnp.concatenate([key_pages[:, 1].reshape((-1, head_dim)), head_new[:, 1]], axis=0)
    slot_count = key_pages.shape[0]
    visible = build_visible(
        is_prefill,
        prefix_len,
        page_table,
        context_len,
        slot_count,
        pages_here + FIN_DEV,
        prefix_pages,
        page_size,
        row_count,
    )
    heads_here = queries.shape[2] // head_dim
    head_queries = queries[0].reshape((row_count, heads_here, head_dim)).transpose(1, 0, 2)
    factor = 1.0 / math.sqrt(head_dim)
    outputs = lax.map(
        partial(
            attend_head, key_rows=key_rows, value_rows=value_rows, visible=visible, factor=factor
        ),
        head_queries,
    )
    return outputs.transpose(1, 0, 2).reshape((1, row_count, heads_here * head_dim))


def solution(mesh):
    placed = (
        P(("pairs", "section"), None, "tp"),
        P(("pairs", "section"), "tp", None, None, None),
        P(("pairs", "section"), "tp", None, None, None, None),
        P("pairs"),
        P("pairs", None),
        P("pairs"),
    )
    return jax.shard_map(
        body,
        mesh=mesh,
        in_specs=placed,
        out_specs=P(("pairs", "section"), None, "tp"),
        check_vma=False,
    )
```

profile of v0, /device:TPU:0, one launch (start us, length us, event | category | flops | bytes accessed | tf_op | source)
XLA Modules:
  0.0 81.4 jit_solution(10468656105959847996)
XLA Ops:
  0.0 0.9 %copy.39 = bf16[1,12,2,8,128]{4,2,3,1,0:T(2,128)(2,1)S(1)} copy(bf16[1,12,2,8,128]{4,3,2,1,0:T(8,128)(2,1)} %param.9) | data formatting | bytes 98304 | tf_op args[1]
  1.0 0.7 gather_fusion.1
  1.7 0.7 fusion.11
  2.4 7.3 %all-to-all-start.1 = ((bf16[1,12,2,8,128]{4,2,1,0,3:T(2,128)(2,1)}), bf16[1,12,2,8,128]{4,2,1,0,3:T(2,128)(2,1)S(1)}, u32[]{:S(2)}, u32[]{:S(2)}) async-start(bf16[1,12,2,8,128]{4,2,1,0,3:T(2,128)(2,1)} %fusion.11), calls=%async_computation.1 | async-start | bytes 98304 | tf_op jit(solution)/shard_map/all_to_all | solution.py:94
  9.7 1.1 %slice.15 = bf16[1,1,2,8,128,128]{5,4,3,2,1,0:T(8,128)(2,1)S(1)} slice(bf16[1,2,2,8,128,128]{5,4,3,2,1,0:T(8,128)(2,1)} %param.10), slice={[0:1], [1:2], [0:2], [0:8], [0:128], [0:128]} | slice | bytes 1048576 | tf_op jit(solution)/shard_map/slice | solution.py:108
  10.7 1.5 %collective-permute-start = (bf16[1,1,2,8,128,128]{5,4,3,2,1,0:T(8,128)(2,1)S(1)}, bf16[1,1,2,8,128,128]{5,4,3,2,1,0:T(8,128)(2,1)S(1)}, u32[]{:S(2)}, u32[]{:S(2)}) collective-permute-start(bf16[1,1,2,8,128,128]{5,4,3,2,1,0:T(8,128)(2,1)S(1)} %slice.15), channel_id=1, source_target_pairs={{0,8},{1,9},{2,10},{3,11},{4,12},{5,13},{6,14},{7,15},{16,24},{17,... | collective-permute-start | bytes 1572872 | tf_op jit(solution)/shard_map/ppermute | solution.py:15
  12.3 0.7 broadcast_compare_fusion
  13.0 0.8 convert_reduce_fusion
  14.0 0.8 %gather_fusion = bf16[8,3,2,128,128]{4,3,2,1,0:T(8,128)(2,1)S(1)} fusion(bf16[3,2,8,128,128]{4,3,2,1,0:T(8,128)(2,1)S(1)} %maximum_bitcast_fusion, s32[1024]{0:T(1024)S(1)} %pad_clamp_fusion), kind=kCustom, calls=%fused_computation | custom fusion | bytes 3145760 | tf_op jit(solution)/shard_map/jit(_take)/gather | solution.py:85
  14.8 1.4 %bitcast_select_fusion = bf16[1,3,2,8,128,128]{5,4,2,1,0,3:T(8,128)(2,1)} fusion(bf16[8,3,2,128,128]{4,3,2,1,0:T(8,128)(2,1)S(1)} %gather_fusion, pred[8]{0:T(512)(128)(4,1)S(1)} %compare_and_fusion.2), kind=kLoop, calls=%fused_computation.16 | loop fusion | flops 786432 | bytes 3145736 | tf_op jit(solution)/shard_map/jit(_take)/select_n | solution.py:85
  16.5 5.7 %all-to-all-start = ((bf16[1,3,2,8,128,128]{5,4,2,1,0,3:T(8,128)(2,1)}), bf16[1,3,2,8,128,128]{5,4,2,1,0,3:T(8,128)(2,1)S(1)}, u32[]{:S(2)}, u32[]{:S(2)}) async-start(bf16[1,3,2,8,128,128]{5,4,2,1,0,3:T(8,128)(2,1)} %bitcast_select_fusion), calls=%async_computation | async-start | bytes 3145728 | tf_op jit(solution)/shard_map/all_to_all | solution.py:93
  23.9 35.8 %all-to-all-done = bf16[1,3,2,8,128,128]{5,4,2,1,0,3:T(8,128)(2,1)S(1)} async-done(((bf16[1,3,2,8,128,128]{5,4,2,1,0,3:T(8,128)(2,1)}), bf16[1,3,2,8,128,128]{5,4,2,1,0,3:T(8,128)(2,1)S(1)}, u32[]{:S(2)}, u32[]{:S(2)}) %all-to-all-start) | async-done | bytes 1572896 | tf_op jit(solution)/shard_map/all_to_all | solution.py:93
  59.8 20.5 %while.10 = (s32[]{:T(128)}, bf16[16,96,128]{2,1,0:T(8,128)(2,1)S(1)}, bf16[16,96,128]{2,1,0:T(8,128)(2,1)S(1)}, bf16[3168,128]{1,0:T(8,128)(2,1)S(1)}, pred[96,...) while((s32[]{:T(128)}, bf16[16,96,128]{2,1,0:T(8,128)(2,1)S(1)}, ...), condition=%wide.region_7.8_spmd, body=%wide.region_4.7_spmd.sunk | while | flops 157866816 | bytes 5642453 | solution.py:129
  59.9 0.5 fusion.52
  61.1 0.5 fusion.52
  62.4 0.5 fusion.52
  63.7 0.5 fusion.52
  66.3 0.5 fusion.52
  68.8 0.5 fusion.52
  71.4 0.5 fusion.52
  73.9 0.5 fusion.52
  76.5 0.5 fusion.52
  79.1 0.5 fusion.52
  80.5 0.9 %reshape.267 = bf16[1,96,2048]{2,1,0:T(8,128)(2,1)} reshape(bf16[96,16,128]{2,1,0:T(8,128)(2,1)S(1)} %copy.32) | data formatting | bytes 786432 | tf_op jit(solution)/shard_map/reshape | solution.py:135
  (72 shorter events, 16.9 us)
Async XLA Ops:
  0.0 13.8 %copy-start = (bf16[1,2,2,8,128,128]{5,4,3,2,1,0:T(8,128)(2,1)S(1)}, bf16[1,2,2,8,128,128]{5,4,3,2,1,0:T(8,128)(2,1)}, u32[]{:S(2)}) copy-start(bf16[1,2,2,8,128,128]{5,4,3,2,1,0:T(8,128)(2,1)} %param.10) | copy-start | bytes 3145732
  2.4 14.1 %all-to-all-start.1 = ((bf16[1,12,2,8,128]{4,2,1,0,3:T(2,128)(2,1)}), bf16[1,12,2,8,128]{4,2,1,0,3:T(2,128)(2,1)S(1)}, u32[]{:S(2)}, u32[]{:S(2)}) async-start(bf16[1,12,2,8,128]{4,2,1,0,3:T(2,128)(2,1)} %fusion.11), calls=%async_computation.1 | async-start | bytes 98304 | tf_op jit(solution)/shard_map/all_to_all | solution.py:94
  10.7 3.1 %collective-permute-start = (bf16[1,1,2,8,128,128]{5,4,3,2,1,0:T(8,128)(2,1)S(1)}, bf16[1,1,2,8,128,128]{5,4,3,2,1,0:T(8,128)(2,1)S(1)}, u32[]{:S(2)}, u32[]{:S(2)}) collective-permute-start(bf16[1,1,2,8,128,128]{5,4,3,2,1,0:T(8,128)(2,1)S(1)} %slice.15), channel_id=1, source_target_pairs={{0,8},{1,9},{2,10},{3,11},{4,12},{5,13},{6,14},{7,15},{16,24},{17,... | collective-permute-start | bytes 1572872 | tf_op jit(solution)/shard_map/ppermute | solution.py:15
  16.2 6.7 %copy-start.2 = (s32[16]{0:T(128)S(1)}, s32[16]{0:T(128)}, u32[]{:S(2)}) copy-start(s32[16]{0:T(128)} %param.13) | copy-start | bytes 196
  16.2 6.8 %copy-start.1 = (bf16[1,96,2048]{2,1,0:T(8,128)(2,1)S(1)}, bf16[1,96,2048]{2,1,0:T(8,128)(2,1)}, u32[]{:S(2)}) copy-start(bf16[1,96,2048]{2,1,0:T(8,128)(2,1)} %param.8) | copy-start | bytes 1179652
  16.5 43.2 %all-to-all-start = ((bf16[1,3,2,8,128,128]{5,4,2,1,0,3:T(8,128)(2,1)}), bf16[1,3,2,8,128,128]{5,4,2,1,0,3:T(8,128)(2,1)S(1)}, u32[]{:S(2)}, u32[]{:S(2)}) async-start(bf16[1,3,2,8,128,128]{5,4,2,1,0,3:T(8,128)(2,1)} %bitcast_select_fusion), calls=%async_computation | async-start | bytes 3145728 | tf_op jit(solution)/shard_map/all_to_all | solution.py:93
where the time goes:
time: 81.8 us; the launch traced here: 81.4 us
  waiting for transfers between devices  36 us (44%)
  matrix products  14.6 us (18%)
  starting transfers between devices  14.5 us (18%)
  other arithmetic  9.86 us (12%)
  local copies, waits for them, and re-layouts  5.2 us (6%)
  between operations  0.86 us (1%)
    all_to_all x1, waiting for transfers between devices, to_heads(): lax.all_to_all(spread(pages, tp_count), 'tp', split_axis=3, concat_axis=1...  35.8 us
    dot_general x16, matrix products, attend_head(): lax.dot_general(head_query, key_rows, (((1,), (1,)), ((), ())), preferred...  8.02 us
    all_to_all x1, starting transfers between devices, to_heads(): lax.all_to_all(spread(new_rows, tp_count), 'tp', split_axis=3, concat_axi...  7.28 us
    dot_general x16, matrix products, attend_head(): jnp.dot(weights, value_rows, preferred_element_type=jnp.float32)  6.61 us
    all_to_all x1, starting transfers between devices, to_heads(): lax.all_to_all(spread(pages, tp_count), 'tp', split_axis=3, concat_axis=1...  5.7 us
    reduce_sum x16, other arithmetic, attend_head(): denominator = jnp.sum(raw_weights, axis=1, keepdims=True)  5.47 us
    select_n x3, other arithmetic, spread(): return jnp.take(pieces, chosen, axis=3)  2.11 us
  transfers between devices with their start and end apart: 3, of which 2 were waited for; matrix products, arithmetic and copies ran while one was open for 7% of the time, Pallas kernels for 0%

commit v1 on v0

v1 whole, which is shorter than its diff:
```python
import functools
import math

import jax
import jax.numpy as jnp
from jax import lax
from jax.experimental import pallas as pl
from jax.experimental.pallas import tpu as pltpu
from jax.sharding import PartitionSpec as P

FIN_DEV = 1
ROW_TILE = 16
MASKED = -1e30
LOG2_E = 1.4426950408889634


def round_up(value, multiple):
    return -(-value // multiple) * multiple


def shift_pairs(size, by):
    return [(i, (i + by) % size) for i in range(size)]


def dot_keys(left, keys):
    return lax.dot_general(
        left, keys, (((1,), (1,)), ((), ())), preferred_element_type=jnp.float32
    )


def weigh(scores, scale):
    highest = jnp.max(scores, axis=1, keepdims=True)
    raw = jnp.exp2((scores - highest) * scale)
    return raw, jnp.sum(raw, axis=1, keepdims=True)


def attend_kernel(
    sizes,
    meta_ref,
    prefix_ref,
    table_ref,
    context_ref,
    queries_ref,
    row_queries_ref,
    *refs,
):
    tp, pages_here, page, new_rows, new_pad, dec_rows, steps, heads = sizes
    prefix_pages = pages_here - FIN_DEV
    per_device = pages_here + FIN_DEV
    chunks, relayed = refs[:tp], refs[tp : 2 * tp]
    out_ref, keys_ref, values_ref, new_keys_ref, new_values_ref, held_ref, sems = refs[2 * tp :]
    me = meta_ref[1]
    head_dim = queries_ref.shape[1] // heads
    scale = LOG2_E / math.sqrt(head_dim)
    row_count = steps * dec_rows
    new_at = pages_here * 2 * page

    def source(d):
        return lax.rem(me + tp - d, tp)

    def load(pages_of):
        copies = []
        for d in range(tp):
            for chunk, at, slot in pages_of(d, source(d)):
                copies.append((chunk.at[pl.ds(at, page)], keys_ref.at[slot]))
                copies.append((chunk.at[pl.ds(at + page, page)], values_ref.at[slot]))
            rows = pl.ds(pl.multiple_of(source(d) * new_pad, new_pad), new_pad)
            copies.append((chunks[d].at[pl.ds(new_at, new_pad)], new_keys_ref.at[rows]))
            copies.append(
                (chunks[d].at[pl.ds(new_at + new_pad, new_pad)], new_values_ref.at[rows])
            )
        started = [
            pltpu.make_async_copy(src, dst, sems.at[i]) for i, (src, dst) in enumerate(copies)
        ]
        for copy in started:
            copy.start()
        for copy in started:
            copy.wait()

    column = lax.broadcasted_iota(jnp.int32, (1, tp * new_pad), 1)
    new_index = (column // new_pad) * new_rows + lax.rem(column, new_pad)
    new_real = lax.rem(column, new_pad) < new_rows

    @pl.when(meta_ref[0] == 0)
    def prefill():
        load(
            lambda d, j: [
                (chunks[d], q * 2 * page, j * prefix_pages + q) for q in range(prefix_pages)
            ]
        )
        cached = tp * prefix_pages
        key_rows = keys_ref[:cached].reshape((cached * page, head_dim))
        value_rows = values_ref[:cached].reshape((cached * page, head_dim))
        cached_ok = (
            lax.broadcasted_iota(jnp.int32, (1, cached * page), 1) < prefix_ref[0]
        )
        query_index = lax.broadcasted_iota(jnp.int32, (row_count, 1), 0)
        new_ok = new_real & (new_index <= query_index)

        def one_head(h, carry):
            columns = pl.ds(pl.multiple_of(h * head_dim, head_dim), head_dim)
            query = queries_ref[:, columns]
            scores = jnp.where(cached_ok, dot_keys(query, key_rows), MASKED)
            new_scores = jnp.where(new_ok, dot_keys(query, new_keys_ref[...]), MASKED)
            highest = jnp.maximum(
                jnp.max(scores, axis=1, keepdims=True), jnp.max(new_scores, axis=1, keepdims=True)
            )
            raw = jnp.exp2((scores - highest) * scale)
            new_raw = jnp.exp2((new_scores - highest) * scale)
            total = jnp.sum(raw, axis=1, keepdims=True) + jnp.sum(new_raw, axis=1, keepdims=True)
            summed = jnp.dot(
                raw.astype(jnp.bfloat16), value_rows, preferred_element_type=jnp.float32
            ) + jnp.dot(
                new_raw.astype(jnp.bfloat16),
                new_values_ref[...],
                preferred_element_type=jnp.float32,
            )
            out_ref[:, columns] = (summed / total).astype(out_ref.dtype)
            return carry

        lax.fori_loop(0, heads, one_head, 0)

    @pl.when(meta_ref[0] != 0)
    def decode():
        load(
            lambda d, j: [
                (chunks[d], q * 2 * page, j * per_device + q) for q in range(pages_here)
            ]
            + [
                (relayed[d], (prefix_pages + q) * 2 * page, j * per_device + pages_here + q)
                for q in range(FIN_DEV)
            ]
        )
        row_pad = row_queries_ref.shape[1]
        max_entries = table_ref.shape[1]
        slot = lax.broadcasted_iota(jnp.int32, (1, page), 1)
        query_step = lax.broadcasted_iota(jnp.int32, (row_pad, 1), 0) // heads
        new_row = jnp.where(new_real, lax.rem(new_index, dec_rows), -1)
        new_early = (new_index // dec_rows) <= query_step

        def one_row(r, carry):
            query = row_queries_ref[r]
            length = context_ref[r]
            slots = [
                jnp.clip(table_ref[r, m], 0, tp * per_device - 1) for m in range(max_entries)
            ]
            scores = [
                jnp.where(slot < length - m * page, dot_keys(query, keys_ref[slots[m]]), MASKED)
                for m in range(max_entries)
            ]
            scores.append(
                jnp.where(
                    new_early & (new_row == r), dot_keys(query, new_keys_ref[...]), MASKED
                )
            )
            raw, total = weigh(jnp.concatenate(scores, axis=1), scale)
            raw = raw.astype(jnp.bfloat16)
            summed = jnp.dot(
                raw[:, max_entries * page :],
                new_values_ref[...],
                preferred_element_type=jnp.float32,
            )
            for m in range(max_entries):
                summed += jnp.dot(
                    raw[:, m * page : (m + 1) * page],
                    values_ref[slots[m]],
                    preferred_element_type=jnp.float32,
                )
            held_ref[pl.ds(pl.multiple_of(r * row_pad, row_pad), row_pad), :] = summed / total
            return carry

        lax.fori_loop(0, dec_rows, one_row, 0)
        for s in range(steps):
            for h in range(heads):
                out_ref[s * dec_rows : (s + 1) * dec_rows, h * head_dim : (h + 1) * head_dim] = (
                    held_ref[pl.ds(s * heads + h, dec_rows, stride=row_pad), :]
                ).astype(out_ref.dtype)


def attend(meta, prefix_len, page_table, context_len, queries, chunks, relayed, sizes):
    tp, pages_here, page, new_rows, new_pad, dec_rows, steps, heads = sizes
    row_count, width = queries.shape
    head_dim = width // heads
    row_pad = round_up(steps * heads, ROW_TILE)
    row_queries = queries.reshape((steps, dec_rows, heads, head_dim)).transpose(1, 0, 2, 3)
    row_queries = row_queries.reshape((dec_rows, steps * heads, head_dim))
    row_queries = jnp.pad(row_queries, ((0, 0), (0, row_pad - steps * heads), (0, 0)))
    slots = tp * (pages_here + FIN_DEV)
    smem = pl.BlockSpec(memory_space=pltpu.SMEM)
    vmem = pl.BlockSpec(memory_space=pltpu.VMEM)
    anywhere = pl.BlockSpec(memory_space=pl.ANY)
    flops = 4 * row_count * width * (tp * page + row_count)
    return pl.pallas_call(
        functools.partial(attend_kernel, sizes),
        out_shape=jax.ShapeDtypeStruct((row_count, width), queries.dtype),
        in_specs=[smem] * 4 + [vmem] * 2 + [anywhere] * (2 * tp),
        out_specs=vmem,
        scratch_shapes=[
            pltpu.VMEM((slots, page, head_dim), queries.dtype),
            pltpu.VMEM((slots, page, head_dim), queries.dtype),
            pltpu.VMEM((tp * new_pad, head_dim), queries.dtype),
            pltpu.VMEM((tp * new_pad, head_dim), queries.dtype),
            pltpu.VMEM((dec_rows * row_pad, head_dim), jnp.float32),
            pltpu.SemaphoreType.DMA((tp * (2 * (pages_here + FIN_DEV) + 2),)),
        ],
        compiler_params=pltpu.CompilerParams(vmem_limit_bytes=40 * 1024 * 1024),
        cost_estimate=pl.CostEstimate(
            flops=flops, bytes_accessed=4 * slots * page * head_dim, transcendentals=0
        ),
        name="attend",
    )(meta, prefix_len, page_table, context_len, queries, row_queries, *chunks, *relayed)


def body(queries, fresh_key_value, key_value_page_store, prefix_len, page_table, context_len):
    tp = lax.axis_size("tp")
    section, me = lax.axis_index("section"), lax.axis_index("tp")
    store, fresh = key_value_page_store[0], fresh_key_value[0]
    pages_here, _, kv_heads, page, head_dim = store.shape
    new_rows = fresh.shape[0]
    new_pad = round_up(new_rows, ROW_TILE)
    heads = queries.shape[2] // head_dim
    dec_rows = page_table.shape[0]
    steps = queries.shape[1] // dec_rows

    def chunk_for(device):
        head = device * kv_heads // tp
        pages = lax.dynamic_index_in_dim(store, head, axis=2, keepdims=False)
        new = lax.dynamic_index_in_dim(fresh, head, axis=2, keepdims=False).transpose(1, 0, 2)
        new = jnp.pad(new, ((0, 0), (0, new_pad - new_rows), (0, 0)))
        return jnp.concatenate([pages.reshape((-1, head_dim)), new.reshape((-1, head_dim))])

    chunks = [chunk_for(me)]
    for d in range(1, tp):
        chunks.append(
            lax.ppermute(chunk_for(lax.rem(me + d, tp)), "tp", shift_pairs(tp, d))
        )
    relayed = [lax.ppermute(chunk, "section", [(0, 1), (1, 0)]) for chunk in chunks]
    sizes = (tp, pages_here, page, new_rows, new_pad, dec_rows, steps, heads)
    meta = jnp.stack([section, me]).astype(jnp.int32)
    out = attend(meta, prefix_len, page_table, context_len, queries[0], chunks, relayed, sizes)
    return out[None]


def solution(mesh):
    placed = (
        P(("pairs", "section"), None, "tp"),
        P(("pairs", "section"), "tp", None, None, None),
        P(("pairs", "section"), "tp", None, None, None, None),
        P("pairs"),
        P("pairs", None),
        P("pairs"),
    )
    return jax.shard_map(
        body,
        mesh=mesh,
        in_specs=placed,
        out_specs=P(("pairs", "section"), None, "tp"),
        check_vma=False,
    )
```

time: 81.8 us -> 48.3 us (0.59)
  the two profiles are of different devices: /device:TPU:0 before, /device:TPU:13 now
where the time goes in v1:
time: 48.3 us; the launch traced here: 48.1 us
  starting transfers between devices  25.2 us (52%)
  Pallas kernels  13.9 us (29%)
  waiting for transfers between devices  4.61 us (10%)
  local copies, waits for them, and re-layouts  3.31 us (7%)
  between operations  0.92 us (2%)
    ppermute x8, starting transfers between devices, body(): lax.ppermute(chunk, 'section', [(0, 1), (1, 0)])  16.5 us
    pallas_call x1, Pallas kernels, attend(): pl.pallas_call(functools.partial(attend_kernel, sizes), out_shape=jax.Sha...  13.9 us
    ppermute x7, starting transfers between devices, body(): lax.ppermute(chunk_for(lax.rem(me + d, tp)), 'tp', shift_pairs(tp, d))  8.68 us
    ppermute x7, waiting for transfers between devices, body(): lax.ppermute(chunk_for(lax.rem(me + d, tp)), 'tp', shift_pairs(tp, d))  4.53 us
    unnamed x18, local copies, waits for them, and re-layouts  1.66 us
    dynamic_slice x1, local copies, waits for them, and re-layouts, chunk_for(): pages = lax.dynamic_index_in_dim(store, head, axis=2, keepdims=False)  1.41 us
  transfers between devices with their start and end apart: 15, of which 4 were waited for; matrix products, arithmetic and copies ran while one was open for 1% of the time, Pallas kernels for 0%

profile of v1, /device:TPU:13, one launch (start us, length us, event | category | flops | bytes accessed | tf_op | source)
XLA Modules:
  0.0 48.1 jit_solution(11261567264209864827)
XLA Ops:
  0.0 0.8 %copy-done.2 = bf16[1,12,2,8,128]{4,3,2,1,0:T(8,128)(2,1)S(1)} copy-done((bf16[1,12,2,8,128]{4,3,2,1,0:T(8,128)(2,1)S(1)}, bf16[1,12,2,8,128]{4,3,2,1,0:T(8,128)(2,1)}, u32[]{:S(2)}) %copy-start.2) | copy-done | bytes 49176
  0.8 0.1 constant_dynamic-slice_fusion
  0.9 1.4 %constant_dynamic-slice_fusion.1 = (bf16[1,2,2,1,128,128]{5,4,3,2,1,0:T(8,128)(2,1)S(1)}, bf16[1,2,2,1,128,128]{5,4,3,2,1,0:T(8,128)(2,1)S(1)}, bf16[1,2,2,1,128...) fusion(bf16[1,2,2,8,128,128]{5,4,3,2,1,0:T(8,128)(2,1)} %param., ...), kind=kLoop, calls=%fused_computation.17 | loop fusion | bytes 2097184 | tf_op jit(solution)/shard_map/jit(dynamic_index_in_dim)/dynamic_slice | solution.py:227
  2.4 0.2 collective-permute-start.5
  2.7 1.3 %collective-permute-start = (bf16[544,128]{1,0:T(8,128)(2,1)S(1)}, bf16[544,128]{1,0:T(8,128)(2,1)S(1)}, u32[]{:S(2)}, u32[]{:S(2)}) collective-permute-start(bf16[544,128]{1,0:T(8,128)(2,1)S(1)} %pad_maximum_fusion.1), channel_id=1, source_target_pairs={{0,1},{1,2},{2,3},{3,4},{4,5},{5,6},{6,7},{7,0},{8,9},{9,10},{10,1... | collective-permute-start | bytes 417800 | tf_op jit(solution)/shard_map/ppermute | solution.py:235
  4.0 1.3 %collective-permute-start.1 = (bf16[544,128]{1,0:T(8,128)(2,1)S(1)}, bf16[544,128]{1,0:T(8,128)(2,1)S(1)}, u32[]{:S(2)}, u32[]{:S(2)}) collective-permute-start(bf16[544,128]{1,0:T(8,128)(2,1)S(1)} %pad_maximum_fusion.2), channel_id=1, source_target_pairs={{0,2},{1,3},{2,4},{3,5},{4,6},{5,7},{6,0},{7,1},{8,10},{9,11},{10,... | collective-permute-start | bytes 417800 | tf_op jit(solution)/shard_map/ppermute | solution.py:235
  5.4 4.1 %collective-permute-start.2 = (bf16[544,128]{1,0:T(8,128)(2,1)S(1)}, bf16[544,128]{1,0:T(8,128)(2,1)S(1)}, u32[]{:S(2)}, u32[]{:S(2)}) collective-permute-start(bf16[544,128]{1,0:T(8,128)(2,1)S(1)} %pad_maximum_fusion.3), channel_id=1, source_target_pairs={{0,3},{1,4},{2,5},{3,6},{4,7},{5,0},{6,1},{7,2},{8,11},{9,12},{10,... | collective-permute-start | bytes 417800 | tf_op jit(solution)/shard_map/ppermute | solution.py:235
  9.6 0.1 collective-permute-start.3
  9.8 1.9 %collective-permute-start.7 = (bf16[544,128]{1,0:T(8,128)(2,1)S(1)}, bf16[544,128]{1,0:T(8,128)(2,1)S(1)}, u32[]{:S(2)}, u32[]{:S(2)}) collective-permute-start(bf16[544,128]{1,0:T(8,128)(2,1)S(1)} %pad_maximum_fusion.refs_0_), channel_id=1, source_target_pairs={{0,8},{8,0},{1,9},{9,1},{2,10},{10,2},{3,11},{11,3},{4,12},{12,4},... | collective-permute-start | bytes 417800 | tf_op jit(solution)/shard_map/ppermute | solution.py:237
  11.7 1.2 %collective-permute-start.4 = (bf16[544,128]{1,0:T(8,128)(2,1)S(1)}, bf16[544,128]{1,0:T(8,128)(2,1)S(1)}, u32[]{:S(2)}, u32[]{:S(2)}) collective-permute-start(bf16[544,128]{1,0:T(8,128)(2,1)S(1)} %pad_maximum_fusion.5), channel_id=1, source_target_pairs={{0,5},{1,6},{2,7},{3,0},{4,1},{5,2},{6,3},{7,4},{8,13},{9,14},{10,... | collective-permute-start | bytes 417800 | tf_op jit(solution)/shard_map/ppermute | solution.py:235
  12.9 2.2 %collective-permute-done.1.refs_2_ = bf16[544,128]{1,0:T(8,128)(2,1)S(1)} collective-permute-done((bf16[544,128]{1,0:T(8,128)(2,1)S(1)}, bf16[544,128]{1,0:T(8,128)(2,1)S(1)}, u32[]{:S(2)}, u32[]{:S(2)}) %collective-permute-start.1) | collective-permute-done | bytes 139296 | tf_op jit(solution)/shard_map/ppermute | solution.py:235
  15.1 0.4 collective-permute-start.6
  15.5 0.2 collective-permute-done.2.refs_3_
  15.6 11.6 %collective-permute-start.13 = (bf16[544,128]{1,0:T(8,128)(2,1)S(1)}, bf16[544,128]{1,0:T(8,128)(2,1)S(1)}, u32[]{:S(2)}, u32[]{:S(2)}) collective-permute-start(bf16[544,128]{1,0:T(8,128)(2,1)S(1)} %collective-permute-done.5.refs_6_), channel_id=1, source_target_pairs={{0,8},{8,0},{1,9},{9,1},{2,10},{10,2},{3,11},{11,3},{4,12},{12,4},... | collective-permute-start | bytes 417800 | tf_op jit(solution)/shard_map/ppermute | solution.py:237
  27.2 1.5 %collective-permute-start.8 = (bf16[544,128]{1,0:T(8,128)(2,1)S(1)}, bf16[544,128]{1,0:T(8,128)(2,1)S(1)}, u32[]{:S(2)}, u32[]{:S(2)}) collective-permute-start(bf16[544,128]{1,0:T(8,128)(2,1)S(1)} %collective-permute-done.refs_1_), channel_id=1, source_target_pairs={{0,8},{8,0},{1,9},{9,1},{2,10},{10,2},{3,11},{11,3},{4,12},{12,4},... | collective-permute-start | bytes 417800 | tf_op jit(solution)/shard_map/ppermute | solution.py:237
  28.8 0.5 %collective-permute-start.10 = (bf16[544,128]{1,0:T(8,128)(2,1)S(1)}, bf16[544,128]{1,0:T(8,128)(2,1)S(1)}, u32[]{:S(2)}, u32[]{:S(2)}) collective-permute-start(bf16[544,128]{1,0:T(8,128)(2,1)S(1)} %collective-permute-done.2.refs_3_), channel_id=1, source_target_pairs={{0,8},{8,0},{1,9},{9,1},{2,10},{10,2},{3,11},{11,3},{4,12},{12,4},... | collective-permute-start | bytes 417800 | tf_op jit(solution)/shard_map/ppermute | solution.py:237
  29.3 2.2 %collective-permute-done.6.refs_7_ = bf16[544,128]{1,0:T(8,128)(2,1)S(1)} collective-permute-done((bf16[544,128]{1,0:T(8,128)(2,1)S(1)}, bf16[544,128]{1,0:T(8,128)(2,1)S(1)}, u32[]{:S(2)}, u32[]{:S(2)}) %collective-permute-start.6) | collective-permute-done | bytes 139296 | tf_op jit(solution)/shard_map/ppermute | solution.py:235
  31.5 0.5 %collective-permute-start.11 = (bf16[544,128]{1,0:T(8,128)(2,1)S(1)}, bf16[544,128]{1,0:T(8,128)(2,1)S(1)}, u32[]{:S(2)}, u32[]{:S(2)}) collective-permute-start(bf16[544,128]{1,0:T(8,128)(2,1)S(1)} %collective-permute-done.3.refs_4_), channel_id=1, source_target_pairs={{0,8},{8,0},{1,9},{9,1},{2,10},{10,2},{3,11},{11,3},{4,12},{12,4},... | collective-permute-start | bytes 417800 | tf_op jit(solution)/shard_map/ppermute | solution.py:237
  32.0 0.5 %collective-permute-start.14 = (bf16[544,128]{1,0:T(8,128)(2,1)S(1)}, bf16[544,128]{1,0:T(8,128)(2,1)S(1)}, u32[]{:S(2)}, u32[]{:S(2)}) collective-permute-start(bf16[544,128]{1,0:T(8,128)(2,1)S(1)} %collective-permute-done.6.refs_7_), channel_id=1, source_target_pairs={{0,8},{8,0},{1,9},{9,1},{2,10},{10,2},{3,11},{11,3},{4,12},{12,4},... | collective-permute-start | bytes 417800 | tf_op jit(solution)/shard_map/ppermute | solution.py:237
  33.2 0.1 copy.18.table_ref
  33.2 0.1 copy.35
  33.4 0.1 pad_add_fusion.meta_ref
  33.5 0.7 %copy-done.1 = s32[16]{0:T(128)S(1)} copy-done((s32[16]{0:T(128)S(1)}, s32[16]{0:T(128)}, u32[]{:S(2)}) %copy-start.1) | copy-done | bytes 88
  34.2 13.9 %attend.1 = bf16[96,2048]{1,0:T(8,128)(2,1)} custom-call(s32[2]{0:T(128)S(1)} %pad_add_fusion.meta_ref, s32[1]{0:T(128)S(6)} %copy.44.prefix_ref, s32[16,4]{1,0:T(8,128)S(1)} %copy.18.table_ref, s32[16]{0:T(128)S(1)} %copy-done.1, bf16[96,2048]{1,0:T(8,128)(2,1)S(1)} %bitcast.60, bf16[16,96,128]{2,1,0:T(8,128)(2,1)S(1)} %bitcast.61, ...), custom_call_target="tpu_custom_call" | custom-call | flops 880803840 | bytes 1572864 | tf_op jit(solution)/shard_map/attend/pallas_call | solution.py:193
  (49 shorter events, 0.4 us)
Async XLA Ops:
  0.0 0.8 %copy-start.2 = (bf16[1,12,2,8,128]{4,3,2,1,0:T(8,128)(2,1)S(1)}, bf16[1,12,2,8,128]{4,3,2,1,0:T(8,128)(2,1)}, u32[]{:S(2)}) copy-start(bf16[1,12,2,8,128]{4,3,2,1,0:T(8,128)(2,1)} %param.7) | copy-start | bytes 147460
  2.4 7.4 %collective-permute-start.5 = (bf16[544,128]{1,0:T(8,128)(2,1)S(1)}, bf16[544,128]{1,0:T(8,128)(2,1)S(1)}, u32[]{:S(2)}, u32[]{:S(2)}) collective-permute-start(bf16[544,128]{1,0:T(8,128)(2,1)S(1)} %pad_maximum_fusion.6), channel_id=1, source_target_pairs={{0,6},{1,7},{2,0},{3,1},{4,2},{5,3},{6,4},{7,5},{8,14},{9,15},{10,... | collective-permute-start | bytes 417800 | tf_op jit(solution)/shard_map/ppermute | solution.py:235
  2.7 9.0 %collective-permute-start = (bf16[544,128]{1,0:T(8,128)(2,1)S(1)}, bf16[544,128]{1,0:T(8,128)(2,1)S(1)}, u32[]{:S(2)}, u32[]{:S(2)}) collective-permute-start(bf16[544,128]{1,0:T(8,128)(2,1)S(1)} %pad_maximum_fusion.1), channel_id=1, source_target_pairs={{0,1},{1,2},{2,3},{3,4},{4,5},{5,6},{6,7},{7,0},{8,9},{9,10},{10,1... | collective-permute-start | bytes 417800 | tf_op jit(solution)/shard_map/ppermute | solution.py:235
  4.0 11.0 %collective-permute-start.1 = (bf16[544,128]{1,0:T(8,128)(2,1)S(1)}, bf16[544,128]{1,0:T(8,128)(2,1)S(1)}, u32[]{:S(2)}, u32[]{:S(2)}) collective-permute-start(bf16[544,128]{1,0:T(8,128)(2,1)S(1)} %pad_maximum_fusion.2), channel_id=1, source_target_pairs={{0,2},{1,3},{2,4},{3,5},{4,6},{5,7},{6,0},{7,1},{8,10},{9,11},{10,... | collective-permute-start | bytes 417800 | tf_op jit(solution)/shard_map/ppermute | solution.py:235
  5.4 10.2 %collective-permute-start.2 = (bf16[544,128]{1,0:T(8,128)(2,1)S(1)}, bf16[544,128]{1,0:T(8,128)(2,1)S(1)}, u32[]{:S(2)}, u32[]{:S(2)}) collective-permute-start(bf16[544,128]{1,0:T(8,128)(2,1)S(1)} %pad_maximum_fusion.3), channel_id=1, source_target_pairs={{0,3},{1,4},{2,5},{3,6},{4,7},{5,0},{6,1},{7,2},{8,11},{9,12},{10,... | collective-permute-start | bytes 417800 | tf_op jit(solution)/shard_map/ppermute | solution.py:235
  9.6 17.7 %collective-permute-start.3 = (bf16[544,128]{1,0:T(8,128)(2,1)S(1)}, bf16[544,128]{1,0:T(8,128)(2,1)S(1)}, u32[]{:S(2)}, u32[]{:S(2)}) collective-permute-start(bf16[544,128]{1,0:T(8,128)(2,1)S(1)} %pad_maximum_fusion.4), channel_id=1, source_target_pairs={{0,4},{1,5},{2,6},{3,7},{4,0},{5,1},{6,2},{7,3},{8,12},{9,13},{10,... | collective-permute-start | bytes 417800 | tf_op jit(solution)/shard_map/ppermute | solution.py:235
  9.7 23.5 %copy-start = (bf16[1,96,2048]{2,1,0:T(8,128)(2,1)S(1)}, bf16[1,96,2048]{2,1,0:T(8,128)(2,1)}, u32[]{:S(2)}) copy-start(bf16[1,96,2048]{2,1,0:T(8,128)(2,1)} %param.6) | copy-start | bytes 1179652
  9.8 18.9 %collective-permute-start.7 = (bf16[544,128]{1,0:T(8,128)(2,1)S(1)}, bf16[544,128]{1,0:T(8,128)(2,1)S(1)}, u32[]{:S(2)}, u32[]{:S(2)}) collective-permute-start(bf16[544,128]{1,0:T(8,128)(2,1)S(1)} %pad_maximum_fusion.refs_0_), channel_id=1, source_target_pairs={{0,8},{8,0},{1,9},{9,1},{2,10},{10,2},{3,11},{11,3},{4,12},{12,4},... | collective-permute-start | bytes 417800 | tf_op jit(solution)/shard_map/ppermute | solution.py:237
  11.7 17.1 %collective-permute-start.4 = (bf16[544,128]{1,0:T(8,128)(2,1)S(1)}, bf16[544,128]{1,0:T(8,128)(2,1)S(1)}, u32[]{:S(2)}, u32[]{:S(2)}) collective-permute-start(bf16[544,128]{1,0:T(8,128)(2,1)S(1)} %pad_maximum_fusion.5), channel_id=1, source_target_pairs={{0,5},{1,6},{2,7},{3,0},{4,1},{5,2},{6,3},{7,4},{8,13},{9,14},{10,... | collective-permute-start | bytes 417800 | tf_op jit(solution)/shard_map/ppermute | solution.py:235
  15.1 16.4 %collective-permute-start.6 = (bf16[544,128]{1,0:T(8,128)(2,1)S(1)}, bf16[544,128]{1,0:T(8,128)(2,1)S(1)}, u32[]{:S(2)}, u32[]{:S(2)}) collective-permute-start(bf16[544,128]{1,0:T(8,128)(2,1)S(1)} %pad_maximum_fusion.7), channel_id=1, source_target_pairs={{0,7},{1,0},{2,1},{3,2},{4,3},{5,4},{6,5},{7,6},{8,15},{9,8},{10,9... | collective-permute-start | bytes 417800 | tf_op jit(solution)/shard_map/ppermute | solution.py:235
  15.6 16.3 %collective-permute-start.13 = (bf16[544,128]{1,0:T(8,128)(2,1)S(1)}, bf16[544,128]{1,0:T(8,128)(2,1)S(1)}, u32[]{:S(2)}, u32[]{:S(2)}) collective-permute-start(bf16[544,128]{1,0:T(8,128)(2,1)S(1)} %collective-permute-done.5.refs_6_), channel_id=1, source_target_pairs={{0,8},{8,0},{1,9},{9,1},{2,10},{10,2},{3,11},{11,3},{4,12},{12,4},... | collective-permute-start | bytes 417800 | tf_op jit(solution)/shard_map/ppermute | solution.py:237
  27.2 4.7 %collective-permute-start.8 = (bf16[544,128]{1,0:T(8,128)(2,1)S(1)}, bf16[544,128]{1,0:T(8,128)(2,1)S(1)}, u32[]{:S(2)}, u32[]{:S(2)}) collective-permute-start(bf16[544,128]{1,0:T(8,128)(2,1)S(1)} %collective-permute-done.refs_1_), channel_id=1, source_target_pairs={{0,8},{8,0},{1,9},{9,1},{2,10},{10,2},{3,11},{11,3},{4,12},{12,4},... | collective-permute-start | bytes 417800 | tf_op jit(solution)/shard_map/ppermute | solution.py:237
  28.7 4.7 %collective-permute-start.9 = (bf16[544,128]{1,0:T(8,128)(2,1)S(1)}, bf16[544,128]{1,0:T(8,128)(2,1)S(1)}, u32[]{:S(2)}, u32[]{:S(2)}) collective-permute-start(bf16[544,128]{1,0:T(8,128)(2,1)S(1)} %collective-permute-done.1.refs_2_), channel_id=1, source_target_pairs={{0,8},{8,0},{1,9},{9,1},{2,10},{10,2},{3,11},{11,3},{4,12},{12,4},... | collective-permute-start | bytes 417800 | tf_op jit(solution)/shard_map/ppermute | solution.py:237
  28.8 4.7 %collective-permute-start.10 = (bf16[544,128]{1,0:T(8,128)(2,1)S(1)}, bf16[544,128]{1,0:T(8,128)(2,1)S(1)}, u32[]{:S(2)}, u32[]{:S(2)}) collective-permute-start(bf16[544,128]{1,0:T(8,128)(2,1)S(1)} %collective-permute-done.2.refs_3_), channel_id=1, source_target_pairs={{0,8},{8,0},{1,9},{9,1},{2,10},{10,2},{3,11},{11,3},{4,12},{12,4},... | collective-permute-start | bytes 417800 | tf_op jit(solution)/shard_map/ppermute | solution.py:237
  31.5 2.0 %collective-permute-start.11 = (bf16[544,128]{1,0:T(8,128)(2,1)S(1)}, bf16[544,128]{1,0:T(8,128)(2,1)S(1)}, u32[]{:S(2)}, u32[]{:S(2)}) collective-permute-start(bf16[544,128]{1,0:T(8,128)(2,1)S(1)} %collective-permute-done.3.refs_4_), channel_id=1, source_target_pairs={{0,8},{8,0},{1,9},{9,1},{2,10},{10,2},{3,11},{11,3},{4,12},{12,4},... | collective-permute-start | bytes 417800 | tf_op jit(solution)/shard_map/ppermute | solution.py:237
  32.0 1.5 %collective-permute-start.12 = (bf16[544,128]{1,0:T(8,128)(2,1)S(1)}, bf16[544,128]{1,0:T(8,128)(2,1)S(1)}, u32[]{:S(2)}, u32[]{:S(2)}) collective-permute-start(bf16[544,128]{1,0:T(8,128)(2,1)S(1)} %collective-permute-done.4.refs_5_), channel_id=1, source_target_pairs={{0,8},{8,0},{1,9},{9,1},{2,10},{10,2},{3,11},{11,3},{4,12},{12,4},... | collective-permute-start | bytes 417800 | tf_op jit(solution)/shard_map/ppermute | solution.py:237
  32.0 1.5 %collective-permute-start.14 = (bf16[544,128]{1,0:T(8,128)(2,1)S(1)}, bf16[544,128]{1,0:T(8,128)(2,1)S(1)}, u32[]{:S(2)}, u32[]{:S(2)}) collective-permute-start(bf16[544,128]{1,0:T(8,128)(2,1)S(1)} %collective-permute-done.6.refs_7_), channel_id=1, source_target_pairs={{0,8},{8,0},{1,9},{9,1},{2,10},{10,2},{3,11},{11,3},{4,12},{12,4},... | collective-permute-start | bytes 417800 | tf_op jit(solution)/shard_map/ppermute | solution.py:237
  32.5 0.7 %copy-start.3 = (s32[16,4]{0,1:T(4,128)S(1)}, s32[16,4]{0,1:T(4,128)}, u32[]{:S(2)}) copy-start(s32[16,4]{0,1:T(4,128)} %param.10) | copy-start | bytes 772
  33.5 0.7 %copy-start.1 = (s32[16]{0:T(128)S(1)}, s32[16]{0:T(128)}, u32[]{:S(2)}) copy-start(s32[16]{0:T(128)} %context_ref.1) | copy-start | bytes 196

commit v2 on v0

v2 whole, which is shorter than its diff:
```python
import functools
import math

import jax
import jax.numpy as jnp
from jax import lax
from jax.experimental import pallas as pl
from jax.experimental.pallas import tpu as pltpu
from jax.sharding import PartitionSpec as P

FIN_DEV = 1
ROW_TILE = 16
LANES = 128
BLOCK_BATCH = 4
MASKED = -1e30
LOG2_E = 1.4426950408889634


def round_up(value, multiple):
    return -(-value // multiple) * multiple


def shift_pairs(size, by):
    return [(i, (i + by) % size) for i in range(size)]


class Sizes:
    def __init__(self, tp, store, fresh, queries, page_table):
        self.tp = tp
        self.pages_here, _, self.kv_heads, self.page, self.head_dim = store
        self.prefix_pages = self.pages_here - FIN_DEV
        self.per_device = self.pages_here + FIN_DEV
        self.new_rows = fresh[0]
        self.new_pad = round_up(self.new_rows, ROW_TILE)
        self.new_keys = tp * self.new_pad
        self.heads = queries[1] // self.head_dim
        self.row_count = queries[0]
        self.dec_rows, self.max_entries = page_table
        self.steps = self.row_count // self.dec_rows
        self.slots = tp * self.per_device
        self.scale = LOG2_E / math.sqrt(self.head_dim)
        self.new_at = self.pages_here * 2 * self.page
        self.prefill_tiles = round_up(self.heads * self.row_count, LANES) // LANES
        self.row_width = round_up(self.steps * self.heads, LANES)
        self.row_tiles = self.row_width // LANES
        self.decode_tiles = self.dec_rows * self.row_tiles
        self.tiles = max(self.prefill_tiles, self.decode_tiles)
        self.prefix_at = 2
        self.context_at = 3
        self.table_at = 3 + self.dec_rows

    def source(self, meta_ref, d):
        return lax.rem(meta_ref[1] + self.tp - d, self.tp)


def score(keys, queries):
    return lax.dot_general(
        keys, queries, (((1,), (1,)), ((), ())), preferred_element_type=jnp.float32
    )


def soften(scores, values, scale):
    highest = jnp.max(scores, axis=0, keepdims=True)
    raw = jnp.exp2((scores - highest) * scale)
    total = jnp.sum(raw, axis=0, keepdims=True)
    summed = lax.dot_general(
        values,
        raw.astype(values.dtype),
        (((0,), (0,)), ((), ())),
        preferred_element_type=jnp.float32,
    )
    return summed, highest, total


def merge(first, second, scale):
    highest = jnp.maximum(first[1], second[1])
    keep = jnp.exp2((first[1] - highest) * scale)
    add = jnp.exp2((second[1] - highest) * scale)
    return (
        first[0] * keep + second[0] * add,
        highest,
        first[2] * keep + second[2] * add,
    )


def read(state, tile):
    return tuple(ref[tile] for ref in state)


def write(state, tile, part):
    for ref, value in zip(state, part):
        ref[tile] = value


def settle(part):
    return (part[0] * (1.0 / part[2])).T


def key_rows(z, count):
    return lax.broadcasted_iota(jnp.int32, (count, LANES), 0)


def add_pages(z, pages, owner_ref, valid_ref, queries_ref, state):
    slot = key_rows(z, z.page)
    for start in range(0, len(pages), BLOCK_BATCH):
        parts = []
        for ref, at, number in pages[start : start + BLOCK_BATCH]:
            visible = slot < valid_ref[number]
            keys, values = ref[at : at + z.page, :], ref[at + z.page : at + 2 * z.page, :]
            for i in range(z.row_tiles):
                tile = owner_ref[number] * z.row_tiles + i
                scores = jnp.where(visible, score(keys, queries_ref[tile]), MASKED)
                parts.append((tile, soften(scores, values, z.scale)))
        for tile, part in parts:
            write(state, tile, merge(read(state, tile), part, z.scale))


def prefix_visible(z, meta_ref, shifts):
    slot = key_rows(z, z.page)
    return [
        slot < meta_ref[z.prefix_at] - (z.source(meta_ref, d) * z.prefix_pages + q) * z.page
        for d in shifts
        for q in range(z.prefix_pages)
    ]


def prefix_rows(z, chunks, shifts, which):
    return [
        chunks[d][(2 * q + which) * z.page : (2 * q + which + 1) * z.page, :]
        for d in shifts
        for q in range(z.prefix_pages)
    ]


def new_rows(z, new_ref, chunks, which):
    sources = [(new_ref, at) for at in range(0, new_ref.shape[0], 2 * z.new_pad)]
    sources += [(chunk, z.new_at) for chunk in chunks]
    rows = [pl.ds(at + which * z.new_pad, z.new_pad) for _, at in sources]
    return [ref[span, :] for (ref, _), span in zip(sources, rows)]


def new_index(z, meta_ref, shifts):
    within = key_rows(z, z.new_pad)
    none = jnp.full_like(within, z.row_count)
    return jnp.concatenate(
        [
            jnp.where(within < z.new_rows, z.source(meta_ref, d) * z.new_rows + within, none)
            for d in shifts
        ],
        axis=0,
    )


def local_pages(z, meta_ref, chunks, shifts):
    return [
        (chunks[d], 2 * q * z.page, z.source(meta_ref, d) * z.per_device + q)
        for d in shifts
        for q in range(z.pages_here)
    ]


def landed_pages(z, meta_ref, landed_ref, shifts):
    return [
        (
            landed_ref,
            2 * (i * FIN_DEV + q) * z.page,
            z.source(meta_ref, d) * z.per_device + z.pages_here + q,
        )
        for i, d in enumerate(shifts)
        for q in range(FIN_DEV)
    ]


def first_kernel(z, shifts, meta_ref, prefill_ref, decode_ref, *refs):
    chunks = dict(zip(shifts, refs))
    owner_ref, valid_ref, packed_ref, new_ref = refs[len(shifts) : len(shifts) + 4]
    state = refs[len(shifts) + 4 :]
    first, last = z.prefix_pages * 2 * z.page, z.new_at
    for i, d in enumerate(shifts):
        packed_ref[i * (last - first) : (i + 1) * (last - first), :] = chunks[d][first:last, :]
        new_ref[i * 2 * z.new_pad : (i + 1) * 2 * z.new_pad, :] = chunks[d][z.new_at :, :]

    def forget(n, carry):
        owner_ref[n] = 0
        valid_ref[n] = 0
        return carry

    def note(r, carry):
        length = meta_ref[z.context_at + r]
        for m in range(z.max_entries):

            @pl.when(m * z.page < length)
            def used():
                number = meta_ref[z.table_at + r * z.max_entries + m]
                number = jnp.clip(number, 0, z.slots - 1)
                owner_ref[number] = r
                valid_ref[number] = jnp.minimum(length - m * z.page, z.page)

        return carry

    lax.fori_loop(0, z.slots, forget, 0)
    lax.fori_loop(0, z.dec_rows, note, 0)

    @pl.when(meta_ref[0] == 0)
    def prefill():
        visible = jnp.concatenate(prefix_visible(z, meta_ref, shifts), axis=0)
        keys = jnp.concatenate(prefix_rows(z, chunks, shifts, 0), axis=0)
        values = jnp.concatenate(prefix_rows(z, chunks, shifts, 1), axis=0)
        for tile in range(z.prefill_tiles):
            scores = jnp.where(visible, score(keys, prefill_ref[tile]), MASKED)
            write(state, tile, soften(scores, values, z.scale))

    @pl.when(meta_ref[0] != 0)
    def decode():
        state[0][...] = jnp.zeros_like(state[0])
        state[1][...] = jnp.full_like(state[1], MASKED)
        state[2][...] = jnp.zeros_like(state[2])
        pages = local_pages(z, meta_ref, chunks, shifts)
        add_pages(z, pages, owner_ref, valid_ref, decode_ref, state)


def second_kernel(z, groups, meta_ref, owner_ref, valid_ref, prefill_ref, decode_ref, *refs):
    shifts = groups[1]
    before, new_ref, refs = refs[:3], refs[3], refs[4:]
    late, state, out_ref, held_ref = refs[: len(shifts)], refs[len(shifts) : -2], refs[-2], refs[-1]
    chunks = dict(zip(shifts, late))
    index = new_index(z, meta_ref, groups[0] + groups[1])
    column = lax.broadcasted_iota(jnp.int32, (1, LANES), 1)
    new_keys = jnp.concatenate(new_rows(z, new_ref, late, 0), axis=0)

    @pl.when(meta_ref[0] == 0)
    def prefill():
        visible = jnp.concatenate(prefix_visible(z, meta_ref, shifts), axis=0)
        keys = jnp.concatenate(prefix_rows(z, chunks, shifts, 0), axis=0)
        values = prefix_rows(z, chunks, shifts, 1) + new_rows(z, new_ref, late, 1)
        values = jnp.concatenate(values, axis=0)
        for tile in range(z.prefill_tiles):
            query = lax.rem(column + tile * LANES, z.row_count)
            scores = jnp.concatenate(
                [
                    jnp.where(visible, score(keys, prefill_ref[tile]), MASKED),
                    jnp.where(index <= query, score(new_keys, prefill_ref[tile]), MASKED),
                ],
                axis=0,
            )
            part = merge(read(before, tile), soften(scores, values, z.scale), z.scale)
            held_ref[tile * LANES : (tile + 1) * LANES, :] = settle(part).astype(held_ref.dtype)
        for h in range(z.heads):
            out_ref[:, h * z.head_dim : (h + 1) * z.head_dim] = held_ref[
                h * z.row_count : (h + 1) * z.row_count, :
            ]

    @pl.when(meta_ref[0] != 0)
    def decode():
        owner = lax.rem(index, z.dec_rows)
        owner = jnp.where(index < z.row_count, owner, -1)
        step = index // z.dec_rows
        new_values = jnp.concatenate(new_rows(z, new_ref, late, 1), axis=0)
        for tile in range(z.decode_tiles):
            row, i = divmod(tile, z.row_tiles)
            query = (column + i * LANES) // z.heads
            visible = (owner == row) & (step <= query)
            scores = jnp.where(visible, score(new_keys, decode_ref[tile]), MASKED)
            part = soften(scores, new_values, z.scale)
            write(state, tile, merge(read(before, tile), part, z.scale))
        pages = local_pages(z, meta_ref, chunks, shifts)
        add_pages(z, pages, owner_ref, valid_ref, decode_ref, state)


def last_kernel(z, groups, meta_ref, owner_ref, valid_ref, decode_ref, *refs):
    landed, refs = refs[: len(groups)], refs[len(groups) :]
    before, done_ref, out_ref, state, held_ref = refs[:3], refs[3], refs[4], refs[5:8], refs[8]

    @pl.when(meta_ref[0] == 0)
    def prefill():
        out_ref[...] = done_ref[...]

    @pl.when(meta_ref[0] != 0)
    def decode():
        for ref, value in zip(state, before):
            ref[...] = value[...]
        pages = []
        for ref, shifts in zip(landed, groups):
            pages += landed_pages(z, meta_ref, ref, shifts)
        add_pages(z, pages, owner_ref, valid_ref, decode_ref, state)
        for tile in range(z.decode_tiles):
            held_ref[tile * LANES : (tile + 1) * LANES, :] = settle(read(state, tile))
        for s in range(z.steps):
            for h in range(z.heads):
                rows = pl.ds(s * z.heads + h, z.dec_rows, stride=z.row_width)
                out_ref[
                    s * z.dec_rows : (s + 1) * z.dec_rows,
                    h * z.head_dim : (h + 1) * z.head_dim,
                ] = held_ref[rows, :].astype(out_ref.dtype)


def call(kernel, z, shifts, name, keys, operands, outputs, scratch=()):
    spaces = {"smem": pltpu.SMEM, "vmem": pltpu.VMEM}
    spec = {key: pl.BlockSpec(memory_space=space) for key, space in spaces.items()}
    return pl.pallas_call(
        functools.partial(kernel, z, shifts),
        out_shape=[shape for _, shape in outputs],
        in_specs=[spec[key] for key, _ in operands],
        out_specs=[spec[key] for key, _ in outputs],
        scratch_shapes=list(scratch),
        compiler_params=pltpu.CompilerParams(vmem_limit_bytes=24 * 1024 * 1024),
        cost_estimate=pl.CostEstimate(
            flops=4 * z.tiles * LANES * keys * z.head_dim,
            bytes_accessed=2 * z.tiles * LANES * z.head_dim * 8,
            transcendentals=z.tiles * LANES * keys,
        ),
        name=name,
    )(*[value for _, value in operands])


def query_tiles(z, queries):
    by_head = queries.reshape((z.row_count, z.heads, z.head_dim)).transpose(1, 0, 2)
    by_head = by_head.reshape((-1, z.head_dim))
    spare = z.prefill_tiles * LANES - by_head.shape[0]
    by_head = jnp.pad(by_head, ((0, spare), (0, 0)))
    by_row = queries.reshape((z.steps, z.dec_rows, z.heads, z.head_dim)).transpose(1, 0, 2, 3)
    by_row = by_row.reshape((z.dec_rows, z.steps * z.heads, z.head_dim))
    by_row = jnp.pad(by_row, ((0, 0), (0, z.row_width - z.steps * z.heads), (0, 0)))
    return (
        by_head.reshape((z.prefill_tiles, LANES, z.head_dim)),
        by_row.reshape((z.decode_tiles, LANES, z.head_dim)),
    )


def hand_over(pages):
    return lax.ppermute(pages, "section", [(0, 1), (1, 0)])


def finished(z, chunks):
    first, last = z.prefix_pages * 2 * z.page, z.new_at
    return jnp.concatenate([chunk[first:last] for chunk in chunks], axis=0)


def attend(z, meta, queries, chunks, early, late):
    prefill, decode = query_tiles(z, queries)
    table = ("smem", jax.ShapeDtypeStruct((z.slots,), jnp.int32))
    state = [
        ("vmem", jax.ShapeDtypeStruct((z.tiles, rows, LANES), jnp.float32))
        for rows in (z.head_dim, 1, 1)
    ]
    out = ("vmem", jax.ShapeDtypeStruct(queries.shape, queries.dtype))
    owner, valid, packed, new, *first = call(
        first_kernel,
        z,
        early,
        "early_pages",
        len(early) * z.page,
        [("smem", meta), ("vmem", prefill), ("vmem", decode)]
        + [("vmem", chunks[d]) for d in early],
        [table, table]
        + [
            ("vmem", jax.ShapeDtypeStruct((len(early) * rows, z.head_dim), queries.dtype))
            for rows in (FIN_DEV * 2 * z.page, 2 * z.new_pad)
        ]
        + state,
    )
    *waiting, owner = lax.optimization_barrier((*chunks, owner))
    landed = [hand_over(packed), hand_over(finished(z, [waiting[d] for d in late]))]
    common = [("smem", meta), ("smem", owner), ("smem", valid)]
    *second, done = call(
        second_kernel,
        z,
        (early, late),
        "late_pages",
        len(late) * z.page + z.new_keys,
        common
        + [("vmem", value) for value in (prefill, decode, *first, new)]
        + [("vmem", waiting[d]) for d in late],
        state + [out],
        [pltpu.VMEM((z.prefill_tiles * LANES, z.head_dim), queries.dtype)],
    )
    (result,) = call(
        last_kernel,
        z,
        (early, late),
        "landed_pages",
        z.page,
        common + [("vmem", value) for value in (decode, *landed, *second, done)],
        [out],
        [pltpu.VMEM(shape.shape, shape.dtype) for _, shape in state]
        + [pltpu.VMEM((z.decode_tiles * LANES, z.head_dim), jnp.float32)],
    )
    return result


def body(queries, fresh_key_value, key_value_page_store, prefix_len, page_table, context_len):
    tp = lax.axis_size("tp")
    section, me = lax.axis_index("section"), lax.axis_index("tp")
    store, fresh = key_value_page_store[0], fresh_key_value[0]
    z = Sizes(tp, store.shape, fresh.shape, queries.shape[1:], page_table.shape)

    def chunk_for(device):
        head = device * z.kv_heads // tp
        pages = lax.dynamic_index_in_dim(store, head, axis=2, keepdims=False)
        new = lax.dynamic_index_in_dim(fresh, head, axis=2, keepdims=False).transpose(1, 0, 2)
        new = jnp.pad(new, ((0, 0), (0, z.new_pad - z.new_rows), (0, 0)))
        return jnp.concatenate([pages.reshape((-1, z.head_dim)), new.reshape((-1, z.head_dim))])

    chunks = [chunk_for(me)]
    for d in range(1, tp):
        chunks.append(lax.ppermute(chunk_for(lax.rem(me + d, tp)), "tp", shift_pairs(tp, d)))
    early = [0, tp - 2] + list(range(1, tp // 2 - 1))
    late = [d for d in range(tp) if d not in early]
    meta = jnp.concatenate(
        [
            jnp.stack([section, me]).astype(jnp.int32),
            prefix_len,
            context_len,
            page_table.reshape((-1,)),
        ]
    )
    return attend(z, meta, queries[0], chunks, early, late)[None]


def solution(mesh):
    placed = (
        P(("pairs", "section"), None, "tp"),
        P(("pairs", "section"), "tp", None, None, None),
        P(("pairs", "section"), "tp", None, None, None, None),
        P("pairs"),
        P("pairs", None),
        P("pairs"),
    )
    return jax.shard_map(
        body,
        mesh=mesh,
        in_specs=placed,
        out_specs=P(("pairs", "section"), None, "tp"),
        check_vma=False,
    )
```

time: 81.8 us -> 43 us (0.53)
  the two profiles are of different devices: /device:TPU:0 before, /device:TPU:13 now
where the time goes in v2:
time: 43 us; the launch traced here: 42.7 us
  Pallas kernels  13 us (30%)
  waiting for transfers between devices  12.7 us (30%)
  starting transfers between devices  11.2 us (26%)
  local copies, waits for them, and re-layouts  4.7 us (11%)
  between operations  1.01 us (2%)
    pallas_call x3, Pallas kernels, call(): pl.pallas_call(functools.partial(kernel, z, shifts), out_shape=[shape for...  13 us
    ppermute x7, waiting for transfers between devices, body(): lax.ppermute(chunk_for(lax.rem(me + d, tp)), 'tp', shift_pairs(tp, d))  12.7 us
    ppermute x7, starting transfers between devices, body(): lax.ppermute(chunk_for(lax.rem(me + d, tp)), 'tp', shift_pairs(tp, d))  10.6 us
    unnamed x22, local copies, waits for them, and re-layouts  1.91 us
    dynamic_slice x1, local copies, waits for them, and re-layouts, chunk_for(): pages = lax.dynamic_index_in_dim(store, head, axis=2, keepdims=False)  1.39 us
  transfers between devices with their start and end apart: 9, of which 2 were waited for; matrix products, arithmetic and copies ran while one was open for 2% of the time, Pallas kernels for 21%

profile of v2, /device:TPU:13, one launch (start us, length us, event | category | flops | bytes accessed | tf_op | source)
XLA Modules:
  0.0 42.7 jit_solution(17789136550154166627)
XLA Ops:
  0.0 0.8 %copy-done.3 = bf16[1,12,2,8,128]{4,3,2,1,0:T(8,128)(2,1)S(1)} copy-done((bf16[1,12,2,8,128]{4,3,2,1,0:T(8,128)(2,1)S(1)}, bf16[1,12,2,8,128]{4,3,2,1,0:T(8,128)(2,1)}, u32[]{:S(2)}) %copy-start.3) | copy-done | bytes 49176
  0.8 0.1 constant_dynamic-slice_fusion
  0.9 1.4 %constant_dynamic-slice_fusion.1 = (bf16[1,2,2,1,128,128]{5,4,3,2,1,0:T(8,128)(2,1)S(1)}, bf16[1,2,2,1,128,128]{5,4,3,2,1,0:T(8,128)(2,1)S(1)}, bf16[1,2,2,1,128...) fusion(bf16[1,2,2,8,128,128]{5,4,3,2,1,0:T(8,128)(2,1)} %param., ...), kind=kLoop, calls=%fused_computation.18 | loop fusion | bytes 2097184 | tf_op jit(solution)/shard_map/jit(dynamic_index_in_dim)/dynamic_slice | solution.py:399
  2.4 0.2 collective-permute-start.5
  2.7 1.3 %collective-permute-start = (bf16[544,128]{1,0:T(8,128)(2,1)S(1)}, bf16[544,128]{1,0:T(8,128)(2,1)S(1)}, u32[]{:S(2)}, u32[]{:S(2)}) collective-permute-start(bf16[544,128]{1,0:T(8,128)(2,1)S(1)} %pad_maximum_fusion.2), channel_id=1, source_target_pairs={{0,1},{1,2},{2,3},{3,4},{4,5},{5,6},{6,7},{7,0},{8,9},{9,10},{10,1... | collective-permute-start | bytes 417800 | tf_op jit(solution)/shard_map/ppermute | solution.py:406
  4.0 1.3 %collective-permute-start.1 = (bf16[544,128]{1,0:T(8,128)(2,1)S(1)}, bf16[544,128]{1,0:T(8,128)(2,1)S(1)}, u32[]{:S(2)}, u32[]{:S(2)}) collective-permute-start(bf16[544,128]{1,0:T(8,128)(2,1)S(1)} %pad_maximum_fusion.3), channel_id=1, source_target_pairs={{0,2},{1,3},{2,4},{3,5},{4,6},{5,7},{6,0},{7,1},{8,10},{9,11},{10,... | collective-permute-start | bytes 417800 | tf_op jit(solution)/shard_map/ppermute | solution.py:406
  5.4 4.1 %collective-permute-start.2 = (bf16[544,128]{1,0:T(8,128)(2,1)S(1)}, bf16[544,128]{1,0:T(8,128)(2,1)S(1)}, u32[]{:S(2)}, u32[]{:S(2)}) collective-permute-start(bf16[544,128]{1,0:T(8,128)(2,1)S(1)} %pad_maximum_fusion.4), channel_id=1, source_target_pairs={{0,3},{1,4},{2,5},{3,6},{4,7},{5,0},{6,1},{7,2},{8,11},{9,12},{10,... | collective-permute-start | bytes 417800 | tf_op jit(solution)/shard_map/ppermute | solution.py:406
  9.6 0.1 collective-permute-start.3
  10.4 0.1 copy.10
  10.5 0.1 reshape.99
  10.7 0.1 copy.19
  10.9 0.6 %copy-done.5 = s32[16]{0:T(128)S(1)} copy-done((s32[16]{0:T(128)S(1)}, s32[16]{0:T(128)}, u32[]{:S(2)}) %copy-start.5) | copy-done | bytes 88
  11.6 0.1 concatenate.30.meta_ref
  11.7 1.2 %collective-permute-start.4 = (bf16[544,128]{1,0:T(8,128)(2,1)S(1)}, bf16[544,128]{1,0:T(8,128)(2,1)S(1)}, u32[]{:S(2)}, u32[]{:S(2)}) collective-permute-start(bf16[544,128]{1,0:T(8,128)(2,1)S(1)} %pad_maximum_fusion.6), channel_id=1, source_target_pairs={{0,5},{1,6},{2,7},{3,0},{4,1},{5,2},{6,3},{7,4},{8,13},{9,14},{10,... | collective-permute-start | bytes 417800 | tf_op jit(solution)/shard_map/ppermute | solution.py:406
  12.9 2.3 %collective-permute-start.6 = (bf16[544,128]{1,0:T(8,128)(2,1)S(1)}, bf16[544,128]{1,0:T(8,128)(2,1)S(1)}, u32[]{:S(2)}, u32[]{:S(2)}) collective-permute-start(bf16[544,128]{1,0:T(8,128)(2,1)S(1)} %pad_maximum_fusion.8), channel_id=1, source_target_pairs={{0,7},{1,0},{2,1},{3,2},{4,3},{5,4},{6,5},{7,6},{8,15},{9,8},{10,9... | collective-permute-start | bytes 417800 | tf_op jit(solution)/shard_map/ppermute | solution.py:406
  15.2 3.5 %early_pages.1 = (s32[24]{0:T(128)S(1)}, s32[24]{0:T(128)S(1)}, bf16[1024,128]{1,0:T(8,128)(2,1)S(1)}, bf16[128,128]{1,0:T(8,128)(2,1)S(1)}, f32[16,128,128]{2,1...) custom-call(s32[83]{0:T(128)S(1)} %concatenate.30.meta_ref, bf16[12,128,128]{2,1,0:T(8,128)(2,1)S(1)} %bitcast.64, ...), custom_call_target="tpu_custom_call" | custom-call | flops 536870912 | bytes 4194304 | tf_op jit(solution)/shard_map/early_pages/pallas_call | solution.py:300
  18.8 8.1 %collective-permute-done.3.refs_5_ = bf16[544,128]{1,0:T(8,128)(2,1)S(1)} collective-permute-done((bf16[544,128]{1,0:T(8,128)(2,1)S(1)}, bf16[544,128]{1,0:T(8,128)(2,1)S(1)}, u32[]{:S(2)}, u32[]{:S(2)}) %collective-permute-start.3) | collective-permute-done | bytes 139296 | tf_op jit(solution)/shard_map/ppermute | solution.py:406
  26.9 4.6 %collective-permute-done.6.refs_7_ = bf16[544,128]{1,0:T(8,128)(2,1)S(1)} collective-permute-done((bf16[544,128]{1,0:T(8,128)(2,1)S(1)}, bf16[544,128]{1,0:T(8,128)(2,1)S(1)}, u32[]{:S(2)}, u32[]{:S(2)}) %collective-permute-start.6) | collective-permute-done | bytes 139296 | tf_op jit(solution)/shard_map/ppermute | solution.py:406
  31.5 0.8 %slice-done = bf16[256,128]{1,0:T(8,128)(2,1)S(1)} async-done(((bf16[544,128]{1,0:T(8,128)(2,1)}), bf16[256,128]{1,0:T(8,128)(2,1)S(1)}, s32[]{:S(2)}) %slice-start) | async-done | bytes 65560 | tf_op jit(solution)/shard_map/slice | solution.py:336
  32.3 0.6 %collective-permute-start.8 = (bf16[1024,128]{1,0:T(8,128)(2,1)S(1)}, bf16[1024,128]{1,0:T(8,128)(2,1)S(1)}, u32[]{:S(2)}, u32[]{:S(2)}) collective-permute-start(bf16[1024,128]{1,0:T(8,128)(2,1)S(1)} %pad_maximum_fusion), channel_id=1, source_target_pairs={{0,8},{8,0},{1,9},{9,1},{2,10},{10,2},{3,11},{11,3},{4,12},{12,4},... | collective-permute-start | bytes 786440 | tf_op jit(solution)/shard_map/ppermute | solution.py:331
  32.9 0.1 collective-permute-start.7
  33.0 0.2 copy-done.1
  33.2 5.6 %late_pages.1 = (f32[16,128,128]{2,1,0:T(8,128)S(1)}, f32[16,1,128]{2,1,0:T(1,128)S(1)}, f32[16,1,128]{2,1,0:T(1,128)S(1)}, bf16[96,2048]{1,0:T(8,128)(2,1)S(1)}) custom-call(s32[83]{0:T(128)S(1)} %concatenate.30.meta_ref, s32[24]{0:T(128)S(1)} %get-tuple-element.22.owner_ref, s32[24]{0:T(128)S(1)} %get-tuple-element.23.valid_ref, ...), custom_call_target="tpu_custom_call" | custom-call | flops 671088640 | bytes 4194304 | tf_op jit(solution)/shard_map/late_pages/pallas_call | solution.py:300
  38.8 3.9 %landed_pages.1 = bf16[96,2048]{1,0:T(8,128)(2,1)} custom-call(s32[83]{0:T(128)S(1)} %concatenate.30.meta_ref, s32[24]{0:T(128)S(1)} %get-tuple-element.22.owner_ref, s32[24]{0:T(128)S(1)} %get-tuple-element.23.valid_ref, bf16[16,128,128]{2,1,0:T(8,128)(2,1)S(1)} %pad.37.decode_ref, bf16[1024,128]{1,0:T(8,128)(2,1)S(1)} %collective-permute-done.7.refs_0_, ...), custom_call_target="tpu_custom_call" | custom-call | flops 134217728 | bytes 4194304 | tf_op jit(solution)/shard_map/landed_pages/pallas_call | solution.py:300
  (52 shorter events, 0.5 us)
Async XLA Ops:
  0.0 0.8 %copy-start.3 = (bf16[1,12,2,8,128]{4,3,2,1,0:T(8,128)(2,1)S(1)}, bf16[1,12,2,8,128]{4,3,2,1,0:T(8,128)(2,1)}, u32[]{:S(2)}) copy-start(bf16[1,12,2,8,128]{4,3,2,1,0:T(8,128)(2,1)} %param.7) | copy-start | bytes 147460
  2.4 9.3 %collective-permute-start.5 = (bf16[544,128]{1,0:T(8,128)(2,1)S(1)}, bf16[544,128]{1,0:T(8,128)(2,1)S(1)}, u32[]{:S(2)}, u32[]{:S(2)}) collective-permute-start(bf16[544,128]{1,0:T(8,128)(2,1)S(1)} %pad_maximum_fusion.7), channel_id=1, source_target_pairs={{0,6},{1,7},{2,0},{3,1},{4,2},{5,3},{6,4},{7,5},{8,14},{9,15},{10,... | collective-permute-start | bytes 417800 | tf_op jit(solution)/shard_map/ppermute | solution.py:406
  2.7 10.2 %collective-permute-start = (bf16[544,128]{1,0:T(8,128)(2,1)S(1)}, bf16[544,128]{1,0:T(8,128)(2,1)S(1)}, u32[]{:S(2)}, u32[]{:S(2)}) collective-permute-start(bf16[544,128]{1,0:T(8,128)(2,1)S(1)} %pad_maximum_fusion.2), channel_id=1, source_target_pairs={{0,1},{1,2},{2,3},{3,4},{4,5},{5,6},{6,7},{7,0},{8,9},{9,10},{10,1... | collective-permute-start | bytes 417800 | tf_op jit(solution)/shard_map/ppermute | solution.py:406
  4.0 11.2 %collective-permute-start.1 = (bf16[544,128]{1,0:T(8,128)(2,1)S(1)}, bf16[544,128]{1,0:T(8,128)(2,1)S(1)}, u32[]{:S(2)}, u32[]{:S(2)}) collective-permute-start(bf16[544,128]{1,0:T(8,128)(2,1)S(1)} %pad_maximum_fusion.3), channel_id=1, source_target_pairs={{0,2},{1,3},{2,4},{3,5},{4,6},{5,7},{6,0},{7,1},{8,10},{9,11},{10,... | collective-permute-start | bytes 417800 | tf_op jit(solution)/shard_map/ppermute | solution.py:406
  5.4 13.4 %collective-permute-start.2 = (bf16[544,128]{1,0:T(8,128)(2,1)S(1)}, bf16[544,128]{1,0:T(8,128)(2,1)S(1)}, u32[]{:S(2)}, u32[]{:S(2)}) collective-permute-start(bf16[544,128]{1,0:T(8,128)(2,1)S(1)} %pad_maximum_fusion.4), channel_id=1, source_target_pairs={{0,3},{1,4},{2,5},{3,6},{4,7},{5,0},{6,1},{7,2},{8,11},{9,12},{10,... | collective-permute-start | bytes 417800 | tf_op jit(solution)/shard_map/ppermute | solution.py:406
  9.5 1.1 %copy-start.2 = (bf16[1,96,2048]{2,1,0:T(8,128)(2,1)S(1)}, bf16[1,96,2048]{2,1,0:T(8,128)(2,1)}, u32[]{:S(2)}) copy-start(bf16[1,96,2048]{2,1,0:T(8,128)(2,1)} %param.6) | copy-start | bytes 1179652
  9.6 17.3 %collective-permute-start.3 = (bf16[544,128]{1,0:T(8,128)(2,1)S(1)}, bf16[544,128]{1,0:T(8,128)(2,1)S(1)}, u32[]{:S(2)}, u32[]{:S(2)}) collective-permute-start(bf16[544,128]{1,0:T(8,128)(2,1)S(1)} %pad_maximum_fusion.5), channel_id=1, source_target_pairs={{0,4},{1,5},{2,6},{3,7},{4,0},{5,1},{6,2},{7,3},{8,12},{9,13},{10,... | collective-permute-start | bytes 417800 | tf_op jit(solution)/shard_map/ppermute | solution.py:406
  9.7 0.7 %copy-start.4 = (s32[16,4]{0,1:T(4,128)S(1)}, s32[16,4]{0,1:T(4,128)}, u32[]{:S(2)}) copy-start(s32[16,4]{0,1:T(4,128)} %param.10) | copy-start | bytes 772
  10.9 0.7 %copy-start.5 = (s32[16]{0:T(128)S(1)}, s32[16]{0:T(128)}, u32[]{:S(2)}) copy-start(s32[16]{0:T(128)} %param.11) | copy-start | bytes 196
  11.7 15.2 %collective-permute-start.4 = (bf16[544,128]{1,0:T(8,128)(2,1)S(1)}, bf16[544,128]{1,0:T(8,128)(2,1)S(1)}, u32[]{:S(2)}, u32[]{:S(2)}) collective-permute-start(bf16[544,128]{1,0:T(8,128)(2,1)S(1)} %pad_maximum_fusion.6), channel_id=1, source_target_pairs={{0,5},{1,6},{2,7},{3,0},{4,1},{5,2},{6,3},{7,4},{8,13},{9,14},{10,... | collective-permute-start | bytes 417800 | tf_op jit(solution)/shard_map/ppermute | solution.py:406
  12.9 18.6 %collective-permute-start.6 = (bf16[544,128]{1,0:T(8,128)(2,1)S(1)}, bf16[544,128]{1,0:T(8,128)(2,1)S(1)}, u32[]{:S(2)}, u32[]{:S(2)}) collective-permute-start(bf16[544,128]{1,0:T(8,128)(2,1)S(1)} %pad_maximum_fusion.8), channel_id=1, source_target_pairs={{0,7},{1,0},{2,1},{3,2},{4,3},{5,4},{6,5},{7,6},{8,15},{9,8},{10,9... | collective-permute-start | bytes 417800 | tf_op jit(solution)/shard_map/ppermute | solution.py:406
  26.9 4.6 %copy-start = (bf16[544,128]{1,0:T(8,128)(2,1)}, bf16[544,128]{1,0:T(8,128)(2,1)S(1)}, u32[]{:S(2)}) copy-start(bf16[544,128]{1,0:T(8,128)(2,1)S(1)} %collective-permute-done.3.refs_5_) | copy-start | bytes 417796
  31.5 0.8 %slice-start = ((bf16[544,128]{1,0:T(8,128)(2,1)}), bf16[256,128]{1,0:T(8,128)(2,1)S(1)}, s32[]{:S(2)}) async-start(bf16[544,128]{1,0:T(8,128)(2,1)} %copy-done), calls=%async_computation | async-start | bytes 131072 | tf_op jit(solution)/shard_map/slice | solution.py:336
  32.3 0.9 %copy-start.1 = (bf16[544,128]{1,0:T(8,128)(2,1)S(1)}, bf16[544,128]{1,0:T(8,128)(2,1)}, u32[]{:S(2)}) copy-start(bf16[544,128]{1,0:T(8,128)(2,1)} %copy-done) | copy-start | bytes 417796
  32.3 6.5 %collective-permute-start.8 = (bf16[1024,128]{1,0:T(8,128)(2,1)S(1)}, bf16[1024,128]{1,0:T(8,128)(2,1)S(1)}, u32[]{:S(2)}, u32[]{:S(2)}) collective-permute-start(bf16[1024,128]{1,0:T(8,128)(2,1)S(1)} %pad_maximum_fusion), channel_id=1, source_target_pairs={{0,8},{8,0},{1,9},{9,1},{2,10},{10,2},{3,11},{11,3},{4,12},{12,4},... | collective-permute-start | bytes 786440 | tf_op jit(solution)/shard_map/ppermute | solution.py:331
  32.9 5.9 %collective-permute-start.7 = (bf16[1024,128]{1,0:T(8,128)(2,1)S(1)}, bf16[1024,128]{1,0:T(8,128)(2,1)S(1)}, u32[]{:S(2)}, u32[]{:S(2)}) collective-permute-start(bf16[1024,128]{1,0:T(8,128)(2,1)S(1)} %get-tuple-element.24), channel_id=1, source_target_pairs={{0,8},{8,0},{1,9},{9,1},{2,10},{10,2},{3,11},{11,3},{4,12},{12,4},... | collective-permute-start | bytes 786440 | tf_op jit(solution)/shard_map/ppermute | solution.py:331

commit v3 on v2

--- a/solution.py
+++ b/solution.py
@@ -54,9 +54,7 @@
 
 
 def score(keys, queries):
-    return lax.dot_general(
-        keys, queries, (((1,), (1,)), ((), ())), preferred_element_type=jnp.float32
-    )
+    return jnp.dot(keys, queries, preferred_element_type=jnp.float32)
 
 
 def soften(scores, values, scale):
@@ -171,13 +169,22 @@
     ]
 
 
+def pack(z, chunks, packed_ref):
+    first, last = z.prefix_pages * 2 * z.page, z.new_at
+    for i, chunk in enumerate(chunks):
+        packed_ref[i * (last - first) : (i + 1) * (last - first), :] = chunk[first:last, :]
+
+
+def pack_kernel(z, shifts, owner_ref, *refs):
+    pack(z, refs[:-1], refs[-1])
+
+
 def first_kernel(z, shifts, meta_ref, prefill_ref, decode_ref, *refs):
     chunks = dict(zip(shifts, refs))
     owner_ref, valid_ref, packed_ref, new_ref = refs[len(shifts) : len(shifts) + 4]
     state = refs[len(shifts) + 4 :]
-    first, last = z.prefix_pages * 2 * z.page, z.new_at
+    pack(z, refs[: len(shifts)], packed_ref)
     for i, d in enumerate(shifts):
-        packed_ref[i * (last - first) : (i + 1) * (last - first), :] = chunks[d][first:last, :]
         new_ref[i * 2 * z.new_pad : (i + 1) * 2 * z.new_pad, :] = chunks[d][z.new_at :, :]
 
     def forget(n, carry):
@@ -231,15 +238,18 @@
     @pl.when(meta_ref[0] == 0)
     def prefill():
         visible = jnp.concatenate(prefix_visible(z, meta_ref, shifts), axis=0)
-        keys = jnp.concatenate(prefix_rows(z, chunks, shifts, 0), axis=0)
+        keys = prefix_rows(z, chunks, shifts, 0)
+        cached = len(keys) * z.page
+        keys = jnp.concatenate(keys + new_rows(z, new_ref, late, 0), axis=0)
         values = prefix_rows(z, chunks, shifts, 1) + new_rows(z, new_ref, late, 1)
         values = jnp.concatenate(values, axis=0)
         for tile in range(z.prefill_tiles):
             query = lax.rem(column + tile * LANES, z.row_count)
+            scores = score(keys, prefill_ref[tile])
             scores = jnp.concatenate(
                 [
-                    jnp.where(visible, score(keys, prefill_ref[tile]), MASKED),
-                    jnp.where(index <= query, score(new_keys, prefill_ref[tile]), MASKED),
+                    jnp.where(visible, scores[:cached], MASKED),
+                    jnp.where(index <= query, scores[cached:], MASKED),
                 ],
                 axis=0,
             )
@@ -303,7 +313,7 @@
         in_specs=[spec[key] for key, _ in operands],
         out_specs=[spec[key] for key, _ in outputs],
         scratch_shapes=list(scratch),
-        compiler_params=pltpu.CompilerParams(vmem_limit_bytes=24 * 1024 * 1024),
+        compiler_params=pltpu.CompilerParams(vmem_limit_bytes=16 * 1024 * 1024),
         cost_estimate=pl.CostEstimate(
             flops=4 * z.tiles * LANES * keys * z.head_dim,
             bytes_accessed=2 * z.tiles * LANES * z.head_dim * 8,
@@ -322,18 +332,13 @@
     by_row = by_row.reshape((z.dec_rows, z.steps * z.heads, z.head_dim))
     by_row = jnp.pad(by_row, ((0, 0), (0, z.row_width - z.steps * z.heads), (0, 0)))
     return (
-        by_head.reshape((z.prefill_tiles, LANES, z.head_dim)),
-        by_row.reshape((z.decode_tiles, LANES, z.head_dim)),
+        by_head.reshape((z.prefill_tiles, LANES, z.head_dim)).transpose(0, 2, 1),
+        by_row.reshape((z.decode_tiles, LANES, z.head_dim)).transpose(0, 2, 1),
     )
 
 
 def hand_over(pages):
     return lax.ppermute(pages, "section", [(0, 1), (1, 0)])
-
-
-def finished(z, chunks):
-    first, last = z.prefix_pages * 2 * z.page, z.new_at
-    return jnp.concatenate([chunk[first:last] for chunk in chunks], axis=0)
 
 
 def attend(z, meta, queries, chunks, early, late):
@@ -343,6 +348,10 @@
         ("vmem", jax.ShapeDtypeStruct((z.tiles, rows, LANES), jnp.float32))
         for rows in (z.head_dim, 1, 1)
     ]
+    def packed_shape(count):
+        rows = count * FIN_DEV * 2 * z.page
+        return ("vmem", jax.ShapeDtypeStruct((rows, z.head_dim), queries.dtype))
+
     out = ("vmem", jax.ShapeDtypeStruct(queries.shape, queries.dtype))
     owner, valid, packed, new, *first = call(
         first_kernel,
@@ -352,15 +361,21 @@
         len(early) * z.page,
         [("smem", meta), ("vmem", prefill), ("vmem", decode)]
         + [("vmem", chunks[d]) for d in early],
-        [table, table]
-        + [
-            ("vmem", jax.ShapeDtypeStruct((len(early) * rows, z.head_dim), queries.dtype))
-            for rows in (FIN_DEV * 2 * z.page, 2 * z.new_pad)
-        ]
+        [table, table, packed_shape(len(early))]
+        + [("vmem", jax.ShapeDtypeStruct((len(early) * 2 * z.new_pad, z.head_dim), queries.dtype))]
         + state,
     )
     *waiting, owner = lax.optimization_barrier((*chunks, owner))
-    landed = [hand_over(packed), hand_over(finished(z, [waiting[d] for d in late]))]
+    (late_packed,) = call(
+        pack_kernel,
+        z,
+        late,
+        "pack_late",
+        1,
+        [("smem", owner)] + [("vmem", chunks[d]) for d in late],
+        [packed_shape(len(late))],
+    )
+    landed = [hand_over(packed), hand_over(late_packed)]
     common = [("smem", meta), ("smem", owner), ("smem", valid)]
     *second, done = call(
         second_kernel,
@@ -370,7 +385,7 @@
         len(late) * z.page + z.new_keys,
         common
         + [("vmem", value) for value in (prefill, decode, *first, new)]
-        + [("vmem", waiting[d]) for d in late],
+        + [("vmem", chunks[d]) for d in late],
         state + [out],
         [pltpu.VMEM((z.prefill_tiles * LANES, z.head_dim), queries.dtype)],
     )

time: 43 us -> 37.1 us (0.86)
  Pallas kernels: 13 us -> 7 us
  waiting for transfers between devices: 12.7 us -> 13.3 us
  local copies, waits for them, and re-layouts: 4.7 us -> 4.23 us
    pallas_call x3 -> x4, Pallas kernels: 13 us -> 7 us  [call(): pl.pallas_call(functools.partial(kernel, z, shifts), out_shape=[shape for...]
    slice x5 -> x0, local copies, waits for them, and re-layouts: 0.84 us -> none  [finished(): return jnp.concatenate([chunk[first:last] for chunk in chunks], axis=0)]
    ppermute x7, waiting for transfers between devices: 12.7 us -> 13.3 us  [body(): lax.ppermute(chunk_for(lax.rem(me + d, tp)), 'tp', shift_pairs(tp, d))]
    reshape x0 -> x2, local copies, waits for them, and re-layouts: none -> 0.52 us  [the longest x1 0.28 us: query_tiles(): by_row = by_row.reshape((z.dec_rows, z.steps * z.heads, z.head_dim))]
    unnamed x22 -> x18, local copies, waits for them, and re-layouts: 1.91 us -> 1.66 us
  transfers between devices with their start and end apart: 9 -> 9, of which waited for: 2 -> 2; matrix products, arithmetic and copies ran while one was open for 2% -> 4% of each run, Pallas kernels for 21% -> 10%
where the time goes in v3:
time: 37.1 us; the launch traced here: 36.9 us
  waiting for transfers between devices  13.3 us (36%)
  starting transfers between devices  11.2 us (30%)
  Pallas kernels  7 us (19%)
  local copies, waits for them, and re-layouts  4.23 us (11%)
  between operations  1 us (3%)
    ppermute x7, waiting for transfers between devices, body(): lax.ppermute(chunk_for(lax.rem(me + d, tp)), 'tp', shift_pairs(tp, d))  13.3 us
    ppermute x7, starting transfers between devices, body(): lax.ppermute(chunk_for(lax.rem(me + d, tp)), 'tp', shift_pairs(tp, d))  10.6 us
    pallas_call x4, Pallas kernels, call(): pl.pallas_call(functools.partial(kernel, z, shifts), out_shape=[shape for...  7 us
    unnamed x18, local copies, waits for them, and re-layouts  1.66 us
    dynamic_slice x1, local copies, waits for them, and re-layouts, chunk_for(): pages = lax.dynamic_index_in_dim(store, head, axis=2, keepdims=False)  1.39 us
  transfers between devices with their start and end apart: 9, of which 2 were waited for; matrix products, arithmetic and copies ran while one was open for 4% of the time, Pallas kernels for 10%

profile of v3, /device:TPU:13, one launch (start us, length us, event | category | flops | bytes accessed | tf_op | source)
XLA Modules:
  0.0 36.9 jit_solution(17867236125992574617)
XLA Ops:
  0.0 0.8 %copy-done.1 = bf16[1,12,2,8,128]{4,3,2,1,0:T(8,128)(2,1)S(1)} copy-done((bf16[1,12,2,8,128]{4,3,2,1,0:T(8,128)(2,1)S(1)}, bf16[1,12,2,8,128]{4,3,2,1,0:T(8,128)(2,1)}, u32[]{:S(2)}) %copy-start.1) | copy-done | bytes 49176
  0.8 0.1 constant_dynamic-slice_fusion
  0.9 1.4 %constant_dynamic-slice_fusion.1 = (bf16[1,2,2,1,128,128]{5,4,3,2,1,0:T(8,128)(2,1)S(1)}, bf16[1,2,2,1,128,128]{5,4,3,2,1,0:T(8,128)(2,1)S(1)}, bf16[1,2,2,1,128...) fusion(bf16[1,2,2,8,128,128]{5,4,3,2,1,0:T(8,128)(2,1)} %param., ...), kind=kLoop, calls=%fused_computation.19 | loop fusion | bytes 2097184 | tf_op jit(solution)/shard_map/jit(dynamic_index_in_dim)/dynamic_slice | solution.py:414
  2.4 0.2 collective-permute-start.5
  2.7 1.3 %collective-permute-start = (bf16[544,128]{1,0:T(8,128)(2,1)S(1)}, bf16[544,128]{1,0:T(8,128)(2,1)S(1)}, u32[]{:S(2)}, u32[]{:S(2)}) collective-permute-start(bf16[544,128]{1,0:T(8,128)(2,1)S(1)} %pad_maximum_fusion.1), channel_id=1, source_target_pairs={{0,1},{1,2},{2,3},{3,4},{4,5},{5,6},{6,7},{7,0},{8,9},{9,10},{10,1... | collective-permute-start | bytes 417800 | tf_op jit(solution)/shard_map/ppermute | solution.py:421
  4.0 1.3 %collective-permute-start.1 = (bf16[544,128]{1,0:T(8,128)(2,1)S(1)}, bf16[544,128]{1,0:T(8,128)(2,1)S(1)}, u32[]{:S(2)}, u32[]{:S(2)}) collective-permute-start(bf16[544,128]{1,0:T(8,128)(2,1)S(1)} %pad_maximum_fusion.2), channel_id=1, source_target_pairs={{0,2},{1,3},{2,4},{3,5},{4,6},{5,7},{6,0},{7,1},{8,10},{9,11},{10,... | collective-permute-start | bytes 417800 | tf_op jit(solution)/shard_map/ppermute | solution.py:421
  5.4 4.1 %collective-permute-start.2 = (bf16[544,128]{1,0:T(8,128)(2,1)S(1)}, bf16[544,128]{1,0:T(8,128)(2,1)S(1)}, u32[]{:S(2)}, u32[]{:S(2)}) collective-permute-start(bf16[544,128]{1,0:T(8,128)(2,1)S(1)} %pad_maximum_fusion.3), channel_id=1, source_target_pairs={{0,3},{1,4},{2,5},{3,6},{4,7},{5,0},{6,1},{7,2},{8,11},{9,12},{10,... | collective-permute-start | bytes 417800 | tf_op jit(solution)/shard_map/ppermute | solution.py:421
  9.8 0.3 copy.32
  10.1 0.1 pad_bitcast_fusion.decode_ref
  11.0 0.1 copy.20
  11.1 0.1 reshape.99
  11.2 0.1 copy.29
  11.3 0.2 copy.30
  11.6 0.6 %copy-done.3 = s32[16]{0:T(128)S(1)} copy-done((s32[16]{0:T(128)S(1)}, s32[16]{0:T(128)}, u32[]{:S(2)}) %copy-start.3) | copy-done | bytes 88
  12.3 1.2 %collective-permute-start.4 = (bf16[544,128]{1,0:T(8,128)(2,1)S(1)}, bf16[544,128]{1,0:T(8,128)(2,1)S(1)}, u32[]{:S(2)}, u32[]{:S(2)}) collective-permute-start(bf16[544,128]{1,0:T(8,128)(2,1)S(1)} %pad_maximum_fusion.5), channel_id=1, source_target_pairs={{0,5},{1,6},{2,7},{3,0},{4,1},{5,2},{6,3},{7,4},{8,13},{9,14},{10,... | collective-permute-start | bytes 417800 | tf_op jit(solution)/shard_map/ppermute | solution.py:421
  13.5 2.3 %collective-permute-start.6 = (bf16[544,128]{1,0:T(8,128)(2,1)S(1)}, bf16[544,128]{1,0:T(8,128)(2,1)S(1)}, u32[]{:S(2)}, u32[]{:S(2)}) collective-permute-start(bf16[544,128]{1,0:T(8,128)(2,1)S(1)} %pad_maximum_fusion.7), channel_id=1, source_target_pairs={{0,7},{1,0},{2,1},{3,2},{4,3},{5,4},{6,5},{7,6},{8,15},{9,8},{10,9... | collective-permute-start | bytes 417800 | tf_op jit(solution)/shard_map/ppermute | solution.py:421
  15.9 2.3 %early_pages.1 = (s32[24]{0:T(128)S(1)}, s32[24]{0:T(128)S(1)}, bf16[1024,128]{1,0:T(8,128)(2,1)S(1)}, bf16[128,128]{1,0:T(8,128)(2,1)S(1)}, f32[16,128,128]{2,1...) custom-call(s32[83]{0:T(128)S(1)} %concatenate.27.meta_ref, bf16[12,128,128]{2,1,0:T(8,128)(2,1)S(1)} %bitcast.69, ...), custom_call_target="tpu_custom_call" | custom-call | flops 536870912 | bytes 4194304 | tf_op jit(solution)/shard_map/early_pages/pallas_call | solution.py:310
  18.1 8.7 %collective-permute-done.3.refs_1_.refs_5_ = bf16[544,128]{1,0:T(8,128)(2,1)S(1)} collective-permute-done((bf16[544,128]{1,0:T(8,128)(2,1)S(1)}, bf16[544,128]{1,0:T(8,128)(2,1)S(1)}, u32[]{:S(2)}, u32[]{:S(2)}) %collective-permute-start.3) | collective-permute-done | bytes 139296 | tf_op jit(solution)/shard_map/ppermute | solution.py:421
  26.9 4.6 %collective-permute-done.6.refs_3_.refs_7_ = bf16[544,128]{1,0:T(8,128)(2,1)S(1)} collective-permute-done((bf16[544,128]{1,0:T(8,128)(2,1)S(1)}, bf16[544,128]{1,0:T(8,128)(2,1)S(1)}, u32[]{:S(2)}, u32[]{:S(2)}) %collective-permute-start.6) | collective-permute-done | bytes 139296 | tf_op jit(solution)/shard_map/ppermute | solution.py:421
  31.5 0.6 %pack_late.1 = bf16[1024,128]{1,0:T(8,128)(2,1)S(1)} custom-call(s32[24]{0:T(128)S(1)} %get-tuple-element.18.owner_ref, bf16[544,128]{1,0:T(8,128)(2,1)S(1)} %collective-permute-done.2.refs_0_.refs_4_, bf16[544,128]{1,0:T(8,128)(2,1)S(1)} %collective-permute-done.3.refs_1_.refs_5_, bf16[544,128]{1,0:T(8,128)(2,1)S(1)} %collective-permute-done.4.refs_2_.refs_6_, ...), custom_call_target="tpu_custom_call" | custom-call | flops 1048576 | bytes 4194304 | tf_op jit(solution)/shard_map/pack_late/pallas_call | solution.py:310
  32.0 0.6 %collective-permute-start.8 = (bf16[1024,128]{1,0:T(8,128)(2,1)S(1)}, bf16[1024,128]{1,0:T(8,128)(2,1)S(1)}, u32[]{:S(2)}, u32[]{:S(2)}) collective-permute-start(bf16[1024,128]{1,0:T(8,128)(2,1)S(1)} %pack_late.1), channel_id=1, source_target_pairs={{0,8},{8,0},{1,9},{9,1},{2,10},{10,2},{3,11},{11,3},{4,12},{12,4},... | collective-permute-start | bytes 786440 | tf_op jit(solution)/shard_map/ppermute | solution.py:341
  32.6 0.1 collective-permute-start.7
  32.7 1.6 %late_pages.1 = (f32[16,128,128]{2,1,0:T(8,128)S(1)}, f32[16,1,128]{2,1,0:T(1,128)S(1)}, f32[16,1,128]{2,1,0:T(1,128)S(1)}, bf16[96,2048]{1,0:T(8,128)(2,1)S(1)}) custom-call(s32[83]{0:T(128)S(1)} %concatenate.27.meta_ref, s32[24]{0:T(128)S(1)} %get-tuple-element.18.owner_ref, s32[24]{0:T(128)S(1)} %get-tuple-element.19.valid_ref, ...), custom_call_target="tpu_custom_call" | custom-call | flops 671088640 | bytes 4194304 | tf_op jit(solution)/shard_map/late_pages/pallas_call | solution.py:310
  34.3 2.6 %landed_pages.1 = bf16[96,2048]{1,0:T(8,128)(2,1)} custom-call(s32[83]{0:T(128)S(1)} %concatenate.27.meta_ref, s32[24]{0:T(128)S(1)} %get-tuple-element.18.owner_ref, s32[24]{0:T(128)S(1)} %get-tuple-element.19.valid_ref, bf16[16,128,128]{2,1,0:T(8,128)(2,1)S(1)} %pad_bitcast_fusion.decode_ref, bf16[1024,128]{1,0:T(8,128)(2,1)S(1)} %collective-permute-done.7.refs_0_, ...), custom_call_target="tpu_custom_call" | custom-call | flops 134217728 | bytes 4194304 | tf_op jit(solution)/shard_map/landed_pages/pallas_call | solution.py:310
  (46 shorter events, 0.5 us)
Async XLA Ops:
  0.0 0.8 %copy-start.1 = (bf16[1,12,2,8,128]{4,3,2,1,0:T(8,128)(2,1)S(1)}, bf16[1,12,2,8,128]{4,3,2,1,0:T(8,128)(2,1)}, u32[]{:S(2)}) copy-start(bf16[1,12,2,8,128]{4,3,2,1,0:T(8,128)(2,1)} %param.7) | copy-start | bytes 147460
  2.4 9.9 %collective-permute-start.5 = (bf16[544,128]{1,0:T(8,128)(2,1)S(1)}, bf16[544,128]{1,0:T(8,128)(2,1)S(1)}, u32[]{:S(2)}, u32[]{:S(2)}) collective-permute-start(bf16[544,128]{1,0:T(8,128)(2,1)S(1)} %pad_maximum_fusion.6), channel_id=1, source_target_pairs={{0,6},{1,7},{2,0},{3,1},{4,2},{5,3},{6,4},{7,5},{8,14},{9,15},{10,... | collective-permute-start | bytes 417800 | tf_op jit(solution)/shard_map/ppermute | solution.py:421
  2.7 10.8 %collective-permute-start = (bf16[544,128]{1,0:T(8,128)(2,1)S(1)}, bf16[544,128]{1,0:T(8,128)(2,1)S(1)}, u32[]{:S(2)}, u32[]{:S(2)}) collective-permute-start(bf16[544,128]{1,0:T(8,128)(2,1)S(1)} %pad_maximum_fusion.1), channel_id=1, source_target_pairs={{0,1},{1,2},{2,3},{3,4},{4,5},{5,6},{6,7},{7,0},{8,9},{9,10},{10,1... | collective-permute-start | bytes 417800 | tf_op jit(solution)/shard_map/ppermute | solution.py:421
  4.0 5.7 %copy-start = (bf16[1,96,2048]{2,1,0:T(8,128)(2,1)S(1)}, bf16[1,96,2048]{2,1,0:T(8,128)(2,1)}, u32[]{:S(2)}) copy-start(bf16[1,96,2048]{2,1,0:T(8,128)(2,1)} %param.6) | copy-start | bytes 1179652
  4.0 11.8 %collective-permute-start.1 = (bf16[544,128]{1,0:T(8,128)(2,1)S(1)}, bf16[544,128]{1,0:T(8,128)(2,1)S(1)}, u32[]{:S(2)}, u32[]{:S(2)}) collective-permute-start(bf16[544,128]{1,0:T(8,128)(2,1)S(1)} %pad_maximum_fusion.2), channel_id=1, source_target_pairs={{0,2},{1,3},{2,4},{3,5},{4,6},{5,7},{6,0},{7,1},{8,10},{9,11},{10,... | collective-permute-start | bytes 417800 | tf_op jit(solution)/shard_map/ppermute | solution.py:421
  5.4 12.7 %collective-permute-start.2 = (bf16[544,128]{1,0:T(8,128)(2,1)S(1)}, bf16[544,128]{1,0:T(8,128)(2,1)S(1)}, u32[]{:S(2)}, u32[]{:S(2)}) collective-permute-start(bf16[544,128]{1,0:T(8,128)(2,1)S(1)} %pad_maximum_fusion.3), channel_id=1, source_target_pairs={{0,3},{1,4},{2,5},{3,6},{4,7},{5,0},{6,1},{7,2},{8,11},{9,12},{10,... | collective-permute-start | bytes 417800 | tf_op jit(solution)/shard_map/ppermute | solution.py:421
  9.6 17.3 %collective-permute-start.3 = (bf16[544,128]{1,0:T(8,128)(2,1)S(1)}, bf16[544,128]{1,0:T(8,128)(2,1)S(1)}, u32[]{:S(2)}, u32[]{:S(2)}) collective-permute-start(bf16[544,128]{1,0:T(8,128)(2,1)S(1)} %pad_maximum_fusion.4), channel_id=1, source_target_pairs={{0,4},{1,5},{2,6},{3,7},{4,0},{5,1},{6,2},{7,3},{8,12},{9,13},{10,... | collective-permute-start | bytes 417800 | tf_op jit(solution)/shard_map/ppermute | solution.py:421
  10.3 0.7 %copy-start.2 = (s32[16,4]{0,1:T(4,128)S(1)}, s32[16,4]{0,1:T(4,128)}, u32[]{:S(2)}) copy-start(s32[16,4]{0,1:T(4,128)} %param.10) | copy-start | bytes 772
  11.6 0.7 %copy-start.3 = (s32[16]{0:T(128)S(1)}, s32[16]{0:T(128)}, u32[]{:S(2)}) copy-start(s32[16]{0:T(128)} %param.11) | copy-start | bytes 196
  12.3 14.6 %collective-permute-start.4 = (bf16[544,128]{1,0:T(8,128)(2,1)S(1)}, bf16[544,128]{1,0:T(8,128)(2,1)S(1)}, u32[]{:S(2)}, u32[]{:S(2)}) collective-permute-start(bf16[544,128]{1,0:T(8,128)(2,1)S(1)} %pad_maximum_fusion.5), channel_id=1, source_target_pairs={{0,5},{1,6},{2,7},{3,0},{4,1},{5,2},{6,3},{7,4},{8,13},{9,14},{10,... | collective-permute-start | bytes 417800 | tf_op jit(solution)/shard_map/ppermute | solution.py:421
  13.5 18.0 %collective-permute-start.6 = (bf16[544,128]{1,0:T(8,128)(2,1)S(1)}, bf16[544,128]{1,0:T(8,128)(2,1)S(1)}, u32[]{:S(2)}, u32[]{:S(2)}) collective-permute-start(bf16[544,128]{1,0:T(8,128)(2,1)S(1)} %pad_maximum_fusion.7), channel_id=1, source_target_pairs={{0,7},{1,0},{2,1},{3,2},{4,3},{5,4},{6,5},{7,6},{8,15},{9,8},{10,9... | collective-permute-start | bytes 417800 | tf_op jit(solution)/shard_map/ppermute | solution.py:421
  32.0 2.2 %collective-permute-start.8 = (bf16[1024,128]{1,0:T(8,128)(2,1)S(1)}, bf16[1024,128]{1,0:T(8,128)(2,1)S(1)}, u32[]{:S(2)}, u32[]{:S(2)}) collective-permute-start(bf16[1024,128]{1,0:T(8,128)(2,1)S(1)} %pack_late.1), channel_id=1, source_target_pairs={{0,8},{8,0},{1,9},{9,1},{2,10},{10,2},{3,11},{11,3},{4,12},{12,4},... | collective-permute-start | bytes 786440 | tf_op jit(solution)/shard_map/ppermute | solution.py:341
  32.6 1.7 %collective-permute-start.7 = (bf16[1024,128]{1,0:T(8,128)(2,1)S(1)}, bf16[1024,128]{1,0:T(8,128)(2,1)S(1)}, u32[]{:S(2)}, u32[]{:S(2)}) collective-permute-start(bf16[1024,128]{1,0:T(8,128)(2,1)S(1)} %get-tuple-element.20), channel_id=1, source_target_pairs={{0,8},{8,0},{1,9},{9,1},{2,10},{10,2},{3,11},{11,3},{4,12},{12,4},... | collective-permute-start | bytes 786440 | tf_op jit(solution)/shard_map/ppermute | solution.py:341

commit v4 on v3

v4 whole, which is shorter than its diff:
```python
import functools
import math

import jax
import jax.numpy as jnp
from jax import lax
from jax.experimental import pallas as pl
from jax.experimental.pallas import tpu as pltpu
from jax.sharding import PartitionSpec as P

FIN_DEV = 1
ROW_TILE = 16
LANES = 128
BLOCK_BATCH = 4
MASKED = -1e30
LOG2_E = 1.4426950408889634


def round_up(value, multiple):
    return -(-value // multiple) * multiple


class Sizes:
    def __init__(self, tp, store, fresh, queries, page_table):
        self.tp = tp
        self.pages_here, _, self.kv_heads, self.page, self.head_dim = store
        self.prefix_pages = self.pages_here - FIN_DEV
        self.per_device = self.pages_here + FIN_DEV
        self.new_rows = fresh[0]
        self.new_pad = round_up(self.new_rows, ROW_TILE)
        self.new_keys = tp * self.new_pad
        self.heads = queries[1] // self.head_dim
        self.row_count = queries[0]
        self.dec_rows, self.max_entries = page_table
        self.steps = self.row_count // self.dec_rows
        self.slots = tp * self.per_device
        self.scale = LOG2_E / math.sqrt(self.head_dim)
        self.new_at = self.pages_here * 2 * self.page
        self.prefill_tiles = round_up(self.heads * self.row_count, LANES) // LANES
        self.row_width = round_up(self.steps * self.heads, LANES)
        self.row_tiles = self.row_width // LANES
        self.decode_tiles = self.dec_rows * self.row_tiles
        self.tiles = max(self.prefill_tiles, self.decode_tiles)
        self.owner_at = 1
        self.valid_at = 1 + self.slots

    def source(self, d):
        return lax.rem(lax.axis_index("tp") + self.tp - d, self.tp)

    def target(self, d):
        return lax.rem(lax.axis_index("tp") + d, self.tp)

    def pairs(self, d):
        return [(i, (i + d) % self.tp) for i in range(self.tp)]


def score(keys, queries):
    return jnp.dot(keys, queries, preferred_element_type=jnp.float32)


def soften(scores, values, scale):
    highest = jnp.max(scores, axis=0, keepdims=True)
    raw = jnp.exp2((scores - highest) * scale)
    total = jnp.sum(raw, axis=0, keepdims=True)
    summed = lax.dot_general(
        values,
        raw.astype(values.dtype),
        (((0,), (0,)), ((), ())),
        preferred_element_type=jnp.float32,
    )
    return summed, highest, total


def merge(first, second, scale):
    highest = jnp.maximum(first[1], second[1])
    keep = jnp.exp2((first[1] - highest) * scale)
    add = jnp.exp2((second[1] - highest) * scale)
    return (
        first[0] * keep + second[0] * add,
        highest,
        first[2] * keep + second[2] * add,
    )


def read(state, tile):
    return tuple(ref[tile] for ref in state)


def write(state, tile, part):
    for ref, value in zip(state, part):
        ref[tile] = value


def settle(part):
    return (part[0] * (1.0 / part[2])).T


def key_rows(z, count):
    return lax.broadcasted_iota(jnp.int32, (count, LANES), 0)


def add_pages(z, pages, plan_ref, queries_ref, state):
    slot = key_rows(z, z.page)
    for start in range(0, len(pages), BLOCK_BATCH):
        parts = []
        for ref, at, number in pages[start : start + BLOCK_BATCH]:
            visible = slot < plan_ref[z.valid_at + number]
            keys, values = ref[at : at + z.page, :], ref[at + z.page : at + 2 * z.page, :]
            for i in range(z.row_tiles):
                tile = plan_ref[z.owner_at + number] * z.row_tiles + i
                scores = jnp.where(visible, score(keys, queries_ref[tile]), MASKED)
                parts.append((tile, soften(scores, values, z.scale)))
        for tile, part in parts:
            write(state, tile, merge(read(state, tile), part, z.scale))


def prefix_visible(z, plan_ref, shifts):
    slot = key_rows(z, z.page)
    return [
        slot < plan_ref[0] - (z.source(d) * z.prefix_pages + q) * z.page
        for d in shifts
        for q in range(z.prefix_pages)
    ]


def prefix_rows(z, chunks, shifts, which):
    return [
        chunks[d][(2 * q + which) * z.page : (2 * q + which + 1) * z.page, :]
        for d in shifts
        for q in range(z.prefix_pages)
    ]


def new_rows(z, new_ref, chunks, which):
    sources = [(new_ref, at) for at in range(0, new_ref.shape[0], 2 * z.new_pad)]
    sources += [(chunk, z.new_at) for chunk in chunks]
    rows = [pl.ds(at + which * z.new_pad, z.new_pad) for _, at in sources]
    return [ref[span, :] for (ref, _), span in zip(sources, rows)]


def new_index(z, shifts):
    within = key_rows(z, z.new_pad)
    none = jnp.full_like(within, z.row_count)
    return jnp.concatenate(
        [
            jnp.where(within < z.new_rows, z.source(d) * z.new_rows + within, none)
            for d in shifts
        ],
        axis=0,
    )


def local_pages(z, chunks, shifts):
    return [
        (chunks[d], 2 * q * z.page, z.source(d) * z.per_device + q)
        for d in shifts
        for q in range(z.pages_here)
    ]


def landed_pages(z, places, shifts):
    return [
        (ref, at + 2 * q * z.page, z.source(d) * z.per_device + z.pages_here + q)
        for (ref, at), d in zip(places, shifts)
        for q in range(FIN_DEV)
    ]


def on_side(side):
    return pl.when(lax.axis_index("section") == side)


def first_kernel(
    z, shifts, prefix_ref, table_ref, context_ref, prefill_ref, decode_ref, *refs
):
    chunks, refs = dict(zip(shifts, refs)), refs[len(shifts) :]
    plan_ref, packed_ref, new_ref, state = refs[0], refs[1], refs[2], refs[3:]
    first, last = z.prefix_pages * 2 * z.page, z.new_at
    for i, d in enumerate(shifts):
        packed_ref[i * (last - first) : (i + 1) * (last - first), :] = chunks[d][first:last, :]
        new_ref[i * 2 * z.new_pad : (i + 1) * 2 * z.new_pad, :] = chunks[d][z.new_at :, :]

    def forget(n, carry):
        plan_ref[z.owner_at + n] = 0
        plan_ref[z.valid_at + n] = 0
        return carry

    def note(r, carry):
        length = context_ref[r]
        for m in range(z.max_entries):

            @pl.when(m * z.page < length)
            def used():
                number = jnp.clip(table_ref[m, r], 0, z.slots - 1)
                plan_ref[z.owner_at + number] = r
                plan_ref[z.valid_at + number] = jnp.minimum(length - m * z.page, z.page)

        return carry

    plan_ref[0] = prefix_ref[0]
    lax.fori_loop(0, z.slots, forget, 0)
    lax.fori_loop(0, z.dec_rows, note, 0)

    @on_side(0)
    def prefill():
        visible = jnp.concatenate(prefix_visible(z, plan_ref, shifts), axis=0)
        keys = jnp.concatenate(prefix_rows(z, chunks, shifts, 0), axis=0)
        values = jnp.concatenate(prefix_rows(z, chunks, shifts, 1), axis=0)
        for tile in range(z.prefill_tiles):
            scores = jnp.where(visible, score(keys, prefill_ref[tile]), MASKED)
            write(state, tile, soften(scores, values, z.scale))

    @on_side(1)
    def decode():
        state[0][...] = jnp.zeros_like(state[0])
        state[1][...] = jnp.full_like(state[1], MASKED)
        state[2][...] = jnp.zeros_like(state[2])
        pages = local_pages(z, chunks, shifts)
        add_pages(z, pages, plan_ref, decode_ref, state)


def second_kernel(z, groups, plan_ref, prefill_ref, decode_ref, *refs):
    shifts = groups[1]
    before, new_ref, refs = refs[:3], refs[3], refs[4:]
    late, refs = refs[: len(shifts)], refs[len(shifts) :]
    state, (out_ref, held_ref, sems) = refs[:3], refs[3:]
    chunks = dict(zip(shifts, late))
    index = new_index(z, groups[0] + groups[1])
    column = lax.broadcasted_iota(jnp.int32, (1, LANES), 1)
    new_keys = jnp.concatenate(new_rows(z, new_ref, late, 0), axis=0)

    @on_side(0)
    def prefill():
        visible = jnp.concatenate(prefix_visible(z, plan_ref, shifts), axis=0)
        keys = prefix_rows(z, chunks, shifts, 0)
        cached = len(keys) * z.page
        keys = jnp.concatenate(keys + new_rows(z, new_ref, late, 0), axis=0)
        values = prefix_rows(z, chunks, shifts, 1) + new_rows(z, new_ref, late, 1)
        values = jnp.concatenate(values, axis=0)
        copies = []
        for tile in range(z.prefill_tiles):
            query = lax.rem(column + tile * LANES, z.row_count)
            scores = score(keys, prefill_ref[tile])
            scores = jnp.concatenate(
                [
                    jnp.where(visible, scores[:cached], MASKED),
                    jnp.where(index <= query, scores[cached:], MASKED),
                ],
                axis=0,
            )
            part = merge(read(before, tile), soften(scores, values, z.scale), z.scale)
            held_ref[tile * LANES : (tile + 1) * LANES, :] = settle(part).astype(held_ref.dtype)
            while len(copies) < min((tile + 1) * LANES // z.row_count, z.heads):
                h = len(copies)
                source = held_ref.at[pl.ds(h * z.row_count, z.row_count)]
                target = out_ref.at[:, pl.ds(h * z.head_dim, z.head_dim)]
                copies.append(pltpu.make_async_copy(source, target, sems.at[h]))
                copies[-1].start()
        for copy in copies:
            copy.wait()

    @on_side(1)
    def decode():
        owner = lax.rem(index, z.dec_rows)
        owner = jnp.where(index < z.row_count, owner, -1)
        step = index // z.dec_rows
        new_values = jnp.concatenate(new_rows(z, new_ref, late, 1), axis=0)
        for tile in range(z.decode_tiles):
            row, i = divmod(tile, z.row_tiles)
            query = (column + i * LANES) // z.heads
            visible = (owner == row) & (step <= query)
            scores = jnp.where(visible, score(new_keys, decode_ref[tile]), MASKED)
            part = soften(scores, new_values, z.scale)
            write(state, tile, merge(read(before, tile), part, z.scale))
        pages = local_pages(z, chunks, shifts)
        add_pages(z, pages, plan_ref, decode_ref, state)


def last_kernel(z, groups, plan_ref, decode_ref, early_ref, *refs):
    late, refs = refs[: len(groups[1])], refs[len(groups[1]) :]
    before, out_ref, refs = refs[:3], refs[4], refs[5:]
    state, (held_ref, rows_ref, sems) = refs[:3], refs[3:]

    @on_side(1)
    def decode():
        for ref, value in zip(state, before):
            ref[...] = value[...]
        places = [(early_ref, i * FIN_DEV * 2 * z.page) for i in range(len(groups[0]))]
        places += [(ref, z.prefix_pages * 2 * z.page) for ref in late]
        pages = landed_pages(z, places, groups[0] + groups[1])
        add_pages(z, pages, plan_ref, decode_ref, state)
        for tile in range(z.decode_tiles):
            held_ref[tile * LANES : (tile + 1) * LANES, :] = settle(read(state, tile))
        copies = []
        for s in range(z.steps):
            span = pl.ds(s * z.dec_rows, z.dec_rows)
            for h in range(z.heads):
                rows = pl.ds(s * z.heads + h, z.dec_rows, stride=z.row_width)
                rows_ref[span, h * z.head_dim : (h + 1) * z.head_dim] = held_ref[rows, :].astype(
                    rows_ref.dtype
                )
            copies.append(
                pltpu.make_async_copy(rows_ref.at[span], out_ref.at[span], sems.at[s])
            )
            copies[-1].start()
        for copy in copies:
            copy.wait()


def call(kernel, z, shifts, name, keys, operands, outputs, scratch=(), aliases=None):
    spaces = {"smem": pltpu.SMEM, "vmem": pltpu.VMEM, "any": pl.ANY}
    spec = {key: pl.BlockSpec(memory_space=space) for key, space in spaces.items()}
    return pl.pallas_call(
        functools.partial(kernel, z, shifts),
        out_shape=[shape for _, shape in outputs],
        in_specs=[spec[key] for key, _ in operands],
        out_specs=[spec[key] for key, _ in outputs],
        scratch_shapes=list(scratch),
        input_output_aliases=aliases or {},
        compiler_params=pltpu.CompilerParams(vmem_limit_bytes=16 * 1024 * 1024),
        cost_estimate=pl.CostEstimate(
            flops=4 * z.tiles * LANES * keys * z.head_dim,
            bytes_accessed=2 * z.tiles * LANES * z.head_dim * 8,
            transcendentals=z.tiles * LANES * keys,
        ),
        name=name,
    )(*[value for _, value in operands])


def query_tiles(z, queries):
    by_head = queries.reshape((z.row_count, z.heads, z.head_dim)).transpose(1, 0, 2)
    by_head = by_head.reshape((-1, z.head_dim))
    spare = z.prefill_tiles * LANES - by_head.shape[0]
    by_head = jnp.pad(by_head, ((0, spare), (0, 0)))
    by_row = queries.reshape((z.steps, z.dec_rows, z.heads, z.head_dim)).transpose(1, 0, 2, 3)
    by_row = by_row.reshape((z.dec_rows, z.steps * z.heads, z.head_dim))
    by_row = jnp.pad(by_row, ((0, 0), (0, z.row_width - z.steps * z.heads), (0, 0)))
    return (
        by_head.reshape((z.prefill_tiles, LANES, z.head_dim)).transpose(0, 2, 1),
        by_row.reshape((z.decode_tiles, LANES, z.head_dim)).transpose(0, 2, 1),
    )


def hand_over(pages):
    return lax.ppermute(pages, "section", [(0, 1), (1, 0)])


def attend(z, inputs, queries, chunks, early, late):
    prefill, decode = query_tiles(z, queries)

    def shaped(space, shape, dtype):
        return (space, jax.ShapeDtypeStruct(shape, dtype))

    state = [
        shaped("vmem", (z.tiles, rows, LANES), jnp.float32) for rows in (z.head_dim, 1, 1)
    ]
    out = shaped("any", queries.shape, queries.dtype)
    plan, packed, new, *first = call(
        first_kernel,
        z,
        early,
        "early_pages",
        len(early) * z.page,
        [("smem", value) for value in inputs]
        + [("vmem", value) for value in (prefill, decode)]
        + [("vmem", chunks[d]) for d in early],
        [shaped("smem", (1 + 2 * z.slots,), jnp.int32)]
        + [
            shaped("vmem", (len(early) * rows, z.head_dim), queries.dtype)
            for rows in (FIN_DEV * 2 * z.page, 2 * z.new_pad)
        ]
        + state,
    )
    *waiting, plan = lax.optimization_barrier((*[chunks[d] for d in early + late], plan))
    landed = [hand_over(packed)] + [hand_over(chunk) for chunk in waiting[len(early) :]]
    *second, done = call(
        second_kernel,
        z,
        (early, late),
        "late_pages",
        len(late) * z.page + z.new_keys,
        [("smem", plan)]
        + [("vmem", value) for value in (prefill, decode, *first, new)]
        + [("vmem", chunks[d]) for d in late],
        state + [out],
        [
            pltpu.VMEM((z.prefill_tiles * LANES, z.head_dim), queries.dtype),
            pltpu.SemaphoreType.DMA((z.heads,)),
        ],
    )
    operands = [("smem", plan)]
    operands += [("vmem", value) for value in (decode, *landed, *second)]
    (result,) = call(
        last_kernel,
        z,
        (early, late),
        "landed_pages",
        z.page,
        operands + [("any", done)],
        [out],
        [pltpu.VMEM(shape.shape, shape.dtype) for _, shape in state]
        + [
            pltpu.VMEM((z.decode_tiles * LANES, z.head_dim), jnp.float32),
            pltpu.VMEM(queries.shape, queries.dtype),
            pltpu.SemaphoreType.DMA((z.steps,)),
        ],
        {len(operands): 0},
    )
    return result


def body(queries, fresh_key_value, key_value_page_store, prefix_len, page_table, context_len):
    tp = lax.axis_size("tp")
    store, fresh = key_value_page_store[0], fresh_key_value[0]
    z = Sizes(tp, store.shape, fresh.shape, queries.shape[1:], page_table.shape)

    def chunk_for(device):
        head = device * z.kv_heads // tp
        pages = lax.dynamic_index_in_dim(store, head, axis=2, keepdims=False)
        new = lax.dynamic_index_in_dim(fresh, head, axis=2, keepdims=False).transpose(1, 0, 2)
        new = jnp.pad(new, ((0, 0), (0, z.new_pad - z.new_rows), (0, 0)))
        return jnp.concatenate([pages.reshape((-1, z.head_dim)), new.reshape((-1, z.head_dim))])

    order = [tp - 2] + list(range(1, tp - 2)) + [tp - 1]
    early, late = [0] + order[: tp // 2 - 1], order[tp // 2 - 1 :]
    chunks = {0: chunk_for(lax.axis_index("tp"))}
    for d in order:
        chunks[d] = lax.ppermute(chunk_for(z.target(d)), "tp", z.pairs(d))
    inputs = (prefix_len, page_table.T, context_len)
    return attend(z, inputs, queries[0], chunks, early, late)[None]


def solution(mesh):
    placed = (
        P(("pairs", "section"), None, "tp"),
        P(("pairs", "section"), "tp", None, None, None),
        P(("pairs", "section"), "tp", None, None, None, None),
        P("pairs"),
        P("pairs", None),
        P("pairs"),
    )
    return jax.shard_map(
        body,
        mesh=mesh,
        in_specs=placed,
        out_specs=P(("pairs", "section"), None, "tp"),
        check_vma=False,
    )
```

time: 37.1 us -> 36.3 us (0.978)
  the two profiles are of different devices: /device:TPU:13 before, /device:TPU:31 now
where the time goes in v4:
time: 36.3 us; the launch traced here: 36.1 us
  starting transfers between devices  18.1 us (50%)
  Pallas kernels  6.57 us (18%)
  waiting for transfers between devices  6.36 us (18%)
  local copies, waits for them, and re-layouts  4 us (11%)
  between operations  0.96 us (3%)
    ppermute x7, starting transfers between devices, body(): chunks[d] = lax.ppermute(chunk_for(z.target(d)), 'tp', z.pairs(d))  13.3 us
    pallas_call x3, Pallas kernels, call(): pl.pallas_call(functools.partial(kernel, z, shifts), out_shape=[shape for...  6.57 us
    ppermute x7, waiting for transfers between devices, body(): chunks[d] = lax.ppermute(chunk_for(z.target(d)), 'tp', z.pairs(d))  6.35 us
    ppermute x5, starting transfers between devices, hand_over(): return lax.ppermute(pages, 'section', [(0, 1), (1, 0)])  4.84 us
    unnamed x17, local copies, waits for them, and re-layouts  1.57 us
    dynamic_slice x1, local copies, waits for them, and re-layouts, chunk_for(): pages = lax.dynamic_index_in_dim(store, head, axis=2, keepdims=False)  1.41 us
  transfers between devices with their start and end apart: 12, of which 2 were waited for; matrix products, arithmetic and copies ran while one was open for 3% of the time, Pallas kernels for 11%

profile of v4, /device:TPU:31, one launch (start us, length us, event | category | flops | bytes accessed | tf_op | source)
XLA Modules:
  0.0 36.1 jit_solution(3719689999217373047)
XLA Ops:
  0.0 0.8 %copy-done.3 = bf16[1,12,2,8,128]{4,3,2,1,0:T(8,128)(2,1)S(1)} copy-done((bf16[1,12,2,8,128]{4,3,2,1,0:T(8,128)(2,1)S(1)}, bf16[1,12,2,8,128]{4,3,2,1,0:T(8,128)(2,1)}, u32[]{:S(2)}) %copy-start.3) | copy-done | bytes 49176
  0.8 0.1 constant_dynamic-slice_fusion
  0.9 1.4 %constant_dynamic-slice_fusion.1 = (bf16[1,2,2,1,128,128]{5,4,3,2,1,0:T(8,128)(2,1)S(1)}, bf16[1,2,2,1,128,128]{5,4,3,2,1,0:T(8,128)(2,1)S(1)}, bf16[1,2,2,1,128...) fusion(bf16[1,2,2,8,128,128]{5,4,3,2,1,0:T(8,128)(2,1)} %param., ...), kind=kLoop, calls=%fused_computation.19 | loop fusion | bytes 2097184 | tf_op jit(solution)/shard_map/jit(dynamic_index_in_dim)/dynamic_slice | solution.py:419
  2.4 0.2 collective-permute-start.5
  2.6 0.2 collective-permute-start
  2.9 0.0 copy-start.2
  2.9 4.0 %collective-permute-start.1 = (bf16[544,128]{1,0:T(8,128)(2,1)S(1)}, bf16[544,128]{1,0:T(8,128)(2,1)S(1)}, u32[]{:S(2)}, u32[]{:S(2)}) collective-permute-start(bf16[544,128]{1,0:T(8,128)(2,1)S(1)} %pad_maximum_fusion.2), channel_id=1, source_target_pairs={{0,1},{1,2},{2,3},{3,4},{4,5},{5,6},{6,7},{7,0},{8,9},{9,10},{10,1... | collective-permute-start | bytes 417800 | tf_op jit(solution)/shard_map/ppermute | solution.py:428
  6.9 0.5 %collective-permute-start.2 = (bf16[544,128]{1,0:T(8,128)(2,1)S(1)}, bf16[544,128]{1,0:T(8,128)(2,1)S(1)}, u32[]{:S(2)}, u32[]{:S(2)}) collective-permute-start(bf16[544,128]{1,0:T(8,128)(2,1)S(1)} %pad_maximum_fusion.3), channel_id=1, source_target_pairs={{0,2},{1,3},{2,4},{3,5},{4,6},{5,7},{6,0},{7,1},{8,10},{9,11},{10,... | collective-permute-start | bytes 417800 | tf_op jit(solution)/shard_map/ppermute | solution.py:428
  7.4 0.2 collective-permute-start.3
  7.7 0.1 copy.47
  8.5 0.1 copy.27
  8.6 0.2 copy.28
  8.9 0.3 copy.30
  9.2 0.1 pad_bitcast_fusion.decode_ref
  9.4 2.4 %collective-permute-done.refs_1_ = bf16[544,128]{1,0:T(8,128)(2,1)S(1)} collective-permute-done((bf16[544,128]{1,0:T(8,128)(2,1)S(1)}, bf16[544,128]{1,0:T(8,128)(2,1)S(1)}, u32[]{:S(2)}, u32[]{:S(2)}) %collective-permute-start) | collective-permute-done | bytes 139296 | tf_op jit(solution)/shard_map/ppermute | solution.py:428
  11.8 8.3 %collective-permute-start.6 = (bf16[544,128]{1,0:T(8,128)(2,1)S(1)}, bf16[544,128]{1,0:T(8,128)(2,1)S(1)}, u32[]{:S(2)}, u32[]{:S(2)}) collective-permute-start(bf16[544,128]{1,0:T(8,128)(2,1)S(1)} %pad_maximum_fusion.7), channel_id=1, source_target_pairs={{0,7},{1,0},{2,1},{3,2},{4,3},{5,4},{6,5},{7,6},{8,15},{9,8},{10,9... | collective-permute-start | bytes 417800 | tf_op jit(solution)/shard_map/ppermute | solution.py:428
  20.1 0.7 %copy-done.1 = s32[16]{0:T(128)S(1)} copy-done((s32[16]{0:T(128)S(1)}, s32[16]{0:T(128)}, u32[]{:S(2)}) %copy-start.1) | copy-done | bytes 88
  20.7 2.3 %early_pages.1 = (s32[49]{0:T(128)S(1)}, bf16[1024,128]{1,0:T(8,128)(2,1)S(1)}, bf16[128,128]{1,0:T(8,128)(2,1)S(1)}, f32[16,128,128]{2,1,0:T(8,128)S(1)}, f32[1...) custom-call(s32[1]{0:T(128)S(6)} %copy.58.prefix_ref, s32[4,16]{1,0:T(4,128)S(1)} %bitcast.70, s32[16]{0:T(128)S(1)} %copy-done.1, ...), custom_call_target="tpu_custom_call" | custom-call | flops 536870912 | bytes 4194304 | tf_op jit(solution)/shard_map/early_pages/pallas_call | solution.py:313
  23.0 3.8 %collective-permute-start.7 = (bf16[1024,128]{1,0:T(8,128)(2,1)S(1)}, bf16[1024,128]{1,0:T(8,128)(2,1)S(1)}, u32[]{:S(2)}, u32[]{:S(2)}) collective-permute-start(bf16[1024,128]{1,0:T(8,128)(2,1)S(1)} %get-tuple-element.22), channel_id=1, source_target_pairs={{0,8},{8,0},{1,9},{9,1},{2,10},{10,2},{3,11},{11,3},{4,12},{12,4},... | collective-permute-start | bytes 786440 | tf_op jit(solution)/shard_map/ppermute | solution.py:345
  26.8 3.9 %collective-permute-done.4.refs_5_ = bf16[544,128]{1,0:T(8,128)(2,1)S(1)} collective-permute-done((bf16[544,128]{1,0:T(8,128)(2,1)S(1)}, bf16[544,128]{1,0:T(8,128)(2,1)S(1)}, u32[]{:S(2)}, u32[]{:S(2)}) %collective-permute-start.4) | collective-permute-done | bytes 139296 | tf_op jit(solution)/shard_map/ppermute | solution.py:428
  30.7 0.5 %collective-permute-start.8 = (bf16[544,128]{1,0:T(8,128)(2,1)S(1)}, bf16[544,128]{1,0:T(8,128)(2,1)S(1)}, u32[]{:S(2)}, u32[]{:S(2)}) collective-permute-start(bf16[544,128]{1,0:T(8,128)(2,1)S(1)} %collective-permute-done.3.refs_4_), channel_id=1, source_target_pairs={{0,8},{8,0},{1,9},{9,1},{2,10},{10,2},{3,11},{11,3},{4,12},{12,4},... | collective-permute-start | bytes 417800 | tf_op jit(solution)/shard_map/ppermute | solution.py:345
  31.3 0.5 %collective-permute-start.10 = (bf16[544,128]{1,0:T(8,128)(2,1)S(1)}, bf16[544,128]{1,0:T(8,128)(2,1)S(1)}, u32[]{:S(2)}, u32[]{:S(2)}) collective-permute-start(bf16[544,128]{1,0:T(8,128)(2,1)S(1)} %collective-permute-done.5.refs_6_), channel_id=1, source_target_pairs={{0,8},{8,0},{1,9},{9,1},{2,10},{10,2},{3,11},{11,3},{4,12},{12,4},... | collective-permute-start | bytes 417800 | tf_op jit(solution)/shard_map/ppermute | solution.py:345
  31.8 1.7 %late_pages.1 = (f32[16,128,128]{2,1,0:T(8,128)S(1)}, f32[16,1,128]{2,1,0:T(1,128)S(1)}, f32[16,1,128]{2,1,0:T(1,128)S(1)}, bf16[96,2048]{1,0:T(8,128)(2,1)}) custom-call(s32[49]{0:T(128)S(1)} %get-tuple-element.21.plan_ref, bf16[12,128,128]{2,1,0:T(8,128)(2,1)S(1)} %bitcast.69, bf16[16,128,128]{2,1,0:T(8,128)(2,1)S(1)} %pad_bitcast_fusion.decode_ref, ...), custom_call_target="tpu_custom_call" | custom-call | flops 671088640 | bytes 4194304 | tf_op jit(solution)/shard_map/late_pages/pallas_call | solution.py:313
  33.6 2.5 %landed_pages.1 = bf16[96,2048]{1,0:T(8,128)(2,1)} custom-call(s32[49]{0:T(128)S(1)} %get-tuple-element.21.plan_ref, bf16[16,128,128]{2,1,0:T(8,128)(2,1)S(1)} %pad_bitcast_fusion.decode_ref, bf16[1024,128]{1,0:T(8,128)(2,1)S(1)} %collective-permute-done.7.early_ref, ...), custom_call_target="tpu_custom_call", output_to_operand_aliasing={{}: (10, {})} | custom-call | flops 134217728 | bytes 4194304 | tf_op jit(solution)/shard_map/landed_pages/pallas_call | solution.py:313
  (48 shorter events, 0.3 us)
Async XLA Ops:
  0.0 0.8 %copy-start.3 = (bf16[1,12,2,8,128]{4,3,2,1,0:T(8,128)(2,1)S(1)}, bf16[1,12,2,8,128]{4,3,2,1,0:T(8,128)(2,1)}, u32[]{:S(2)}) copy-start(bf16[1,12,2,8,128]{4,3,2,1,0:T(8,128)(2,1)} %param.7) | copy-start | bytes 147460
  2.4 24.4 %collective-permute-start.5 = (bf16[544,128]{1,0:T(8,128)(2,1)S(1)}, bf16[544,128]{1,0:T(8,128)(2,1)S(1)}, u32[]{:S(2)}, u32[]{:S(2)}) collective-permute-start(bf16[544,128]{1,0:T(8,128)(2,1)S(1)} %pad_maximum_fusion.6), channel_id=1, source_target_pairs={{0,5},{1,6},{2,7},{3,0},{4,1},{5,2},{6,3},{7,4},{8,13},{9,14},{10,... | collective-permute-start | bytes 417800 | tf_op jit(solution)/shard_map/ppermute | solution.py:428
  2.6 9.2 %collective-permute-start = (bf16[544,128]{1,0:T(8,128)(2,1)S(1)}, bf16[544,128]{1,0:T(8,128)(2,1)S(1)}, u32[]{:S(2)}, u32[]{:S(2)}) collective-permute-start(bf16[544,128]{1,0:T(8,128)(2,1)S(1)} %pad_maximum_fusion.1), channel_id=1, source_target_pairs={{0,6},{1,7},{2,0},{3,1},{4,2},{5,3},{6,4},{7,5},{8,14},{9,15},{10,... | collective-permute-start | bytes 417800 | tf_op jit(solution)/shard_map/ppermute | solution.py:428
  2.9 4.8 %copy-start.2 = (bf16[1,96,2048]{2,1,0:T(8,128)(2,1)S(1)}, bf16[1,96,2048]{2,1,0:T(8,128)(2,1)}, u32[]{:S(2)}) copy-start(bf16[1,96,2048]{2,1,0:T(8,128)(2,1)} %param.6) | copy-start | bytes 1179652
  2.9 8.9 %collective-permute-start.1 = (bf16[544,128]{1,0:T(8,128)(2,1)S(1)}, bf16[544,128]{1,0:T(8,128)(2,1)S(1)}, u32[]{:S(2)}, u32[]{:S(2)}) collective-permute-start(bf16[544,128]{1,0:T(8,128)(2,1)S(1)} %pad_maximum_fusion.2), channel_id=1, source_target_pairs={{0,1},{1,2},{2,3},{3,4},{4,5},{5,6},{6,7},{7,0},{8,9},{9,10},{10,1... | collective-permute-start | bytes 417800 | tf_op jit(solution)/shard_map/ppermute | solution.py:428
  6.9 13.1 %collective-permute-start.2 = (bf16[544,128]{1,0:T(8,128)(2,1)S(1)}, bf16[544,128]{1,0:T(8,128)(2,1)S(1)}, u32[]{:S(2)}, u32[]{:S(2)}) collective-permute-start(bf16[544,128]{1,0:T(8,128)(2,1)S(1)} %pad_maximum_fusion.3), channel_id=1, source_target_pairs={{0,2},{1,3},{2,4},{3,5},{4,6},{5,7},{6,0},{7,1},{8,10},{9,11},{10,... | collective-permute-start | bytes 417800 | tf_op jit(solution)/shard_map/ppermute | solution.py:428
  7.4 19.4 %collective-permute-start.3 = (bf16[544,128]{1,0:T(8,128)(2,1)S(1)}, bf16[544,128]{1,0:T(8,128)(2,1)S(1)}, u32[]{:S(2)}, u32[]{:S(2)}) collective-permute-start(bf16[544,128]{1,0:T(8,128)(2,1)S(1)} %pad_maximum_fusion.4), channel_id=1, source_target_pairs={{0,3},{1,4},{2,5},{3,6},{4,7},{5,0},{6,1},{7,2},{8,11},{9,12},{10,... | collective-permute-start | bytes 417800 | tf_op jit(solution)/shard_map/ppermute | solution.py:428
  9.3 10.7 %copy-start = (s32[16,4]{0,1:T(4,128)S(1)}, s32[16,4]{0,1:T(4,128)}, u32[]{:S(2)}) copy-start(s32[16,4]{0,1:T(4,128)} %param.10) | copy-start | bytes 772
  11.8 18.9 %collective-permute-start.4 = (bf16[544,128]{1,0:T(8,128)(2,1)S(1)}, bf16[544,128]{1,0:T(8,128)(2,1)S(1)}, u32[]{:S(2)}, u32[]{:S(2)}) collective-permute-start(bf16[544,128]{1,0:T(8,128)(2,1)S(1)} %pad_maximum_fusion.5), channel_id=1, source_target_pairs={{0,4},{1,5},{2,6},{3,7},{4,0},{5,1},{6,2},{7,3},{8,12},{9,13},{10,... | collective-permute-start | bytes 417800 | tf_op jit(solution)/shard_map/ppermute | solution.py:428
  11.8 18.9 %collective-permute-start.6 = (bf16[544,128]{1,0:T(8,128)(2,1)S(1)}, bf16[544,128]{1,0:T(8,128)(2,1)S(1)}, u32[]{:S(2)}, u32[]{:S(2)}) collective-permute-start(bf16[544,128]{1,0:T(8,128)(2,1)S(1)} %pad_maximum_fusion.7), channel_id=1, source_target_pairs={{0,7},{1,0},{2,1},{3,2},{4,3},{5,4},{6,5},{7,6},{8,15},{9,8},{10,9... | collective-permute-start | bytes 417800 | tf_op jit(solution)/shard_map/ppermute | solution.py:428
  20.1 0.7 %copy-start.1 = (s32[16]{0:T(128)S(1)}, s32[16]{0:T(128)}, u32[]{:S(2)}) copy-start(s32[16]{0:T(128)} %context_ref.1) | copy-start | bytes 196
  23.0 10.5 %collective-permute-start.7 = (bf16[1024,128]{1,0:T(8,128)(2,1)S(1)}, bf16[1024,128]{1,0:T(8,128)(2,1)S(1)}, u32[]{:S(2)}, u32[]{:S(2)}) collective-permute-start(bf16[1024,128]{1,0:T(8,128)(2,1)S(1)} %get-tuple-element.22), channel_id=1, source_target_pairs={{0,8},{8,0},{1,9},{9,1},{2,10},{10,2},{3,11},{11,3},{4,12},{12,4},... | collective-permute-start | bytes 786440 | tf_op jit(solution)/shard_map/ppermute | solution.py:345
  30.7 2.8 %collective-permute-start.8 = (bf16[544,128]{1,0:T(8,128)(2,1)S(1)}, bf16[544,128]{1,0:T(8,128)(2,1)S(1)}, u32[]{:S(2)}, u32[]{:S(2)}) collective-permute-start(bf16[544,128]{1,0:T(8,128)(2,1)S(1)} %collective-permute-done.3.refs_4_), channel_id=1, source_target_pairs={{0,8},{8,0},{1,9},{9,1},{2,10},{10,2},{3,11},{11,3},{4,12},{12,4},... | collective-permute-start | bytes 417800 | tf_op jit(solution)/shard_map/ppermute | solution.py:345
  31.3 2.3 %collective-permute-start.9 = (bf16[544,128]{1,0:T(8,128)(2,1)S(1)}, bf16[544,128]{1,0:T(8,128)(2,1)S(1)}, u32[]{:S(2)}, u32[]{:S(2)}) collective-permute-start(bf16[544,128]{1,0:T(8,128)(2,1)S(1)} %collective-permute-done.4.refs_5_), channel_id=1, source_target_pairs={{0,8},{8,0},{1,9},{9,1},{2,10},{10,2},{3,11},{11,3},{4,12},{12,4},... | collective-permute-start | bytes 417800 | tf_op jit(solution)/shard_map/ppermute | solution.py:345
  31.3 2.3 %collective-permute-start.10 = (bf16[544,128]{1,0:T(8,128)(2,1)S(1)}, bf16[544,128]{1,0:T(8,128)(2,1)S(1)}, u32[]{:S(2)}, u32[]{:S(2)}) collective-permute-start(bf16[544,128]{1,0:T(8,128)(2,1)S(1)} %collective-permute-done.5.refs_6_), channel_id=1, source_target_pairs={{0,8},{8,0},{1,9},{9,1},{2,10},{10,2},{3,11},{11,3},{4,12},{12,4},... | collective-permute-start | bytes 417800 | tf_op jit(solution)/shard_map/ppermute | solution.py:345
  31.8 1.8 %collective-permute-start.11 = (bf16[544,128]{1,0:T(8,128)(2,1)S(1)}, bf16[544,128]{1,0:T(8,128)(2,1)S(1)}, u32[]{:S(2)}, u32[]{:S(2)}) collective-permute-start(bf16[544,128]{1,0:T(8,128)(2,1)S(1)} %collective-permute-done.6.refs_7_), channel_id=1, source_target_pairs={{0,8},{8,0},{1,9},{9,1},{2,10},{10,2},{3,11},{11,3},{4,12},{12,4},... | collective-permute-start | bytes 417800 | tf_op jit(solution)/shard_map/ppermute | solution.py:345

commit v5 on v4

--- a/solution.py
+++ b/solution.py
@@ -41,6 +41,7 @@
         self.row_tiles = self.row_width // LANES
         self.decode_tiles = self.dec_rows * self.row_tiles
         self.tiles = max(self.prefill_tiles, self.decode_tiles)
+        self.chunk_rows = self.new_at + 2 * self.new_pad
         self.owner_at = 1
         self.valid_at = 1 + self.slots
 
@@ -219,8 +220,11 @@
         add_pages(z, pages, plan_ref, decode_ref, state)
 
 
-def second_kernel(z, groups, plan_ref, prefill_ref, decode_ref, *refs):
+def second_kernel(z, groups, stored_plan_ref, prefill_ref, decode_ref, *refs):
     shifts = groups[1]
+    refs, (plan_ref, plan_sem) = refs[:-2], refs[-2:]
+    plan_copy = pltpu.make_async_copy(stored_plan_ref, plan_ref, plan_sem)
+    plan_copy.start()
     before, new_ref, refs = refs[:3], refs[3], refs[4:]
     late, refs = refs[: len(shifts)], refs[len(shifts) :]
     state, (out_ref, held_ref, sems) = refs[:3], refs[3:]
@@ -231,6 +235,7 @@
 
     @on_side(0)
     def prefill():
+        plan_copy.wait()
         visible = jnp.concatenate(prefix_visible(z, plan_ref, shifts), axis=0)
         keys = prefix_rows(z, chunks, shifts, 0)
         cached = len(keys) * z.page
@@ -273,18 +278,27 @@
             part = soften(scores, new_values, z.scale)
             write(state, tile, merge(read(before, tile), part, z.scale))
         pages = local_pages(z, chunks, shifts)
+        plan_copy.wait()
         add_pages(z, pages, plan_ref, decode_ref, state)
 
 
-def last_kernel(z, groups, plan_ref, decode_ref, early_ref, *refs):
+def last_kernel(z, groups, stored_plan_ref, decode_ref, early_ref, *refs):
+    refs, (plan_ref, plan_sem) = refs[:-2], refs[-2:]
+    plan_copy = pltpu.make_async_copy(stored_plan_ref, plan_ref, plan_sem)
+    plan_copy.start()
     late, refs = refs[: len(groups[1])], refs[len(groups[1]) :]
     before, out_ref, refs = refs[:3], refs[4], refs[5:]
     state, (held_ref, rows_ref, sems) = refs[:3], refs[3:]
+
+    @on_side(0)
+    def prefill():
+        plan_copy.wait()
 
     @on_side(1)
     def decode():
         for ref, value in zip(state, before):
             ref[...] = value[...]
+        plan_copy.wait()
         places = [(early_ref, i * FIN_DEV * 2 * z.page) for i in range(len(groups[0]))]
         places += [(ref, z.prefix_pages * 2 * z.page) for ref in late]
         pages = landed_pages(z, places, groups[0] + groups[1])
@@ -379,16 +393,18 @@
         (early, late),
         "late_pages",
         len(late) * z.page + z.new_keys,
-        [("smem", plan)]
+        [("any", plan)]
         + [("vmem", value) for value in (prefill, decode, *first, new)]
         + [("vmem", chunks[d]) for d in late],
         state + [out],
         [
             pltpu.VMEM((z.prefill_tiles * LANES, z.head_dim), queries.dtype),
             pltpu.SemaphoreType.DMA((z.heads,)),
+            pltpu.SMEM(plan.shape, plan.dtype),
+            pltpu.SemaphoreType.DMA,
         ],
     )
-    operands = [("smem", plan)]
+    operands = [("any", plan)]
     operands += [("vmem", value) for value in (decode, *landed, *second)]
     (result,) = call(
         last_kernel,
@@ -403,6 +419,8 @@
             pltpu.VMEM((z.decode_tiles * LANES, z.head_dim), jnp.float32),
             pltpu.VMEM(queries.shape, queries.dtype),
             pltpu.SemaphoreType.DMA((z.steps,)),
+            pltpu.SMEM(plan.shape, plan.dtype),
+            pltpu.SemaphoreType.DMA,
         ],
         {len(operands): 0},
     )

time: 36.3 us -> 36 us (level)
  the two profiles are of different devices: /device:TPU:31 before, /device:TPU:29 now
where the time goes in v5:
time: 36 us; the launch traced here: 35.8 us
  starting transfers between devices  18.1 us (50%)
  waiting for transfers between devices  6.36 us (18%)
  Pallas kernels  6.22 us (17%)
  local copies, waits for them, and re-layouts  4 us (11%)
  between operations  0.96 us (3%)
    ppermute x7, starting transfers between devices, body(): chunks[d] = lax.ppermute(chunk_for(z.target(d)), 'tp', z.pairs(d))  13.3 us
    ppermute x7, waiting for transfers between devices, body(): chunks[d] = lax.ppermute(chunk_for(z.target(d)), 'tp', z.pairs(d))  6.35 us
    pallas_call x3, Pallas kernels, call(): pl.pallas_call(functools.partial(kernel, z, shifts), out_shape=[shape for...  6.22 us
    ppermute x5, starting transfers between devices, hand_over(): return lax.ppermute(pages, 'section', [(0, 1), (1, 0)])  4.84 us
    unnamed x17, local copies, waits for them, and re-layouts  1.57 us
    dynamic_slice x1, local copies, waits for them, and re-layouts, chunk_for(): pages = lax.dynamic_index_in_dim(store, head, axis=2, keepdims=False)  1.41 us
  transfers between devices with their start and end apart: 12, of which 2 were waited for; matrix products, arithmetic and copies ran while one was open for 3% of the time, Pallas kernels for 10%

profile of v5, /device:TPU:29, one launch (start us, length us, event | category | flops | bytes accessed | tf_op | source)
XLA Modules:
  0.0 35.8 jit_solution(16017598398500534827)
XLA Ops:
  0.0 0.8 %copy-done.3 = bf16[1,12,2,8,128]{4,3,2,1,0:T(8,128)(2,1)S(1)} copy-done((bf16[1,12,2,8,128]{4,3,2,1,0:T(8,128)(2,1)S(1)}, bf16[1,12,2,8,128]{4,3,2,1,0:T(8,128)(2,1)}, u32[]{:S(2)}) %copy-start.3) | copy-done | bytes 49176
  0.8 0.1 constant_dynamic-slice_fusion
  0.9 1.4 %constant_dynamic-slice_fusion.1 = (bf16[1,2,2,1,128,128]{5,4,3,2,1,0:T(8,128)(2,1)S(1)}, bf16[1,2,2,1,128,128]{5,4,3,2,1,0:T(8,128)(2,1)S(1)}, bf16[1,2,2,1,128...) fusion(bf16[1,2,2,8,128,128]{5,4,3,2,1,0:T(8,128)(2,1)} %param., ...), kind=kLoop, calls=%fused_computation.19 | loop fusion | bytes 2097184 | tf_op jit(solution)/shard_map/jit(dynamic_index_in_dim)/dynamic_slice | solution.py:437
  2.4 0.2 collective-permute-start.5
  2.6 0.2 collective-permute-start
  2.9 4.0 %collective-permute-start.1 = (bf16[544,128]{1,0:T(8,128)(2,1)S(1)}, bf16[544,128]{1,0:T(8,128)(2,1)S(1)}, u32[]{:S(2)}, u32[]{:S(2)}) collective-permute-start(bf16[544,128]{1,0:T(8,128)(2,1)S(1)} %pad_maximum_fusion.2), channel_id=1, source_target_pairs={{0,1},{1,2},{2,3},{3,4},{4,5},{5,6},{6,7},{7,0},{8,9},{9,10},{10,1... | collective-permute-start | bytes 417800 | tf_op jit(solution)/shard_map/ppermute | solution.py:446
  6.9 0.5 %collective-permute-start.2 = (bf16[544,128]{1,0:T(8,128)(2,1)S(1)}, bf16[544,128]{1,0:T(8,128)(2,1)S(1)}, u32[]{:S(2)}, u32[]{:S(2)}) collective-permute-start(bf16[544,128]{1,0:T(8,128)(2,1)S(1)} %pad_maximum_fusion.3), channel_id=1, source_target_pairs={{0,2},{1,3},{2,4},{3,5},{4,6},{5,7},{6,0},{7,1},{8,10},{9,11},{10,... | collective-permute-start | bytes 417800 | tf_op jit(solution)/shard_map/ppermute | solution.py:446
  7.4 0.2 collective-permute-start.3
  7.7 0.1 copy.47
  8.5 0.1 copy.27
  8.6 0.2 copy.28
  8.9 0.3 copy.30
  9.2 0.1 pad_bitcast_fusion.decode_ref
  9.3 0.0 copy-start
  9.4 2.4 %collective-permute-done.refs_1_ = bf16[544,128]{1,0:T(8,128)(2,1)S(1)} collective-permute-done((bf16[544,128]{1,0:T(8,128)(2,1)S(1)}, bf16[544,128]{1,0:T(8,128)(2,1)S(1)}, u32[]{:S(2)}, u32[]{:S(2)}) %collective-permute-start) | collective-permute-done | bytes 139296 | tf_op jit(solution)/shard_map/ppermute | solution.py:446
  11.8 8.3 %collective-permute-start.6 = (bf16[544,128]{1,0:T(8,128)(2,1)S(1)}, bf16[544,128]{1,0:T(8,128)(2,1)S(1)}, u32[]{:S(2)}, u32[]{:S(2)}) collective-permute-start(bf16[544,128]{1,0:T(8,128)(2,1)S(1)} %pad_maximum_fusion.7), channel_id=1, source_target_pairs={{0,7},{1,0},{2,1},{3,2},{4,3},{5,4},{6,5},{7,6},{8,15},{9,8},{10,9... | collective-permute-start | bytes 417800 | tf_op jit(solution)/shard_map/ppermute | solution.py:446
  20.1 0.7 %copy-done.1 = s32[16]{0:T(128)S(1)} copy-done((s32[16]{0:T(128)S(1)}, s32[16]{0:T(128)}, u32[]{:S(2)}) %copy-start.1) | copy-done | bytes 88
  20.7 2.3 %early_pages.1 = (s32[49]{0:T(128)S(1)}, bf16[1024,128]{1,0:T(8,128)(2,1)S(1)}, bf16[128,128]{1,0:T(8,128)(2,1)S(1)}, f32[16,128,128]{2,1,0:T(8,128)S(1)}, f32[1...) custom-call(s32[1]{0:T(128)S(6)} %copy.58.prefix_ref, s32[4,16]{1,0:T(4,128)S(1)} %bitcast.70, s32[16]{0:T(128)S(1)} %copy-done.1, ...), custom_call_target="tpu_custom_call" | custom-call | flops 536870912 | bytes 4194304 | tf_op jit(solution)/shard_map/early_pages/pallas_call | solution.py:327
  23.0 3.8 %collective-permute-start.7 = (bf16[1024,128]{1,0:T(8,128)(2,1)S(1)}, bf16[1024,128]{1,0:T(8,128)(2,1)S(1)}, u32[]{:S(2)}, u32[]{:S(2)}) collective-permute-start(bf16[1024,128]{1,0:T(8,128)(2,1)S(1)} %get-tuple-element.22), channel_id=1, source_target_pairs={{0,8},{8,0},{1,9},{9,1},{2,10},{10,2},{3,11},{11,3},{4,12},{12,4},... | collective-permute-start | bytes 786440 | tf_op jit(solution)/shard_map/ppermute | solution.py:359
  26.8 3.9 %collective-permute-done.4.refs_5_ = bf16[544,128]{1,0:T(8,128)(2,1)S(1)} collective-permute-done((bf16[544,128]{1,0:T(8,128)(2,1)S(1)}, bf16[544,128]{1,0:T(8,128)(2,1)S(1)}, u32[]{:S(2)}, u32[]{:S(2)}) %collective-permute-start.4) | collective-permute-done | bytes 139296 | tf_op jit(solution)/shard_map/ppermute | solution.py:446
  30.7 0.5 %collective-permute-start.8 = (bf16[544,128]{1,0:T(8,128)(2,1)S(1)}, bf16[544,128]{1,0:T(8,128)(2,1)S(1)}, u32[]{:S(2)}, u32[]{:S(2)}) collective-permute-start(bf16[544,128]{1,0:T(8,128)(2,1)S(1)} %collective-permute-done.3.refs_4_), channel_id=1, source_target_pairs={{0,8},{8,0},{1,9},{9,1},{2,10},{10,2},{3,11},{11,3},{4,12},{12,4},... | collective-permute-start | bytes 417800 | tf_op jit(solution)/shard_map/ppermute | solution.py:359
  31.3 0.5 %collective-permute-start.10 = (bf16[544,128]{1,0:T(8,128)(2,1)S(1)}, bf16[544,128]{1,0:T(8,128)(2,1)S(1)}, u32[]{:S(2)}, u32[]{:S(2)}) collective-permute-start(bf16[544,128]{1,0:T(8,128)(2,1)S(1)} %collective-permute-done.5.refs_6_), channel_id=1, source_target_pairs={{0,8},{8,0},{1,9},{9,1},{2,10},{10,2},{3,11},{11,3},{4,12},{12,4},... | collective-permute-start | bytes 417800 | tf_op jit(solution)/shard_map/ppermute | solution.py:359
  31.8 1.4 %late_pages.1 = (f32[16,128,128]{2,1,0:T(8,128)S(1)}, f32[16,1,128]{2,1,0:T(1,128)S(1)}, f32[16,1,128]{2,1,0:T(1,128)S(1)}, bf16[96,2048]{1,0:T(8,128)(2,1)}) custom-call(s32[49]{0:T(128)S(1)} %get-tuple-element.21.stored_plan_ref, bf16[12,128,128]{2,1,0:T(8,128)(2,1)S(1)} %bitcast.69, bf16[16,128,128]{2,1,0:T(8,128)(2,1)S(1)} %pad_bitcast_fusion.decode_ref, ...), custom_call_target="tpu_custom_call" | custom-call | flops 671088640 | bytes 4194304 | tf_op jit(solution)/shard_map/late_pages/pallas_call | solution.py:327
  33.2 2.5 %landed_pages.1 = bf16[96,2048]{1,0:T(8,128)(2,1)} custom-call(s32[49]{0:T(128)S(1)} %get-tuple-element.21.stored_plan_ref, bf16[16,128,128]{2,1,0:T(8,128)(2,1)S(1)} %pad_bitcast_fusion.decode_ref, bf16[1024,128]{1,0:T(8,128)(2,1)S(1)} %collective-permute-done.7.early_ref, ...), custom_call_target="tpu_custom_call", output_to_operand_aliasing={{}: (10, {})} | custom-call | flops 134217728 | bytes 4194304 | tf_op jit(solution)/shard_map/landed_pages/pallas_call | solution.py:327
  (48 shorter events, 0.3 us)
Async XLA Ops:
  0.0 0.8 %copy-start.3 = (bf16[1,12,2,8,128]{4,3,2,1,0:T(8,128)(2,1)S(1)}, bf16[1,12,2,8,128]{4,3,2,1,0:T(8,128)(2,1)}, u32[]{:S(2)}) copy-start(bf16[1,12,2,8,128]{4,3,2,1,0:T(8,128)(2,1)} %param.7) | copy-start | bytes 147460
  2.4 24.4 %collective-permute-start.5 = (bf16[544,128]{1,0:T(8,128)(2,1)S(1)}, bf16[544,128]{1,0:T(8,128)(2,1)S(1)}, u32[]{:S(2)}, u32[]{:S(2)}) collective-permute-start(bf16[544,128]{1,0:T(8,128)(2,1)S(1)} %pad_maximum_fusion.6), channel_id=1, source_target_pairs={{0,5},{1,6},{2,7},{3,0},{4,1},{5,2},{6,3},{7,4},{8,13},{9,14},{10,... | collective-permute-start | bytes 417800 | tf_op jit(solution)/shard_map/ppermute | solution.py:446
  2.6 9.2 %collective-permute-start = (bf16[544,128]{1,0:T(8,128)(2,1)S(1)}, bf16[544,128]{1,0:T(8,128)(2,1)S(1)}, u32[]{:S(2)}, u32[]{:S(2)}) collective-permute-start(bf16[544,128]{1,0:T(8,128)(2,1)S(1)} %pad_maximum_fusion.1), channel_id=1, source_target_pairs={{0,6},{1,7},{2,0},{3,1},{4,2},{5,3},{6,4},{7,5},{8,14},{9,15},{10,... | collective-permute-start | bytes 417800 | tf_op jit(solution)/shard_map/ppermute | solution.py:446
  2.9 4.8 %copy-start.2 = (bf16[1,96,2048]{2,1,0:T(8,128)(2,1)S(1)}, bf16[1,96,2048]{2,1,0:T(8,128)(2,1)}, u32[]{:S(2)}) copy-start(bf16[1,96,2048]{2,1,0:T(8,128)(2,1)} %param.6) | copy-start | bytes 1179652
  2.9 8.9 %collective-permute-start.1 = (bf16[544,128]{1,0:T(8,128)(2,1)S(1)}, bf16[544,128]{1,0:T(8,128)(2,1)S(1)}, u32[]{:S(2)}, u32[]{:S(2)}) collective-permute-start(bf16[544,128]{1,0:T(8,128)(2,1)S(1)} %pad_maximum_fusion.2), channel_id=1, source_target_pairs={{0,1},{1,2},{2,3},{3,4},{4,5},{5,6},{6,7},{7,0},{8,9},{9,10},{10,1... | collective-permute-start | bytes 417800 | tf_op jit(solution)/shard_map/ppermute | solution.py:446
  6.9 13.1 %collective-permute-start.2 = (bf16[544,128]{1,0:T(8,128)(2,1)S(1)}, bf16[544,128]{1,0:T(8,128)(2,1)S(1)}, u32[]{:S(2)}, u32[]{:S(2)}) collective-permute-start(bf16[544,128]{1,0:T(8,128)(2,1)S(1)} %pad_maximum_fusion.3), channel_id=1, source_target_pairs={{0,2},{1,3},{2,4},{3,5},{4,6},{5,7},{6,0},{7,1},{8,10},{9,11},{10,... | collective-permute-start | bytes 417800 | tf_op jit(solution)/shard_map/ppermute | solution.py:446
  7.4 19.4 %collective-permute-start.3 = (bf16[544,128]{1,0:T(8,128)(2,1)S(1)}, bf16[544,128]{1,0:T(8,128)(2,1)S(1)}, u32[]{:S(2)}, u32[]{:S(2)}) collective-permute-start(bf16[544,128]{1,0:T(8,128)(2,1)S(1)} %pad_maximum_fusion.4), channel_id=1, source_target_pairs={{0,3},{1,4},{2,5},{3,6},{4,7},{5,0},{6,1},{7,2},{8,11},{9,12},{10,... | collective-permute-start | bytes 417800 | tf_op jit(solution)/shard_map/ppermute | solution.py:446
  9.3 10.7 %copy-start = (s32[16,4]{0,1:T(4,128)S(1)}, s32[16,4]{0,1:T(4,128)}, u32[]{:S(2)}) copy-start(s32[16,4]{0,1:T(4,128)} %param.10) | copy-start | bytes 772
  11.8 18.9 %collective-permute-start.4 = (bf16[544,128]{1,0:T(8,128)(2,1)S(1)}, bf16[544,128]{1,0:T(8,128)(2,1)S(1)}, u32[]{:S(2)}, u32[]{:S(2)}) collective-permute-start(bf16[544,128]{1,0:T(8,128)(2,1)S(1)} %pad_maximum_fusion.5), channel_id=1, source_target_pairs={{0,4},{1,5},{2,6},{3,7},{4,0},{5,1},{6,2},{7,3},{8,12},{9,13},{10,... | collective-permute-start | bytes 417800 | tf_op jit(solution)/shard_map/ppermute | solution.py:446
  11.8 18.9 %collective-permute-start.6 = (bf16[544,128]{1,0:T(8,128)(2,1)S(1)}, bf16[544,128]{1,0:T(8,128)(2,1)S(1)}, u32[]{:S(2)}, u32[]{:S(2)}) collective-permute-start(bf16[544,128]{1,0:T(8,128)(2,1)S(1)} %pad_maximum_fusion.7), channel_id=1, source_target_pairs={{0,7},{1,0},{2,1},{3,2},{4,3},{5,4},{6,5},{7,6},{8,15},{9,8},{10,9... | collective-permute-start | bytes 417800 | tf_op jit(solution)/shard_map/ppermute | solution.py:446
  20.1 0.7 %copy-start.1 = (s32[16]{0:T(128)S(1)}, s32[16]{0:T(128)}, u32[]{:S(2)}) copy-start(s32[16]{0:T(128)} %context_ref.1) | copy-start | bytes 196
  23.0 10.2 %collective-permute-start.7 = (bf16[1024,128]{1,0:T(8,128)(2,1)S(1)}, bf16[1024,128]{1,0:T(8,128)(2,1)S(1)}, u32[]{:S(2)}, u32[]{:S(2)}) collective-permute-start(bf16[1024,128]{1,0:T(8,128)(2,1)S(1)} %get-tuple-element.22), channel_id=1, source_target_pairs={{0,8},{8,0},{1,9},{9,1},{2,10},{10,2},{3,11},{11,3},{4,12},{12,4},... | collective-permute-start | bytes 786440 | tf_op jit(solution)/shard_map/ppermute | solution.py:359
  30.7 2.5 %collective-permute-start.8 = (bf16[544,128]{1,0:T(8,128)(2,1)S(1)}, bf16[544,128]{1,0:T(8,128)(2,1)S(1)}, u32[]{:S(2)}, u32[]{:S(2)}) collective-permute-start(bf16[544,128]{1,0:T(8,128)(2,1)S(1)} %collective-permute-done.3.refs_4_), channel_id=1, source_target_pairs={{0,8},{8,0},{1,9},{9,1},{2,10},{10,2},{3,11},{11,3},{4,12},{12,4},... | collective-permute-start | bytes 417800 | tf_op jit(solution)/shard_map/ppermute | solution.py:359
  31.3 1.9 %collective-permute-start.9 = (bf16[544,128]{1,0:T(8,128)(2,1)S(1)}, bf16[544,128]{1,0:T(8,128)(2,1)S(1)}, u32[]{:S(2)}, u32[]{:S(2)}) collective-permute-start(bf16[544,128]{1,0:T(8,128)(2,1)S(1)} %collective-permute-done.4.refs_5_), channel_id=1, source_target_pairs={{0,8},{8,0},{1,9},{9,1},{2,10},{10,2},{3,11},{11,3},{4,12},{12,4},... | collective-permute-start | bytes 417800 | tf_op jit(solution)/shard_map/ppermute | solution.py:359
  31.3 1.9 %collective-permute-start.10 = (bf16[544,128]{1,0:T(8,128)(2,1)S(1)}, bf16[544,128]{1,0:T(8,128)(2,1)S(1)}, u32[]{:S(2)}, u32[]{:S(2)}) collective-permute-start(bf16[544,128]{1,0:T(8,128)(2,1)S(1)} %collective-permute-done.5.refs_6_), channel_id=1, source_target_pairs={{0,8},{8,0},{1,9},{9,1},{2,10},{10,2},{3,11},{11,3},{4,12},{12,4},... | collective-permute-start | bytes 417800 | tf_op jit(solution)/shard_map/ppermute | solution.py:359
  31.8 1.4 %collective-permute-start.11 = (bf16[544,128]{1,0:T(8,128)(2,1)S(1)}, bf16[544,128]{1,0:T(8,128)(2,1)S(1)}, u32[]{:S(2)}, u32[]{:S(2)}) collective-permute-start(bf16[544,128]{1,0:T(8,128)(2,1)S(1)} %collective-permute-done.6.refs_7_), channel_id=1, source_target_pairs={{0,8},{8,0},{1,9},{9,1},{2,10},{10,2},{3,11},{11,3},{4,12},{12,4},... | collective-permute-start | bytes 417800 | tf_op jit(solution)/shard_map/ppermute | solution.py:359

commit v6 on v5

--- a/solution.py
+++ b/solution.py
@@ -416,7 +416,7 @@
         [out],
         [pltpu.VMEM(shape.shape, shape.dtype) for _, shape in state]
         + [
-            pltpu.VMEM((z.decode_tiles * LANES, z.head_dim), jnp.float32),
+            pltpu.VMEM((z.decode_tiles * LANES + z.row_width, z.head_dim), jnp.float32),
             pltpu.VMEM(queries.shape, queries.dtype),
             pltpu.SemaphoreType.DMA((z.steps,)),
             pltpu.SMEM(plan.shape, plan.dtype),
@@ -439,7 +439,7 @@
         new = jnp.pad(new, ((0, 0), (0, z.new_pad - z.new_rows), (0, 0)))
         return jnp.concatenate([pages.reshape((-1, z.head_dim)), new.reshape((-1, z.head_dim))])
 
-    order = [tp - 2] + list(range(1, tp - 2)) + [tp - 1]
+    order = [2, tp - 2, 1] + list(range(3, tp - 2)) + [tp - 1]
     early, late = [0] + order[: tp // 2 - 1], order[tp // 2 - 1 :]
     chunks = {0: chunk_for(lax.axis_index("tp"))}
     for d in order:

time: 36 us -> 35.9 us (level)
  the two profiles are of different devices: /device:TPU:29 before, /device:TPU:13 now
where the time goes in v6:
time: 35.9 us; the launch traced here: 35.2 us
  starting transfers between devices  19 us (53%)
  Pallas kernels  6.22 us (17%)
  waiting for transfers between devices  4.92 us (14%)
  local copies, waits for them, and re-layouts  4 us (11%)
  between operations  0.97 us (3%)
    ppermute x7, starting transfers between devices, body(): chunks[d] = lax.ppermute(chunk_for(z.target(d)), 'tp', z.pairs(d))  15 us
    pallas_call x3, Pallas kernels, call(): pl.pallas_call(functools.partial(kernel, z, shifts), out_shape=[shape for...  6.22 us
    ppermute x7, waiting for transfers between devices, body(): chunks[d] = lax.ppermute(chunk_for(z.target(d)), 'tp', z.pairs(d))  4.9 us
    ppermute x5, starting transfers between devices, hand_over(): return lax.ppermute(pages, 'section', [(0, 1), (1, 0)])  3.98 us
    unnamed x17, local copies, waits for them, and re-layouts  1.57 us
    dynamic_slice x1, local copies, waits for them, and re-layouts, chunk_for(): pages = lax.dynamic_index_in_dim(store, head, axis=2, keepdims=False)  1.41 us
  transfers between devices with their start and end apart: 12, of which 3 were waited for; matrix products, arithmetic and copies ran while one was open for 3% of the time, Pallas kernels for 11%

profile of v6, /device:TPU:13, one launch (start us, length us, event | category | flops | bytes accessed | tf_op | source)
XLA Modules:
  0.0 35.2 jit_solution(10737945887246528999)
XLA Ops:
  0.0 0.8 %copy-done.3 = bf16[1,12,2,8,128]{4,3,2,1,0:T(8,128)(2,1)S(1)} copy-done((bf16[1,12,2,8,128]{4,3,2,1,0:T(8,128)(2,1)S(1)}, bf16[1,12,2,8,128]{4,3,2,1,0:T(8,128)(2,1)}, u32[]{:S(2)}) %copy-start.3) | copy-done | bytes 49176
  0.8 0.1 constant_dynamic-slice_fusion
  0.9 1.4 %constant_dynamic-slice_fusion.1 = (bf16[1,2,2,1,128,128]{5,4,3,2,1,0:T(8,128)(2,1)S(1)}, bf16[1,2,2,1,128,128]{5,4,3,2,1,0:T(8,128)(2,1)S(1)}, bf16[1,2,2,1,128...) fusion(bf16[1,2,2,8,128,128]{5,4,3,2,1,0:T(8,128)(2,1)} %param., ...), kind=kLoop, calls=%fused_computation.19 | loop fusion | bytes 2097184 | tf_op jit(solution)/shard_map/jit(dynamic_index_in_dim)/dynamic_slice | solution.py:437
  2.5 1.4 %collective-permute-start = (bf16[544,128]{1,0:T(8,128)(2,1)S(1)}, bf16[544,128]{1,0:T(8,128)(2,1)S(1)}, u32[]{:S(2)}, u32[]{:S(2)}) collective-permute-start(bf16[544,128]{1,0:T(8,128)(2,1)S(1)} %pad_maximum_fusion.1), channel_id=1, source_target_pairs={{0,2},{1,3},{2,4},{3,5},{4,6},{5,7},{6,0},{7,1},{8,10},{9,11},{10,... | collective-permute-start | bytes 417800 | tf_op jit(solution)/shard_map/ppermute | solution.py:446
  4.0 2.1 %collective-permute-start.1 = (bf16[544,128]{1,0:T(8,128)(2,1)S(1)}, bf16[544,128]{1,0:T(8,128)(2,1)S(1)}, u32[]{:S(2)}, u32[]{:S(2)}) collective-permute-start(bf16[544,128]{1,0:T(8,128)(2,1)S(1)} %pad_maximum_fusion.2), channel_id=1, source_target_pairs={{0,6},{1,7},{2,0},{3,1},{4,2},{5,3},{6,4},{7,5},{8,14},{9,15},{10,... | collective-permute-start | bytes 417800 | tf_op jit(solution)/shard_map/ppermute | solution.py:446
  6.2 1.3 %collective-permute-start.2 = (bf16[544,128]{1,0:T(8,128)(2,1)S(1)}, bf16[544,128]{1,0:T(8,128)(2,1)S(1)}, u32[]{:S(2)}, u32[]{:S(2)}) collective-permute-start(bf16[544,128]{1,0:T(8,128)(2,1)S(1)} %pad_maximum_fusion.3), channel_id=1, source_target_pairs={{0,1},{1,2},{2,3},{3,4},{4,5},{5,6},{6,7},{7,0},{8,9},{9,10},{10,1... | collective-permute-start | bytes 417800 | tf_op jit(solution)/shard_map/ppermute | solution.py:446
  7.5 2.1 %collective-permute-start.3 = (bf16[544,128]{1,0:T(8,128)(2,1)S(1)}, bf16[544,128]{1,0:T(8,128)(2,1)S(1)}, u32[]{:S(2)}, u32[]{:S(2)}) collective-permute-start(bf16[544,128]{1,0:T(8,128)(2,1)S(1)} %pad_maximum_fusion.4), channel_id=1, source_target_pairs={{0,3},{1,4},{2,5},{3,6},{4,7},{5,0},{6,1},{7,2},{8,11},{9,12},{10,... | collective-permute-start | bytes 417800 | tf_op jit(solution)/shard_map/ppermute | solution.py:446
  9.7 0.1 copy.47
  10.5 0.1 copy.27
  10.6 0.2 copy.28
  10.9 0.3 copy.30
  11.2 0.1 pad_bitcast_fusion.decode_ref
  11.3 0.7 %collective-permute-done.refs_1_ = bf16[544,128]{1,0:T(8,128)(2,1)S(1)} collective-permute-done((bf16[544,128]{1,0:T(8,128)(2,1)S(1)}, bf16[544,128]{1,0:T(8,128)(2,1)S(1)}, u32[]{:S(2)}, u32[]{:S(2)}) %collective-permute-start) | collective-permute-done | bytes 139296 | tf_op jit(solution)/shard_map/ppermute | solution.py:446
  12.0 1.4 %collective-permute-start.4 = (bf16[544,128]{1,0:T(8,128)(2,1)S(1)}, bf16[544,128]{1,0:T(8,128)(2,1)S(1)}, u32[]{:S(2)}, u32[]{:S(2)}) collective-permute-start(bf16[544,128]{1,0:T(8,128)(2,1)S(1)} %pad_maximum_fusion.5), channel_id=1, source_target_pairs={{0,4},{1,5},{2,6},{3,7},{4,0},{5,1},{6,2},{7,3},{8,12},{9,13},{10,... | collective-permute-start | bytes 417800 | tf_op jit(solution)/shard_map/ppermute | solution.py:446
  13.4 6.6 %collective-permute-start.6 = (bf16[544,128]{1,0:T(8,128)(2,1)S(1)}, bf16[544,128]{1,0:T(8,128)(2,1)S(1)}, u32[]{:S(2)}, u32[]{:S(2)}) collective-permute-start(bf16[544,128]{1,0:T(8,128)(2,1)S(1)} %pad_maximum_fusion.7), channel_id=1, source_target_pairs={{0,7},{1,0},{2,1},{3,2},{4,3},{5,4},{6,5},{7,6},{8,15},{9,8},{10,9... | collective-permute-start | bytes 417800 | tf_op jit(solution)/shard_map/ppermute | solution.py:446
  20.1 0.7 %copy-done.1 = s32[16]{0:T(128)S(1)} copy-done((s32[16]{0:T(128)S(1)}, s32[16]{0:T(128)}, u32[]{:S(2)}) %copy-start.1) | copy-done | bytes 88
  20.7 2.3 %early_pages.1 = (s32[49]{0:T(128)S(1)}, bf16[1024,128]{1,0:T(8,128)(2,1)S(1)}, bf16[128,128]{1,0:T(8,128)(2,1)S(1)}, f32[16,128,128]{2,1,0:T(8,128)S(1)}, f32[1...) custom-call(s32[1]{0:T(128)S(6)} %copy.58.prefix_ref, s32[4,16]{1,0:T(4,128)S(1)} %bitcast.70, s32[16]{0:T(128)S(1)} %copy-done.1, ...), custom_call_target="tpu_custom_call" | custom-call | flops 536870912 | bytes 4194304 | tf_op jit(solution)/shard_map/early_pages/pallas_call | solution.py:327
  23.0 2.8 %collective-permute-start.7 = (bf16[1024,128]{1,0:T(8,128)(2,1)S(1)}, bf16[1024,128]{1,0:T(8,128)(2,1)S(1)}, u32[]{:S(2)}, u32[]{:S(2)}) collective-permute-start(bf16[1024,128]{1,0:T(8,128)(2,1)S(1)} %get-tuple-element.22), channel_id=1, source_target_pairs={{0,8},{8,0},{1,9},{9,1},{2,10},{10,2},{3,11},{11,3},{4,12},{12,4},... | collective-permute-start | bytes 786440 | tf_op jit(solution)/shard_map/ppermute | solution.py:359
  25.8 1.3 %collective-permute-done.4.refs_5_ = bf16[544,128]{1,0:T(8,128)(2,1)S(1)} collective-permute-done((bf16[544,128]{1,0:T(8,128)(2,1)S(1)}, bf16[544,128]{1,0:T(8,128)(2,1)S(1)}, u32[]{:S(2)}, u32[]{:S(2)}) %collective-permute-start.4) | collective-permute-done | bytes 139296 | tf_op jit(solution)/shard_map/ppermute | solution.py:446
  27.1 2.9 %collective-permute-done.6.refs_7_ = bf16[544,128]{1,0:T(8,128)(2,1)S(1)} collective-permute-done((bf16[544,128]{1,0:T(8,128)(2,1)S(1)}, bf16[544,128]{1,0:T(8,128)(2,1)S(1)}, u32[]{:S(2)}, u32[]{:S(2)}) %collective-permute-start.6) | collective-permute-done | bytes 139296 | tf_op jit(solution)/shard_map/ppermute | solution.py:446
  30.0 0.7 %collective-permute-start.8 = (bf16[544,128]{1,0:T(8,128)(2,1)S(1)}, bf16[544,128]{1,0:T(8,128)(2,1)S(1)}, u32[]{:S(2)}, u32[]{:S(2)}) collective-permute-start(bf16[544,128]{1,0:T(8,128)(2,1)S(1)} %collective-permute-done.3.refs_4_), channel_id=1, source_target_pairs={{0,8},{8,0},{1,9},{9,1},{2,10},{10,2},{3,11},{11,3},{4,12},{12,4},... | collective-permute-start | bytes 417800 | tf_op jit(solution)/shard_map/ppermute | solution.py:359
  30.7 0.5 %collective-permute-start.10 = (bf16[544,128]{1,0:T(8,128)(2,1)S(1)}, bf16[544,128]{1,0:T(8,128)(2,1)S(1)}, u32[]{:S(2)}, u32[]{:S(2)}) collective-permute-start(bf16[544,128]{1,0:T(8,128)(2,1)S(1)} %collective-permute-done.5.refs_6_), channel_id=1, source_target_pairs={{0,8},{8,0},{1,9},{9,1},{2,10},{10,2},{3,11},{11,3},{4,12},{12,4},... | collective-permute-start | bytes 417800 | tf_op jit(solution)/shard_map/ppermute | solution.py:359
  31.2 1.4 %late_pages.1 = (f32[16,128,128]{2,1,0:T(8,128)S(1)}, f32[16,1,128]{2,1,0:T(1,128)S(1)}, f32[16,1,128]{2,1,0:T(1,128)S(1)}, bf16[96,2048]{1,0:T(8,128)(2,1)}) custom-call(s32[49]{0:T(128)S(1)} %get-tuple-element.21.stored_plan_ref, bf16[12,128,128]{2,1,0:T(8,128)(2,1)S(1)} %bitcast.69, bf16[16,128,128]{2,1,0:T(8,128)(2,1)S(1)} %pad_bitcast_fusion.decode_ref, ...), custom_call_target="tpu_custom_call" | custom-call | flops 671088640 | bytes 4194304 | tf_op jit(solution)/shard_map/late_pages/pallas_call | solution.py:327
  32.7 2.5 %landed_pages.1 = bf16[96,2048]{1,0:T(8,128)(2,1)} custom-call(s32[49]{0:T(128)S(1)} %get-tuple-element.21.stored_plan_ref, bf16[16,128,128]{2,1,0:T(8,128)(2,1)S(1)} %pad_bitcast_fusion.decode_ref, bf16[1024,128]{1,0:T(8,128)(2,1)S(1)} %collective-permute-done.7.early_ref, ...), custom_call_target="tpu_custom_call", output_to_operand_aliasing={{}: (10, {})} | custom-call | flops 134217728 | bytes 4194304 | tf_op jit(solution)/shard_map/landed_pages/pallas_call | solution.py:327
  (48 shorter events, 0.4 us)
Async XLA Ops:
  0.0 0.8 %copy-start.3 = (bf16[1,12,2,8,128]{4,3,2,1,0:T(8,128)(2,1)S(1)}, bf16[1,12,2,8,128]{4,3,2,1,0:T(8,128)(2,1)}, u32[]{:S(2)}) copy-start(bf16[1,12,2,8,128]{4,3,2,1,0:T(8,128)(2,1)} %param.7) | copy-start | bytes 147460
  2.4 23.4 %collective-permute-start.5 = (bf16[544,128]{1,0:T(8,128)(2,1)S(1)}, bf16[544,128]{1,0:T(8,128)(2,1)S(1)}, u32[]{:S(2)}, u32[]{:S(2)}) collective-permute-start(bf16[544,128]{1,0:T(8,128)(2,1)S(1)} %pad_maximum_fusion.6), channel_id=1, source_target_pairs={{0,5},{1,6},{2,7},{3,0},{4,1},{5,2},{6,3},{7,4},{8,13},{9,14},{10,... | collective-permute-start | bytes 417800 | tf_op jit(solution)/shard_map/ppermute | solution.py:446
  2.5 9.5 %collective-permute-start = (bf16[544,128]{1,0:T(8,128)(2,1)S(1)}, bf16[544,128]{1,0:T(8,128)(2,1)S(1)}, u32[]{:S(2)}, u32[]{:S(2)}) collective-permute-start(bf16[544,128]{1,0:T(8,128)(2,1)S(1)} %pad_maximum_fusion.1), channel_id=1, source_target_pairs={{0,2},{1,3},{2,4},{3,5},{4,6},{5,7},{6,0},{7,1},{8,10},{9,11},{10,... | collective-permute-start | bytes 417800 | tf_op jit(solution)/shard_map/ppermute | solution.py:446
  4.0 5.6 %copy-start.2 = (bf16[1,96,2048]{2,1,0:T(8,128)(2,1)S(1)}, bf16[1,96,2048]{2,1,0:T(8,128)(2,1)}, u32[]{:S(2)}) copy-start(bf16[1,96,2048]{2,1,0:T(8,128)(2,1)} %param.6) | copy-start | bytes 1179652
  4.0 9.4 %collective-permute-start.1 = (bf16[544,128]{1,0:T(8,128)(2,1)S(1)}, bf16[544,128]{1,0:T(8,128)(2,1)S(1)}, u32[]{:S(2)}, u32[]{:S(2)}) collective-permute-start(bf16[544,128]{1,0:T(8,128)(2,1)S(1)} %pad_maximum_fusion.2), channel_id=1, source_target_pairs={{0,6},{1,7},{2,0},{3,1},{4,2},{5,3},{6,4},{7,5},{8,14},{9,15},{10,... | collective-permute-start | bytes 417800 | tf_op jit(solution)/shard_map/ppermute | solution.py:446
  6.2 13.9 %collective-permute-start.2 = (bf16[544,128]{1,0:T(8,128)(2,1)S(1)}, bf16[544,128]{1,0:T(8,128)(2,1)S(1)}, u32[]{:S(2)}, u32[]{:S(2)}) collective-permute-start(bf16[544,128]{1,0:T(8,128)(2,1)S(1)} %pad_maximum_fusion.3), channel_id=1, source_target_pairs={{0,1},{1,2},{2,3},{3,4},{4,5},{5,6},{6,7},{7,0},{8,9},{9,10},{10,1... | collective-permute-start | bytes 417800 | tf_op jit(solution)/shard_map/ppermute | solution.py:446
  7.5 18.3 %collective-permute-start.3 = (bf16[544,128]{1,0:T(8,128)(2,1)S(1)}, bf16[544,128]{1,0:T(8,128)(2,1)S(1)}, u32[]{:S(2)}, u32[]{:S(2)}) collective-permute-start(bf16[544,128]{1,0:T(8,128)(2,1)S(1)} %pad_maximum_fusion.4), channel_id=1, source_target_pairs={{0,3},{1,4},{2,5},{3,6},{4,7},{5,0},{6,1},{7,2},{8,11},{9,12},{10,... | collective-permute-start | bytes 417800 | tf_op jit(solution)/shard_map/ppermute | solution.py:446
  11.3 8.8 %copy-start = (s32[16,4]{0,1:T(4,128)S(1)}, s32[16,4]{0,1:T(4,128)}, u32[]{:S(2)}) copy-start(s32[16,4]{0,1:T(4,128)} %param.10) | copy-start | bytes 772
  12.0 15.1 %collective-permute-start.4 = (bf16[544,128]{1,0:T(8,128)(2,1)S(1)}, bf16[544,128]{1,0:T(8,128)(2,1)S(1)}, u32[]{:S(2)}, u32[]{:S(2)}) collective-permute-start(bf16[544,128]{1,0:T(8,128)(2,1)S(1)} %pad_maximum_fusion.5), channel_id=1, source_target_pairs={{0,4},{1,5},{2,6},{3,7},{4,0},{5,1},{6,2},{7,3},{8,12},{9,13},{10,... | collective-permute-start | bytes 417800 | tf_op jit(solution)/shard_map/ppermute | solution.py:446
  13.4 16.6 %collective-permute-start.6 = (bf16[544,128]{1,0:T(8,128)(2,1)S(1)}, bf16[544,128]{1,0:T(8,128)(2,1)S(1)}, u32[]{:S(2)}, u32[]{:S(2)}) collective-permute-start(bf16[544,128]{1,0:T(8,128)(2,1)S(1)} %pad_maximum_fusion.7), channel_id=1, source_target_pairs={{0,7},{1,0},{2,1},{3,2},{4,3},{5,4},{6,5},{7,6},{8,15},{9,8},{10,9... | collective-permute-start | bytes 417800 | tf_op jit(solution)/shard_map/ppermute | solution.py:446
  20.1 0.7 %copy-start.1 = (s32[16]{0:T(128)S(1)}, s32[16]{0:T(128)}, u32[]{:S(2)}) copy-start(s32[16]{0:T(128)} %context_ref.1) | copy-start | bytes 196
  23.0 9.6 %collective-permute-start.7 = (bf16[1024,128]{1,0:T(8,128)(2,1)S(1)}, bf16[1024,128]{1,0:T(8,128)(2,1)S(1)}, u32[]{:S(2)}, u32[]{:S(2)}) collective-permute-start(bf16[1024,128]{1,0:T(8,128)(2,1)S(1)} %get-tuple-element.22), channel_id=1, source_target_pairs={{0,8},{8,0},{1,9},{9,1},{2,10},{10,2},{3,11},{11,3},{4,12},{12,4},... | collective-permute-start | bytes 786440 | tf_op jit(solution)/shard_map/ppermute | solution.py:359
  30.0 2.6 %collective-permute-start.8 = (bf16[544,128]{1,0:T(8,128)(2,1)S(1)}, bf16[544,128]{1,0:T(8,128)(2,1)S(1)}, u32[]{:S(2)}, u32[]{:S(2)}) collective-permute-start(bf16[544,128]{1,0:T(8,128)(2,1)S(1)} %collective-permute-done.3.refs_4_), channel_id=1, source_target_pairs={{0,8},{8,0},{1,9},{9,1},{2,10},{10,2},{3,11},{11,3},{4,12},{12,4},... | collective-permute-start | bytes 417800 | tf_op jit(solution)/shard_map/ppermute | solution.py:359
  30.7 1.9 %collective-permute-start.9 = (bf16[544,128]{1,0:T(8,128)(2,1)S(1)}, bf16[544,128]{1,0:T(8,128)(2,1)S(1)}, u32[]{:S(2)}, u32[]{:S(2)}) collective-permute-start(bf16[544,128]{1,0:T(8,128)(2,1)S(1)} %collective-permute-done.4.refs_5_), channel_id=1, source_target_pairs={{0,8},{8,0},{1,9},{9,1},{2,10},{10,2},{3,11},{11,3},{4,12},{12,4},... | collective-permute-start | bytes 417800 | tf_op jit(solution)/shard_map/ppermute | solution.py:359
  30.7 1.9 %collective-permute-start.10 = (bf16[544,128]{1,0:T(8,128)(2,1)S(1)}, bf16[544,128]{1,0:T(8,128)(2,1)S(1)}, u32[]{:S(2)}, u32[]{:S(2)}) collective-permute-start(bf16[544,128]{1,0:T(8,128)(2,1)S(1)} %collective-permute-done.5.refs_6_), channel_id=1, source_target_pairs={{0,8},{8,0},{1,9},{9,1},{2,10},{10,2},{3,11},{11,3},{4,12},{12,4},... | collective-permute-start | bytes 417800 | tf_op jit(solution)/shard_map/ppermute | solution.py:359
  31.2 1.4 %collective-permute-start.11 = (bf16[544,128]{1,0:T(8,128)(2,1)S(1)}, bf16[544,128]{1,0:T(8,128)(2,1)S(1)}, u32[]{:S(2)}, u32[]{:S(2)}) collective-permute-start(bf16[544,128]{1,0:T(8,128)(2,1)S(1)} %collective-permute-done.6.refs_7_), channel_id=1, source_target_pairs={{0,8},{8,0},{1,9},{9,1},{2,10},{10,2},{3,11},{11,3},{4,12},{12,4},... | collective-permute-start | bytes 417800 | tf_op jit(solution)/shard_map/ppermute | solution.py:359

commit v7 on v6

--- a/solution.py
+++ b/solution.py
@@ -92,8 +92,8 @@
         ref[tile] = value
 
 
-def settle(part):
-    return (part[0] * (1.0 / part[2])).T
+def settle(part, kind):
+    return (part[0] * (1.0 / part[2])).astype(kind).T
 
 
 def key_rows(z, count):
@@ -254,7 +254,7 @@
                 axis=0,
             )
             part = merge(read(before, tile), soften(scores, values, z.scale), z.scale)
-            held_ref[tile * LANES : (tile + 1) * LANES, :] = settle(part).astype(held_ref.dtype)
+            held_ref[tile * LANES : (tile + 1) * LANES, :] = settle(part, held_ref.dtype)
             while len(copies) < min((tile + 1) * LANES // z.row_count, z.heads):
                 h = len(copies)
                 source = held_ref.at[pl.ds(h * z.row_count, z.row_count)]
@@ -304,7 +304,7 @@
         pages = landed_pages(z, places, groups[0] + groups[1])
         add_pages(z, pages, plan_ref, decode_ref, state)
         for tile in range(z.decode_tiles):
-            held_ref[tile * LANES : (tile + 1) * LANES, :] = settle(read(state, tile))
+            held_ref[tile * LANES : (tile + 1) * LANES, :] = settle(read(state, tile), held_ref.dtype)
         copies = []
         for s in range(z.steps):
             span = pl.ds(s * z.dec_rows, z.dec_rows)

time: 35.9 us -> 35.9 us (level)
  no operation moved by 1% of the time
where the time goes in v7:
time: 35.9 us; the launch traced here: 35.2 us
  starting transfers between devices  19 us (53%)
  Pallas kernels  6.22 us (17%)
  waiting for transfers between devices  4.92 us (14%)
  local copies, waits for them, and re-layouts  4 us (11%)
  between operations  0.97 us (3%)
    ppermute x7, starting transfers between devices, body(): chunks[d] = lax.ppermute(chunk_for(z.target(d)), 'tp', z.pairs(d))  15 us
    pallas_call x3, Pallas kernels, call(): pl.pallas_call(functools.partial(kernel, z, shifts), out_shape=[shape for...  6.22 us
    ppermute x7, waiting for transfers between devices, body(): chunks[d] = lax.ppermute(chunk_for(z.target(d)), 'tp', z.pairs(d))  4.9 us
    ppermute x5, starting transfers between devices, hand_over(): return lax.ppermute(pages, 'section', [(0, 1), (1, 0)])  3.98 us
    unnamed x17, local copies, waits for them, and re-layouts  1.57 us
    dynamic_slice x1, local copies, waits for them, and re-layouts, chunk_for(): pages = lax.dynamic_index_in_dim(store, head, axis=2, keepdims=False)  1.41 us
  transfers between devices with their start and end apart: 12, of which 3 were waited for; matrix products, arithmetic and copies ran while one was open for 3% of the time, Pallas kernels for 11%

profile of v7, /device:TPU:13, one launch (start us, length us, event | category | flops | bytes accessed | tf_op | source)
XLA Modules:
  0.0 35.2 jit_solution(1140003944280904254)
XLA Ops:
  0.0 0.8 %copy-done.3 = bf16[1,12,2,8,128]{4,3,2,1,0:T(8,128)(2,1)S(1)} copy-done((bf16[1,12,2,8,128]{4,3,2,1,0:T(8,128)(2,1)S(1)}, bf16[1,12,2,8,128]{4,3,2,1,0:T(8,128)(2,1)}, u32[]{:S(2)}) %copy-start.3) | copy-done | bytes 49176
  0.8 0.1 constant_dynamic-slice_fusion
  0.9 1.4 %constant_dynamic-slice_fusion.1 = (bf16[1,2,2,1,128,128]{5,4,3,2,1,0:T(8,128)(2,1)S(1)}, bf16[1,2,2,1,128,128]{5,4,3,2,1,0:T(8,128)(2,1)S(1)}, bf16[1,2,2,1,128...) fusion(bf16[1,2,2,8,128,128]{5,4,3,2,1,0:T(8,128)(2,1)} %param., ...), kind=kLoop, calls=%fused_computation.19 | loop fusion | bytes 2097184 | tf_op jit(solution)/shard_map/jit(dynamic_index_in_dim)/dynamic_slice | solution.py:437
  2.5 1.4 %collective-permute-start = (bf16[544,128]{1,0:T(8,128)(2,1)S(1)}, bf16[544,128]{1,0:T(8,128)(2,1)S(1)}, u32[]{:S(2)}, u32[]{:S(2)}) collective-permute-start(bf16[544,128]{1,0:T(8,128)(2,1)S(1)} %pad_maximum_fusion.1), channel_id=1, source_target_pairs={{0,2},{1,3},{2,4},{3,5},{4,6},{5,7},{6,0},{7,1},{8,10},{9,11},{10,... | collective-permute-start | bytes 417800 | tf_op jit(solution)/shard_map/ppermute | solution.py:446
  4.0 2.1 %collective-permute-start.1 = (bf16[544,128]{1,0:T(8,128)(2,1)S(1)}, bf16[544,128]{1,0:T(8,128)(2,1)S(1)}, u32[]{:S(2)}, u32[]{:S(2)}) collective-permute-start(bf16[544,128]{1,0:T(8,128)(2,1)S(1)} %pad_maximum_fusion.2), channel_id=1, source_target_pairs={{0,6},{1,7},{2,0},{3,1},{4,2},{5,3},{6,4},{7,5},{8,14},{9,15},{10,... | collective-permute-start | bytes 417800 | tf_op jit(solution)/shard_map/ppermute | solution.py:446
  6.2 1.3 %collective-permute-start.2 = (bf16[544,128]{1,0:T(8,128)(2,1)S(1)}, bf16[544,128]{1,0:T(8,128)(2,1)S(1)}, u32[]{:S(2)}, u32[]{:S(2)}) collective-permute-start(bf16[544,128]{1,0:T(8,128)(2,1)S(1)} %pad_maximum_fusion.3), channel_id=1, source_target_pairs={{0,1},{1,2},{2,3},{3,4},{4,5},{5,6},{6,7},{7,0},{8,9},{9,10},{10,1... | collective-permute-start | bytes 417800 | tf_op jit(solution)/shard_map/ppermute | solution.py:446
  7.5 2.1 %collective-permute-start.3 = (bf16[544,128]{1,0:T(8,128)(2,1)S(1)}, bf16[544,128]{1,0:T(8,128)(2,1)S(1)}, u32[]{:S(2)}, u32[]{:S(2)}) collective-permute-start(bf16[544,128]{1,0:T(8,128)(2,1)S(1)} %pad_maximum_fusion.4), channel_id=1, source_target_pairs={{0,3},{1,4},{2,5},{3,6},{4,7},{5,0},{6,1},{7,2},{8,11},{9,12},{10,... | collective-permute-start | bytes 417800 | tf_op jit(solution)/shard_map/ppermute | solution.py:446
  9.7 0.1 copy.47
  10.5 0.1 copy.27
  10.6 0.2 copy.28
  10.9 0.3 copy.30
  11.2 0.1 pad_bitcast_fusion.decode_ref
  11.3 0.7 %collective-permute-done.refs_1_ = bf16[544,128]{1,0:T(8,128)(2,1)S(1)} collective-permute-done((bf16[544,128]{1,0:T(8,128)(2,1)S(1)}, bf16[544,128]{1,0:T(8,128)(2,1)S(1)}, u32[]{:S(2)}, u32[]{:S(2)}) %collective-permute-start) | collective-permute-done | bytes 139296 | tf_op jit(solution)/shard_map/ppermute | solution.py:446
  12.0 1.4 %collective-permute-start.4 = (bf16[544,128]{1,0:T(8,128)(2,1)S(1)}, bf16[544,128]{1,0:T(8,128)(2,1)S(1)}, u32[]{:S(2)}, u32[]{:S(2)}) collective-permute-start(bf16[544,128]{1,0:T(8,128)(2,1)S(1)} %pad_maximum_fusion.5), channel_id=1, source_target_pairs={{0,4},{1,5},{2,6},{3,7},{4,0},{5,1},{6,2},{7,3},{8,12},{9,13},{10,... | collective-permute-start | bytes 417800 | tf_op jit(solution)/shard_map/ppermute | solution.py:446
  13.4 6.6 %collective-permute-start.6 = (bf16[544,128]{1,0:T(8,128)(2,1)S(1)}, bf16[544,128]{1,0:T(8,128)(2,1)S(1)}, u32[]{:S(2)}, u32[]{:S(2)}) collective-permute-start(bf16[544,128]{1,0:T(8,128)(2,1)S(1)} %pad_maximum_fusion.7), channel_id=1, source_target_pairs={{0,7},{1,0},{2,1},{3,2},{4,3},{5,4},{6,5},{7,6},{8,15},{9,8},{10,9... | collective-permute-start | bytes 417800 | tf_op jit(solution)/shard_map/ppermute | solution.py:446
  20.1 0.7 %copy-done.1 = s32[16]{0:T(128)S(1)} copy-done((s32[16]{0:T(128)S(1)}, s32[16]{0:T(128)}, u32[]{:S(2)}) %copy-start.1) | copy-done | bytes 88
  20.7 2.3 %early_pages.1 = (s32[49]{0:T(128)S(1)}, bf16[1024,128]{1,0:T(8,128)(2,1)S(1)}, bf16[128,128]{1,0:T(8,128)(2,1)S(1)}, f32[16,128,128]{2,1,0:T(8,128)S(1)}, f32[1...) custom-call(s32[1]{0:T(128)S(6)} %copy.58.prefix_ref, s32[4,16]{1,0:T(4,128)S(1)} %bitcast.70, s32[16]{0:T(128)S(1)} %copy-done.1, ...), custom_call_target="tpu_custom_call" | custom-call | flops 536870912 | bytes 4194304 | tf_op jit(solution)/shard_map/early_pages/pallas_call | solution.py:327
  23.0 2.8 %collective-permute-start.7 = (bf16[1024,128]{1,0:T(8,128)(2,1)S(1)}, bf16[1024,128]{1,0:T(8,128)(2,1)S(1)}, u32[]{:S(2)}, u32[]{:S(2)}) collective-permute-start(bf16[1024,128]{1,0:T(8,128)(2,1)S(1)} %get-tuple-element.22), channel_id=1, source_target_pairs={{0,8},{8,0},{1,9},{9,1},{2,10},{10,2},{3,11},{11,3},{4,12},{12,4},... | collective-permute-start | bytes 786440 | tf_op jit(solution)/shard_map/ppermute | solution.py:359
  25.8 1.3 %collective-permute-done.4.refs_5_ = bf16[544,128]{1,0:T(8,128)(2,1)S(1)} collective-permute-done((bf16[544,128]{1,0:T(8,128)(2,1)S(1)}, bf16[544,128]{1,0:T(8,128)(2,1)S(1)}, u32[]{:S(2)}, u32[]{:S(2)}) %collective-permute-start.4) | collective-permute-done | bytes 139296 | tf_op jit(solution)/shard_map/ppermute | solution.py:446
  27.1 2.9 %collective-permute-done.6.refs_7_ = bf16[544,128]{1,0:T(8,128)(2,1)S(1)} collective-permute-done((bf16[544,128]{1,0:T(8,128)(2,1)S(1)}, bf16[544,128]{1,0:T(8,128)(2,1)S(1)}, u32[]{:S(2)}, u32[]{:S(2)}) %collective-permute-start.6) | collective-permute-done | bytes 139296 | tf_op jit(solution)/shard_map/ppermute | solution.py:446
  30.0 0.7 %collective-permute-start.8 = (bf16[544,128]{1,0:T(8,128)(2,1)S(1)}, bf16[544,128]{1,0:T(8,128)(2,1)S(1)}, u32[]{:S(2)}, u32[]{:S(2)}) collective-permute-start(bf16[544,128]{1,0:T(8,128)(2,1)S(1)} %collective-permute-done.3.refs_4_), channel_id=1, source_target_pairs={{0,8},{8,0},{1,9},{9,1},{2,10},{10,2},{3,11},{11,3},{4,12},{12,4},... | collective-permute-start | bytes 417800 | tf_op jit(solution)/shard_map/ppermute | solution.py:359
  30.7 0.5 %collective-permute-start.10 = (bf16[544,128]{1,0:T(8,128)(2,1)S(1)}, bf16[544,128]{1,0:T(8,128)(2,1)S(1)}, u32[]{:S(2)}, u32[]{:S(2)}) collective-permute-start(bf16[544,128]{1,0:T(8,128)(2,1)S(1)} %collective-permute-done.5.refs_6_), channel_id=1, source_target_pairs={{0,8},{8,0},{1,9},{9,1},{2,10},{10,2},{3,11},{11,3},{4,12},{12,4},... | collective-permute-start | bytes 417800 | tf_op jit(solution)/shard_map/ppermute | solution.py:359
  31.2 1.4 %late_pages.1 = (f32[16,128,128]{2,1,0:T(8,128)S(1)}, f32[16,1,128]{2,1,0:T(1,128)S(1)}, f32[16,1,128]{2,1,0:T(1,128)S(1)}, bf16[96,2048]{1,0:T(8,128)(2,1)}) custom-call(s32[49]{0:T(128)S(1)} %get-tuple-element.21.stored_plan_ref, bf16[12,128,128]{2,1,0:T(8,128)(2,1)S(1)} %bitcast.69, bf16[16,128,128]{2,1,0:T(8,128)(2,1)S(1)} %pad_bitcast_fusion.decode_ref, ...), custom_call_target="tpu_custom_call" | custom-call | flops 671088640 | bytes 4194304 | tf_op jit(solution)/shard_map/late_pages/pallas_call | solution.py:327
  32.7 2.5 %landed_pages.1 = bf16[96,2048]{1,0:T(8,128)(2,1)} custom-call(s32[49]{0:T(128)S(1)} %get-tuple-element.21.stored_plan_ref, bf16[16,128,128]{2,1,0:T(8,128)(2,1)S(1)} %pad_bitcast_fusion.decode_ref, bf16[1024,128]{1,0:T(8,128)(2,1)S(1)} %collective-permute-done.7.early_ref, ...), custom_call_target="tpu_custom_call", output_to_operand_aliasing={{}: (10, {})} | custom-call | flops 134217728 | bytes 4194304 | tf_op jit(solution)/shard_map/landed_pages/pallas_call | solution.py:327
  (48 shorter events, 0.4 us)
Async XLA Ops:
  0.0 0.8 %copy-start.3 = (bf16[1,12,2,8,128]{4,3,2,1,0:T(8,128)(2,1)S(1)}, bf16[1,12,2,8,128]{4,3,2,1,0:T(8,128)(2,1)}, u32[]{:S(2)}) copy-start(bf16[1,12,2,8,128]{4,3,2,1,0:T(8,128)(2,1)} %param.7) | copy-start | bytes 147460
  2.4 23.4 %collective-permute-start.5 = (bf16[544,128]{1,0:T(8,128)(2,1)S(1)}, bf16[544,128]{1,0:T(8,128)(2,1)S(1)}, u32[]{:S(2)}, u32[]{:S(2)}) collective-permute-start(bf16[544,128]{1,0:T(8,128)(2,1)S(1)} %pad_maximum_fusion.6), channel_id=1, source_target_pairs={{0,5},{1,6},{2,7},{3,0},{4,1},{5,2},{6,3},{7,4},{8,13},{9,14},{10,... | collective-permute-start | bytes 417800 | tf_op jit(solution)/shard_map/ppermute | solution.py:446
  2.5 9.5 %collective-permute-start = (bf16[544,128]{1,0:T(8,128)(2,1)S(1)}, bf16[544,128]{1,0:T(8,128)(2,1)S(1)}, u32[]{:S(2)}, u32[]{:S(2)}) collective-permute-start(bf16[544,128]{1,0:T(8,128)(2,1)S(1)} %pad_maximum_fusion.1), channel_id=1, source_target_pairs={{0,2},{1,3},{2,4},{3,5},{4,6},{5,7},{6,0},{7,1},{8,10},{9,11},{10,... | collective-permute-start | bytes 417800 | tf_op jit(solution)/shard_map/ppermute | solution.py:446
  4.0 5.6 %copy-start.2 = (bf16[1,96,2048]{2,1,0:T(8,128)(2,1)S(1)}, bf16[1,96,2048]{2,1,0:T(8,128)(2,1)}, u32[]{:S(2)}) copy-start(bf16[1,96,2048]{2,1,0:T(8,128)(2,1)} %param.6) | copy-start | bytes 1179652
  4.0 9.4 %collective-permute-start.1 = (bf16[544,128]{1,0:T(8,128)(2,1)S(1)}, bf16[544,128]{1,0:T(8,128)(2,1)S(1)}, u32[]{:S(2)}, u32[]{:S(2)}) collective-permute-start(bf16[544,128]{1,0:T(8,128)(2,1)S(1)} %pad_maximum_fusion.2), channel_id=1, source_target_pairs={{0,6},{1,7},{2,0},{3,1},{4,2},{5,3},{6,4},{7,5},{8,14},{9,15},{10,... | collective-permute-start | bytes 417800 | tf_op jit(solution)/shard_map/ppermute | solution.py:446
  6.2 13.9 %collective-permute-start.2 = (bf16[544,128]{1,0:T(8,128)(2,1)S(1)}, bf16[544,128]{1,0:T(8,128)(2,1)S(1)}, u32[]{:S(2)}, u32[]{:S(2)}) collective-permute-start(bf16[544,128]{1,0:T(8,128)(2,1)S(1)} %pad_maximum_fusion.3), channel_id=1, source_target_pairs={{0,1},{1,2},{2,3},{3,4},{4,5},{5,6},{6,7},{7,0},{8,9},{9,10},{10,1... | collective-permute-start | bytes 417800 | tf_op jit(solution)/shard_map/ppermute | solution.py:446
  7.5 18.3 %collective-permute-start.3 = (bf16[544,128]{1,0:T(8,128)(2,1)S(1)}, bf16[544,128]{1,0:T(8,128)(2,1)S(1)}, u32[]{:S(2)}, u32[]{:S(2)}) collective-permute-start(bf16[544,128]{1,0:T(8,128)(2,1)S(1)} %pad_maximum_fusion.4), channel_id=1, source_target_pairs={{0,3},{1,4},{2,5},{3,6},{4,7},{5,0},{6,1},{7,2},{8,11},{9,12},{10,... | collective-permute-start | bytes 417800 | tf_op jit(solution)/shard_map/ppermute | solution.py:446
  11.3 8.8 %copy-start = (s32[16,4]{0,1:T(4,128)S(1)}, s32[16,4]{0,1:T(4,128)}, u32[]{:S(2)}) copy-start(s32[16,4]{0,1:T(4,128)} %param.10) | copy-start | bytes 772
  12.0 15.1 %collective-permute-start.4 = (bf16[544,128]{1,0:T(8,128)(2,1)S(1)}, bf16[544,128]{1,0:T(8,128)(2,1)S(1)}, u32[]{:S(2)}, u32[]{:S(2)}) collective-permute-start(bf16[544,128]{1,0:T(8,128)(2,1)S(1)} %pad_maximum_fusion.5), channel_id=1, source_target_pairs={{0,4},{1,5},{2,6},{3,7},{4,0},{5,1},{6,2},{7,3},{8,12},{9,13},{10,... | collective-permute-start | bytes 417800 | tf_op jit(solution)/shard_map/ppermute | solution.py:446
  13.4 16.6 %collective-permute-start.6 = (bf16[544,128]{1,0:T(8,128)(2,1)S(1)}, bf16[544,128]{1,0:T(8,128)(2,1)S(1)}, u32[]{:S(2)}, u32[]{:S(2)}) collective-permute-start(bf16[544,128]{1,0:T(8,128)(2,1)S(1)} %pad_maximum_fusion.7), channel_id=1, source_target_pairs={{0,7},{1,0},{2,1},{3,2},{4,3},{5,4},{6,5},{7,6},{8,15},{9,8},{10,9... | collective-permute-start | bytes 417800 | tf_op jit(solution)/shard_map/ppermute | solution.py:446
  20.1 0.7 %copy-start.1 = (s32[16]{0:T(128)S(1)}, s32[16]{0:T(128)}, u32[]{:S(2)}) copy-start(s32[16]{0:T(128)} %context_ref.1) | copy-start | bytes 196
  23.0 9.6 %collective-permute-start.7 = (bf16[1024,128]{1,0:T(8,128)(2,1)S(1)}, bf16[1024,128]{1,0:T(8,128)(2,1)S(1)}, u32[]{:S(2)}, u32[]{:S(2)}) collective-permute-start(bf16[1024,128]{1,0:T(8,128)(2,1)S(1)} %get-tuple-element.22), channel_id=1, source_target_pairs={{0,8},{8,0},{1,9},{9,1},{2,10},{10,2},{3,11},{11,3},{4,12},{12,4},... | collective-permute-start | bytes 786440 | tf_op jit(solution)/shard_map/ppermute | solution.py:359
  30.0 2.6 %collective-permute-start.8 = (bf16[544,128]{1,0:T(8,128)(2,1)S(1)}, bf16[544,128]{1,0:T(8,128)(2,1)S(1)}, u32[]{:S(2)}, u32[]{:S(2)}) collective-permute-start(bf16[544,128]{1,0:T(8,128)(2,1)S(1)} %collective-permute-done.3.refs_4_), channel_id=1, source_target_pairs={{0,8},{8,0},{1,9},{9,1},{2,10},{10,2},{3,11},{11,3},{4,12},{12,4},... | collective-permute-start | bytes 417800 | tf_op jit(solution)/shard_map/ppermute | solution.py:359
  30.7 1.9 %collective-permute-start.9 = (bf16[544,128]{1,0:T(8,128)(2,1)S(1)}, bf16[544,128]{1,0:T(8,128)(2,1)S(1)}, u32[]{:S(2)}, u32[]{:S(2)}) collective-permute-start(bf16[544,128]{1,0:T(8,128)(2,1)S(1)} %collective-permute-done.4.refs_5_), channel_id=1, source_target_pairs={{0,8},{8,0},{1,9},{9,1},{2,10},{10,2},{3,11},{11,3},{4,12},{12,4},... | collective-permute-start | bytes 417800 | tf_op jit(solution)/shard_map/ppermute | solution.py:359
  30.7 1.9 %collective-permute-start.10 = (bf16[544,128]{1,0:T(8,128)(2,1)S(1)}, bf16[544,128]{1,0:T(8,128)(2,1)S(1)}, u32[]{:S(2)}, u32[]{:S(2)}) collective-permute-start(bf16[544,128]{1,0:T(8,128)(2,1)S(1)} %collective-permute-done.5.refs_6_), channel_id=1, source_target_pairs={{0,8},{8,0},{1,9},{9,1},{2,10},{10,2},{3,11},{11,3},{4,12},{12,4},... | collective-permute-start | bytes 417800 | tf_op jit(solution)/shard_map/ppermute | solution.py:359
  31.2 1.4 %collective-permute-start.11 = (bf16[544,128]{1,0:T(8,128)(2,1)S(1)}, bf16[544,128]{1,0:T(8,128)(2,1)S(1)}, u32[]{:S(2)}, u32[]{:S(2)}) collective-permute-start(bf16[544,128]{1,0:T(8,128)(2,1)S(1)} %collective-permute-done.6.refs_7_), channel_id=1, source_target_pairs={{0,8},{8,0},{1,9},{9,1},{2,10},{10,2},{3,11},{11,3},{4,12},{12,4},... | collective-permute-start | bytes 417800 | tf_op jit(solution)/shard_map/ppermute | solution.py:359
